TPU v7x, 32 devices: a whole 2x2x4 slice. The times are simulated.
32 devices in a mesh: grp: 2 (over x), src: 2 (over core), lat: 8 (over z, y).
Axes of the slice: x: 2, y: 2, z: 4, core: 2. Of those that a mesh axis runs over, the one named last changes fastest.
Arguments:
- store: bfloat16 [256, 2, 4096], P(('grp', 'lat'), 'src'), parts along dimension 0, may hold values from -6.4 to 6.4
- row_index: int32 [128], P(('grp', 'lat')), parts along dimension 0, may hold values from 0 to 15
- w_enc: bfloat16 [4, 4096, 1024], P(('grp', 'src'), None, 'lat'), parts along dimension 0, may hold values from -0.0625 to 0.0625
- decoder_matrix: bfloat16 [4, 1024, 4096], P(('grp', 'src'), 'lat'), parts along dimension 0, may hold values from -0.46875 to 0.46875
- m_enc: bfloat16 [4, 4096, 1024], P(('grp', 'src'), None, 'lat'), parts along dimension 0, may hold values from -0.0001235962 to 0.0001235962
- v_enc: bfloat16 [4, 4096, 1024], P(('grp', 'src'), None, 'lat'), parts along dimension 0, may hold values from 1.16415322e-13 to 1.4202669e-09
- m_dec: bfloat16 [4, 1024, 4096], P(('grp', 'src'), 'lat'), parts along dimension 0, may hold values from -0.0001235962 to 0.0001235962
- v_dec: bfloat16 [4, 1024, 4096], P(('grp', 'src'), 'lat'), parts along dimension 0, may hold values from 1.16415322e-13 to 1.4202669e-09
Outputs:
- encoder_step: bfloat16 [4, 4096, 1024], P(('grp', 'src'), None, 'lat'), parts along dimension 0
- decoder_step: bfloat16 [4, 1024, 4096], P(('grp', 'src'), 'lat'), parts along dimension 0
There are 2 independent parts, one for each index of `grp`. A program takes and returns all parts, laid end to end along the dimension named above; each array names one. Nothing has to cross between parts.
All inputs are finite; a program needn't handle non-finite values.
Results may differ from a plain program's by a relative error of at most 0.009.
Values may be sent and summed in bfloat16 or wider, within the bound.
No kernel may reach another device: no remote copies, remote signals or barrier semaphores. Data moves between devices by JAX's collectives and lax.ppermute only.
A program may use at most 128 MiB of HBM per device.

v0:
```python
import jax
import jax.numpy as jnp
from jax import lax
from jax.sharding import PartitionSpec as P

sparsity = 0.5
beta_one = 0.9
beta_two = 0.95
adam_eps = 1e-08
clip_rms = 1.0
norm_eps = 1e-06


def adam_direction(gradient, moment_one, moment_two):
    first_wide = moment_one.astype(jnp.float32)
    second_wide = moment_two.astype(jnp.float32)
    new_first = beta_one * first_wide + (1.0 - beta_one) * gradient
    new_second = beta_two * second_wide + (1.0 - beta_two) * gradient * gradient
    return new_first / (jnp.sqrt(new_second) + adam_eps)


def body(store, row_index, w_enc, decoder_matrix, m_enc, v_enc, m_dec, v_dec):
    own_rows = store[row_index]
    batch_rows = lax.all_gather(own_rows, "lat", axis=0, tiled=True)
    partial_value = jnp.einsum("bsd,sdl->bl", batch_rows, w_enc, preferred_element_type=jnp.float32)
    dec_square = jnp.square(decoder_matrix.astype(jnp.float32))
    dec_norm = jnp.sqrt(jnp.sum(dec_square, axis=2) + norm_eps)
    preact, norm_total = lax.psum((partial_value, jnp.sum(dec_norm, axis=0)), "src")
    feature_codes = jnp.maximum(preact, 0.0).astype(jnp.bfloat16)
    source_count = w_enc.shape[0] * lax.axis_size("src")
    features = w_enc.shape[1]
    latent_count = w_enc.shape[2] * lax.axis_size("lat")
    batch_count = batch_rows.shape[0]
    rebuilt_output = lax.psum_scatter(
        jnp.einsum(
            "ip,xpt->ixt", feature_codes, decoder_matrix, preferred_element_type=jnp.float32
        ),
        "lat",
        scatter_dimension=0,
        tiled=True,
    )
    own_error = (rebuilt_output - own_rows.astype(jnp.float32)).astype(jnp.bfloat16)
    residual_error_rows = lax.all_gather(own_error, "lat", axis=0, tiled=True)
    element_count = float(batch_count * source_count * features)
    squared_error_scale = 2.0 / element_count
    sparse_scale = sparsity / element_count
    column_sums = jnp.sum(feature_codes.astype(jnp.float32), axis=0)
    decoder_gradient = squared_error_scale * jnp.einsum(
        "yt,ygh->gth", feature_codes, residual_error_rows, preferred_element_type=jnp.float32
    )
    decoder_gradient = (
        decoder_gradient
        + sparse_scale
        * column_sums[None, :, None]
        * decoder_matrix.astype(jnp.float32)
        / dec_norm[:, :, None]
    )
    dec_dir = adam_direction(decoder_gradient, m_dec, v_dec)
    partial_gradient_value = jnp.einsum(
        "jva,vfa->jf", residual_error_rows, decoder_matrix, preferred_element_type=jnp.float32
    )
    latent_code_gradient = lax.psum(partial_gradient_value, "src")
    pre_grad = jnp.where(
        preact > 0,
        squared_error_scale * latent_code_gradient + sparse_scale * norm_total[None, :],
        0.0,
    )
    pre_grad = pre_grad.astype(jnp.bfloat16)
    grad_enc = jnp.einsum("bsd,bl->sdl", batch_rows, pre_grad, preferred_element_type=jnp.float32)
    enc_dir = adam_direction(grad_enc, m_enc, v_enc)
    squares = lax.psum(jnp.sum(enc_dir * enc_dir) + jnp.sum(dec_dir * dec_dir), ("src", "lat"))
    update_rms = jnp.sqrt(squares / float(2 * source_count * features * latent_count))
    factor = 1.0 / jnp.maximum(1.0, update_rms / clip_rms)
    return ((enc_dir * factor).astype(jnp.bfloat16), (dec_dir * factor).astype(jnp.bfloat16))


def solution(mesh):
    return jax.shard_map(
        body,
        mesh=mesh,
        in_specs=(
            P(("grp", "lat"), "src", None),
            P(("grp", "lat")),
            P(("grp", "src"), None, "lat"),
            P(("grp", "src"), "lat", None),
            P(("grp", "src"), None, "lat"),
            P(("grp", "src"), None, "lat"),
            P(("grp", "src"), "lat", None),
            P(("grp", "src"), "lat", None),
        ),
        out_specs=(P(("grp", "src"), None, "lat"), P(("grp", "src"), "lat", None)),
        check_vma=False,
    )
```

profile of v0, /device:TPU:0, one launch (start us, length us, event | category | flops | bytes accessed | tf_op | source)
XLA Modules:
  0.0 205.9 jit_solution(17111781160323208349)
XLA Ops:
  7.2 0.0 copy-start
  7.2 0.0 copy-start.1
  7.2 0.0 reduce-scatter.2.cloned.1.call-start
  7.2 0.8 compare_select_fusion
  8.0 1.6 gather_fusion
  9.6 33.0 %all-gather = bf16[64,4096]{1,0:T(8,128)(2,1)S(1)} all-gather(bf16[8,4096]{1,0:T(8,128)(2,1)S(1)} %gather_fusion), channel_id=2, replica_groups=mesh['grp'=2,'src'=2,'lat'=8] {'lat'}, dimensions={0}, use_global_device_ids=true | all-gather | bytes 589824 | tf_op jit(solution)/shard_map/all_gather | solution.py:24
  42.6 0.0 copy-start.2
  42.6 0.8 copy-done.2
  43.4 0.0 copy-done
  43.4 0.3 fusion.16
  43.7 3.4 %psum.28 = f32[64,128]{1,0:T(8,128)S(1)} all-reduce(f32[64,128]{1,0:T(8,128)S(1)} %fusion.16), channel_id=1, replica_groups=mesh['grp'=2,'src'=2,'lat'=8] {'src'}, use_global_device_ids=true, to_apply=%region_0.0 | all-reduce | flops 8192 | bytes 65536 | tf_op jit(solution)/shard_map/psum | solution.py:28
  47.2 0.0 copy-done.1
  47.2 1.3 convolution_bitcast_fusion
  48.4 0.0 reduce-scatter.2.cloned.1.call-update
  48.5 0.7 copy.10
  49.1 2.3 %copy.11 = bf16[1,128,4096]{1,2,0:T(8,128)(2,1)} copy(bf16[1,128,4096]{2,1,0:T(8,128)(2,1)} %param.14) | data formatting | bytes 2097152 | tf_op args[6]
  51.4 2.3 %copy.12 = bf16[1,128,4096]{1,2,0:T(8,128)(2,1)} copy(bf16[1,128,4096]{2,1,0:T(8,128)(2,1)} %param.15) | data formatting | bytes 2097152 | tf_op args[7]
  53.7 0.6 fusion.2
  54.3 59.6 %reduce-scatter.2.cloned.1.call-done = f32[8,1,4096]{2,0,1:T(8,128)} async-done(((f32[64,1,4096]{2,0,1:T(8,128)}), f32[8,1,4096]{2,0,1:T(8,128)}) %reduce-scatter.2.cloned.1.call-update) | async-done | bytes 131088 | tf_op jit(solution)/shard_map/reduce_scatter | solution.py:34
  113.9 0.9 fusion.20
  114.8 31.5 %all_gather.7 = bf16[64,1,4096]{2,0,1:T(8,128)(2,1)S(1)} all-gather(bf16[8,1,4096]{2,0,1:T(8,128)(2,1)S(1)} %fusion.20), channel_id=1, replica_groups=mesh['grp'=2,'src'=2,'lat'=8] {'lat'}, dimensions={0}, use_global_device_ids=true | all-gather | bytes 589824 | tf_op jit(solution)/shard_map/all_gather | solution.py:43
  146.3 0.0 copy-start.4
  146.3 0.8 copy-done.4
  147.1 0.5 fusion.13
  147.6 3.5 %all-reduce = (f32[64,128]{1,0:T(8,128)S(1)}, f32[128]{0:T(128)S(1)}) all-reduce(f32[64,128]{1,0:T(8,128)S(1)} %fusion.13, f32[128]{0:T(128)S(1)} %add_sqrt_fusion), channel_id=1, replica_groups=mesh['grp'=2,'src'=2,'lat'=8] {'src'}, use_global_device_ids=true, to_apply=%region_2.0 | all-reduce | flops 8320 | bytes 66560 | tf_op jit(solution)/shard_map/psum | solution.py:62
  151.1 0.0 copy-start.3
  151.1 0.0 copy-start.6
  151.1 0.0 copy-start.7
  151.1 5.7 %multiply_reduce_fusion = (f32[]{:T(128)}, f32[1,128,4096]{1,2,0:T(8,128)}) fusion(bf16[1,128,4096]{1,2,0:T(8,128)(2,1)} %copy.12, f32[128]{0:T(128)S(1)} %add_sqrt_fusion, bf16[1,128,4096]{1,2,0:T(8,128)(2,1)S(1)} %copy.10, f32[128]{0:T(128)S(1)} %broadcast_multiply_fusion, f32[64,128]{1,0:T(8,128)S(1)} %psum.28, bf16[64,1,4096]{2,0,1:T(8,128)(2,1)} %copy-done.4, ...), kind=kOutput, calls=%fused_computation.23 | convolution fusion | flops 76562432 | bytes 5800964 | tf_op jit(solution)/shard_map/yt,ygh->gth/dot_general | solution.py:48
  156.9 0.0 copy-done.3
  156.9 0.0 copy-done.6
  156.9 0.0 copy-done.7
  156.9 3.5 %multiply_reduce_fusion.1 = (f32[]{:T(128)}, f32[1,4096,128]{2,1,0:T(8,128)}) fusion(bf16[1,4096,128]{2,1,0:T(8,128)(2,1)S(1)} %copy-done.6, bf16[64,4096]{1,0:T(8,128)(2,1)S(1)} %copy-done.3, f32[64,128]{1,0:T(8,128)S(1)} %get-tuple-element.4, f32[64,128]{1,0:T(8,128)S(1)} %psum.28, f32[128]{0:T(128)S(1)} %broadcast_multiply_fusion.1, ...), kind=kOutput, calls=%fused_computation.24 | convolution fusion | flops 73965568 | bytes 4784644 | tf_op jit(solution)/shard_map/bsd,bl->sdl/dot_general | solution.py:69
  161.6 32.1 %psum.31 = f32[]{:T(128)} all-reduce(f32[]{:T(128)S(6)} %add.78), channel_id=1, replica_groups=mesh['grp'=2,'src'=2,'lat'=8] {'src','lat'}, use_global_device_ids=true, to_apply=%region_8.9 | all-reduce | flops 1 | bytes 8 | tf_op jit(solution)/shard_map/psum | solution.py:71
  194.5 0.0 copy-start.5
  194.5 1.9 multiply_convert_fusion
  196.3 0.4 copy-done.5
  196.7 1.1 multiply_convert_fusion.1
  197.8 1.3 copy.13
  (5 shorter events, 0.0 us)
Async XLA Ops:
  7.2 36.2 %copy-start = (bf16[1,4096,128]{2,1,0:T(8,128)(2,1)S(1)}, bf16[1,4096,128]{2,1,0:T(8,128)(2,1)}, u32[]{:S(2)}) copy-start(bf16[1,4096,128]{2,1,0:T(8,128)(2,1)} %param.10) | copy-start | bytes 3145732
  7.2 40.0 %copy-start.1 = (bf16[1,128,4096]{2,1,0:T(8,128)(2,1)S(1)}, bf16[1,128,4096]{2,1,0:T(8,128)(2,1)}, u32[]{:S(2)}) copy-start(bf16[1,128,4096]{2,1,0:T(8,128)(2,1)} %param.11) | copy-start | bytes 3145732
  7.2 106.7 %reduce-scatter.2.cloned.1.call-start = ((), (), s32[]{:S(2)}) async-start(), calls=%async_computation.1 | async-start | bytes 1179648 | tf_op jit(solution)/shard_map/reduce_scatter | solution.py:34
  42.6 0.8 copy-start.2
  146.3 0.8 copy-start.4
  151.1 5.8 %copy-start.3 = (bf16[64,4096]{1,0:T(8,128)(2,1)S(1)}, bf16[64,4096]{1,0:T(8,128)(2,1)}, u32[]{:S(2)}) copy-start(bf16[64,4096]{1,0:T(8,128)(2,1)} %copy-done.2) | copy-start | bytes 1572868
  151.1 5.8 %copy-start.6 = (bf16[1,4096,128]{2,1,0:T(8,128)(2,1)S(1)}, bf16[1,4096,128]{2,1,0:T(8,128)(2,1)}, u32[]{:S(2)}) copy-start(bf16[1,4096,128]{2,1,0:T(8,128)(2,1)} %param.13) | copy-start | bytes 3145732
  151.1 5.8 %copy-start.7 = (bf16[1,4096,128]{2,1,0:T(8,128)(2,1)S(1)}, bf16[1,4096,128]{2,1,0:T(8,128)(2,1)}, u32[]{:S(2)}) copy-start(bf16[1,4096,128]{2,1,0:T(8,128)(2,1)} %param.12) | copy-start | bytes 3145732
  194.5 2.2 %copy-start.5 = (f32[1,4096,128]{2,1,0:T(8,128)S(1)}, f32[1,4096,128]{2,1,0:T(8,128)}, u32[]{:S(2)}) copy-start(f32[1,4096,128]{2,1,0:T(8,128)} %get-tuple-element.7) | copy-start | bytes 6291460
Sparse Core Ops, SparseCore 0:
  48.6 65.2 reduce-scatter.1
where the time goes:
time: 206 us
  blocking collectives  104 us (50%)
  waiting for transfers between devices  59.6 us (29%)
  between operations  16.2 us (8%)
  matrix products  11.3 us (5%)
  local copies, waits for them, and re-layouts  10 us (5%)
  other arithmetic  5.25 us (3%)
    reduce_scatter x1, waiting for transfers between devices, body(): lax.psum_scatter(jnp.einsum('ip,xpt->ixt', feature_codes, decoder_matrix,...  59.6 us
    all_gather x1, blocking collectives, body(): batch_rows = lax.all_gather(own_rows, 'lat', axis=0, tiled=True)  33 us
    psum x1, blocking collectives, body(): lax.psum(jnp.sum(enc_dir * enc_dir) + jnp.sum(dec_dir * dec_dir), ('src',...  32.1 us
    all_gather x1, blocking collectives, body(): residual_error_rows = lax.all_gather(own_error, 'lat', axis=0, tiled=True)  31.5 us
    unnamed x20, local copies, waits for them, and re-layouts  8.48 us
    dot_general x1, matrix products, body(): jnp.einsum('yt,ygh->gth', feature_codes, residual_error_rows, preferred_e...  5.74 us
  transfers between devices with their start and end apart: 1, of which 1 were waited for; matrix products, arithmetic and copies ran while one was open for 3% of the time, Pallas kernels for 0%

commit v1 on v0

v1 whole, which is shorter than its diff:
```python
import jax
import jax.numpy as jnp
from jax import lax
from jax.sharding import PartitionSpec as P

sparsity = 0.5
beta_one = 0.9
beta_two = 0.95
adam_eps = 1e-08
clip_rms = 1.0
norm_eps = 1e-06
f32 = jnp.float32
bf16 = jnp.bfloat16


def swap(value, axis, bits):
    count = lax.axis_size(axis)
    return lax.ppermute(value, axis, [(i, i ^ bits) for i in range(count)])


def adam_direction(gradient, moment_one, moment_two):
    first_wide = moment_one.astype(f32)
    second_wide = moment_two.astype(f32)
    new_first = beta_one * first_wide + (1.0 - beta_one) * gradient
    new_second = beta_two * second_wide + (1.0 - beta_two) * gradient * gradient
    return new_first / (jnp.sqrt(new_second) + adam_eps)


def pack(value):
    top = jnp.max(jnp.abs(value), axis=-1, keepdims=True)
    level = jnp.ceil(16.0 * jnp.log2(jnp.maximum(top, 1e-30)))
    scaled = jnp.round(value * (32767.0 * jnp.exp2(level * -0.0625)))
    scaled = jnp.clip(scaled, -32767.0, 32767.0)
    level = jnp.broadcast_to(level, value.shape[:-1] + (128,))
    return jnp.concatenate([scaled, level], axis=-1).astype(jnp.int16)


def unpack(packed):
    wide = packed.astype(f32)
    return wide[..., :-128] * (jnp.exp2(wide[..., -128:-127] * 0.0625) * (1.0 / 32767.0))


def quad_gather(quarter):
    return [quarter] + [swap(quarter, "lat", k) for k in (1, 2, 3)]


def body(store, row_index, w_enc, decoder_matrix, m_enc, v_enc, m_dec, v_dec):
    lat_count = lax.axis_size("lat")
    high_bits = [4 << i for i in range((lat_count // 4).bit_length() - 1)]
    store = store[:, 0, :]
    w_enc, decoder_matrix, m_enc, v_enc, m_dec, v_dec = (
        a[0] for a in (w_enc, decoder_matrix, m_enc, v_enc, m_dec, v_dec)
    )
    features, latents = w_enc.shape
    own_count = row_index.shape[0]
    batch_count = own_count * lat_count
    source_count = lax.axis_size("src")
    element_count = float(batch_count * source_count * features)
    squared_error_scale = 2.0 / element_count
    sparse_scale = sparsity / element_count

    pick = row_index[:, None] == jnp.arange(store.shape[0], dtype=row_index.dtype)[None, :]
    own_rows = jnp.dot(pick.astype(bf16), store, preferred_element_type=f32).astype(bf16)
    quarter = own_rows
    for bit in high_bits:
        quarter = jnp.concatenate([quarter, swap(quarter, "lat", bit)])
    quarter_count = quarter.shape[0]
    batch_rows = jnp.concatenate(quad_gather(quarter))

    partial_value = jnp.dot(batch_rows, w_enc, preferred_element_type=f32)
    dec_wide = decoder_matrix.astype(f32)
    dec_norm = jnp.sqrt(jnp.sum(dec_wide * dec_wide, axis=1) + norm_eps)
    preact = partial_value + swap(partial_value, "src", 1)
    norm_total = dec_norm + swap(dec_norm, "src", 1)
    feature_codes = jnp.maximum(preact, 0.0).astype(bf16)
    parts = jnp.dot(feature_codes, decoder_matrix, preferred_element_type=f32)
    parts = parts.reshape(4, quarter_count, features)
    total = parts[0]
    for k in (1, 2, 3):
        total = total + unpack(swap(pack(parts[k]), "lat", k))
    for at, bit in enumerate(high_bits):
        other = unpack(swap(pack(total), "lat", bit))
        span = own_count << at
        other = jnp.flip(other.reshape(-1, 2, span, features), 1).reshape(quarter_count, features)
        total = total + other
    quarter_error = (total - quarter.astype(f32)).astype(bf16)
    error_rows = jnp.concatenate(quad_gather(quarter_error))

    column_sums = jnp.sum(feature_codes.astype(f32), axis=0)
    decoder_gradient = squared_error_scale * lax.dot_general(
        feature_codes, error_rows, (((0,), (0,)), ((), ())), preferred_element_type=f32
    )
    decoder_gradient = decoder_gradient + (sparse_scale * column_sums / dec_norm)[:, None] * dec_wide
    dec_dir = adam_direction(decoder_gradient, m_dec, v_dec)
    partial_back = lax.dot_general(
        error_rows, decoder_matrix, (((1,), (1,)), ((), ())), preferred_element_type=f32
    )
    back = partial_back + swap(partial_back, "src", 1)
    pre_grad = jnp.where(
        preact > 0, squared_error_scale * back + sparse_scale * norm_total[None, :], 0.0
    ).astype(bf16)
    grad_enc = lax.dot_general(
        batch_rows, pre_grad, (((0,), (0,)), ((), ())), preferred_element_type=f32
    )
    enc_dir = adam_direction(grad_enc, m_enc, v_enc)
    squares = jnp.sum(enc_dir * enc_dir) + jnp.sum(dec_dir * dec_dir)
    squares = squares.reshape(1, 1)
    squares = squares + swap(squares, "src", 1)
    bit = 1
    while bit < lat_count:
        squares = squares + swap(squares, "lat", bit)
        bit *= 2
    update_rms = jnp.sqrt(squares / float(2 * source_count * features * latents * lat_count))
    factor = 1.0 / jnp.maximum(1.0, update_rms / clip_rms)
    return ((enc_dir * factor).astype(bf16)[None], (dec_dir * factor).astype(bf16)[None])


def solution(mesh):
    return jax.shard_map(
        body,
        mesh=mesh,
        in_specs=(
            P(("grp", "lat"), "src", None),
            P(("grp", "lat")),
            P(("grp", "src"), None, "lat"),
            P(("grp", "src"), "lat", None),
            P(("grp", "src"), None, "lat"),
            P(("grp", "src"), None, "lat"),
            P(("grp", "src"), "lat", None),
            P(("grp", "src"), "lat", None),
        ),
        out_specs=(P(("grp", "src"), None, "lat"), P(("grp", "src"), "lat", None)),
        check_vma=False,
    )
```

time: 206 us -> 75.6 us (0.37)
  blocking collectives: 104 us -> 0 us
  waiting for transfers between devices: 59.6 us -> 28.1 us
  starting transfers between devices: 0.04 us -> 29.5 us
  between operations: 16.2 us -> 4.71 us
  local copies, waits for them, and re-layouts: 10 us -> 0.36 us
  matrix products: 11.3 us -> 8.5 us
    all_gather x2 -> x0, blocking collectives: 64.5 us -> none  [the longest x1 33 us: body(): batch_rows = lax.all_gather(own_rows, 'lat', axis=0, tiled=True)]
    reduce_scatter x1 -> x0, waiting for transfers between devices: 59.6 us -> none  [body(): lax.psum_scatter(jnp.einsum('ip,xpt->ixt', feature_codes, decoder_matrix,...]
    psum x3 -> x0, blocking collectives: 39 us -> none  [the longest x1 32.1 us: body(): lax.psum(jnp.sum(enc_dir * enc_dir) + jnp.sum(dec_dir * dec_dir), ('src',...]
    ppermute x0 -> x18, starting transfers between devices: none -> 29.5 us  [swap(): return lax.ppermute(value, axis, [(i, i ^ bits) for i in range(count)])]
    ppermute x0 -> x18, waiting for transfers between devices: none -> 28.1 us  [swap(): return lax.ppermute(value, axis, [(i, i ^ bits) for i in range(count)])]
    unnamed x20 -> x17, local copies, waits for them, and re-layouts: 8.48 us -> 0.06 us
    convert_element_type x3 -> x5, other arithmetic: 3.85 us -> 0.2 us  [the longest x4 0.16 us: unpack(): wide = packed.astype(f32)]
    dot_general x5 -> x6, matrix products: 11.3 us -> 8.5 us  [the longest x1 3.55 us: body(): lax.dot_general(batch_rows, pre_grad, (((0,), (0,)), ((), ())), preferred...]
  transfers between devices with their start and end apart: 1 -> 18, of which waited for: 1 -> 13; matrix products, arithmetic and copies ran while one was open for 3% -> 5% of each run, Pallas kernels for 0% -> 0%
where the time goes in v1:
time: 75.6 us; the launch traced here: 75.4 us
  starting transfers between devices  29.5 us (39%)
  waiting for transfers between devices  28.1 us (37%)
  matrix products  8.5 us (11%)
  between operations  4.71 us (6%)
  other arithmetic  4.15 us (5%)
    ppermute x18, starting transfers between devices, swap(): return lax.ppermute(value, axis, [(i, i ^ bits) for i in range(count)])  29.5 us
    ppermute x18, waiting for transfers between devices, swap(): return lax.ppermute(value, axis, [(i, i ^ bits) for i in range(count)])  28.1 us
    dot_general x1, matrix products, body(): lax.dot_general(batch_rows, pre_grad, (((0,), (0,)), ((), ())), preferred...  3.55 us
    dot_general x1, matrix products, body(): lax.dot_general(feature_codes, error_rows, (((0,), (0,)), ((), ())), pref...  2.58 us
  transfers between devices with their start and end apart: 18, of which 13 were waited for; matrix products, arithmetic and copies ran while one was open for 5% of the time, Pallas kernels for 0%

profile of v1, /device:TPU:0, one launch (start us, length us, event | category | flops | bytes accessed | tf_op | source)
XLA Modules:
  0.0 75.4 jit_solution(5838814794368106956)
XLA Ops:
  0.7 1.3 %constant_dynamic-update-slice_fusion.4 = (bf16[64,4096]{1,0:T(8,128)(2,1)S(1)}, bf16[8,4096]{1,0:T(8,128)(2,1)S(1)}) fusion(bf16[16,1,4096]{2,0,1:T(8,128)(2,1)} %param.8, s32[8]{0:T(128)} %param.9), kind=kOutput, calls=%fused_computation.67 | convolution fusion | flops 1081471 | bytes 262176 | tf_op jit(solution)/shard_map/dot_general | solution.py:63
  1.9 4.1 %collective-permute-start = (bf16[8,4096]{1,0:T(8,128)(2,1)S(1)}, bf16[8,4096]{1,0:T(8,128)(2,1)S(1)}, u32[]{:S(2)}, u32[]{:S(2)}) collective-permute-start(bf16[8,4096]{1,0:T(8,128)(2,1)S(1)} %get-tuple-element.23), channel_id=1, source_target_pairs={{0,4},{1,5},{2,6},{3,7},{4,0},{5,1},{6,2},{7,3},{8,12},{9,13},{10,... | collective-permute-start | bytes 196616 | tf_op jit(solution)/shard_map/ppermute | solution.py:18
  6.0 3.6 %collective-permute-done = bf16[8,4096]{1,0:T(8,128)(2,1)S(1)} collective-permute-done((bf16[8,4096]{1,0:T(8,128)(2,1)S(1)}, bf16[8,4096]{1,0:T(8,128)(2,1)S(1)}, u32[]{:S(2)}, u32[]{:S(2)}) %collective-permute-start) | collective-permute-done | bytes 65568 | tf_op jit(solution)/shard_map/ppermute | solution.py:18
  9.7 1.6 %collective-permute-start.3 = (bf16[16,4096]{1,0:T(8,128)(2,1)S(1)}, bf16[16,4096]{1,0:T(8,128)(2,1)S(1)}, u32[]{:S(2)}, u32[]{:S(2)}) collective-permute-start(bf16[16,4096]{1,0:T(8,128)(2,1)S(1)} %pad_maximum_fusion.1), channel_id=1, source_target_pairs={{0,3},{1,2},{2,1},{3,0},{4,7},{5,6},{6,5},{7,4},{8,11},{9,10},{10,... | collective-permute-start | bytes 393224 | tf_op jit(solution)/shard_map/ppermute | solution.py:18
  11.3 1.7 %collective-permute-start.2 = (bf16[16,4096]{1,0:T(8,128)(2,1)S(1)}, bf16[16,4096]{1,0:T(8,128)(2,1)S(1)}, u32[]{:S(2)}, u32[]{:S(2)}) collective-permute-start(bf16[16,4096]{1,0:T(8,128)(2,1)S(1)} %pad_maximum_fusion.1), channel_id=1, source_target_pairs={{0,2},{1,3},{2,0},{3,1},{4,6},{5,7},{6,4},{7,5},{8,10},{9,11},{10,... | collective-permute-start | bytes 393224 | tf_op jit(solution)/shard_map/ppermute | solution.py:18
  12.9 0.3 collective-permute-start.1
  13.3 4.7 %collective-permute-done.1 = bf16[16,4096]{1,0:T(8,128)(2,1)S(1)} collective-permute-done((bf16[16,4096]{1,0:T(8,128)(2,1)S(1)}, bf16[16,4096]{1,0:T(8,128)(2,1)S(1)}, u32[]{:S(2)}, u32[]{:S(2)}) %collective-permute-start.1) | collective-permute-done | bytes 131104 | tf_op jit(solution)/shard_map/ppermute | solution.py:18
  18.0 0.3 fusion.16
  18.4 0.3 fusion.1
  18.7 0.9 %collective-permute-done.4 = f32[64,128]{1,0:T(8,128)S(1)} collective-permute-done((f32[64,128]{1,0:T(8,128)S(1)}, f32[64,128]{1,0:T(8,128)S(1)}, u32[]{:S(2)}, u32[]{:S(2)}) %collective-permute-start.4) | collective-permute-done | bytes 32800 | tf_op jit(solution)/shard_map/ppermute | solution.py:18
  19.6 0.3 fusion.14
  19.9 0.2 abs_reduce_fusion.3
  20.2 0.2 clamp_convert_fusion.3
  20.3 0.1 broadcast_in_dim.14
  20.4 1.2 %collective-permute-start.6 = (s16[16,4224]{1,0:T(8,128)(2,1)S(1)}, s16[16,4224]{1,0:T(8,128)(2,1)S(1)}, u32[]{:S(2)}, u32[]{:S(2)}) collective-permute-start(s16[16,4224]{1,0:T(8,128)(2,1)S(1)} %pad_add_fusion.1), channel_id=1, source_target_pairs={{0,2},{1,3},{2,0},{3,1},{4,6},{5,7},{6,4},{7,5},{8,10},{9,11},{10,... | collective-permute-start | bytes 405512 | tf_op jit(solution)/shard_map/ppermute | solution.py:18
  21.7 1.3 %collective-permute-start.7 = (s16[16,4224]{1,0:T(8,128)(2,1)S(1)}, s16[16,4224]{1,0:T(8,128)(2,1)S(1)}, u32[]{:S(2)}, u32[]{:S(2)}) collective-permute-start(s16[16,4224]{1,0:T(8,128)(2,1)S(1)} %pad_add_fusion.2), channel_id=1, source_target_pairs={{0,3},{1,2},{2,1},{3,0},{4,7},{5,6},{6,5},{7,4},{8,11},{9,10},{10,... | collective-permute-start | bytes 405512 | tf_op jit(solution)/shard_map/ppermute | solution.py:18
  23.1 1.2 %collective-permute-start.5 = (s16[16,4224]{1,0:T(8,128)(2,1)S(1)}, s16[16,4224]{1,0:T(8,128)(2,1)S(1)}, u32[]{:S(2)}, u32[]{:S(2)}) collective-permute-start(s16[16,4224]{1,0:T(8,128)(2,1)S(1)} %pad_add_fusion), channel_id=1, source_target_pairs={{0,1},{1,0},{2,3},{3,2},{4,5},{5,4},{6,7},{7,6},{8,9},{9,8},{10,11... | collective-permute-start | bytes 405512 | tf_op jit(solution)/shard_map/ppermute | solution.py:18
  24.3 2.6 %collective-permute-done.6 = s16[16,4224]{1,0:T(8,128)(2,1)S(1)} collective-permute-done((s16[16,4224]{1,0:T(8,128)(2,1)S(1)}, s16[16,4224]{1,0:T(8,128)(2,1)S(1)}, u32[]{:S(2)}, u32[]{:S(2)}) %collective-permute-start.6) | collective-permute-done | bytes 135200 | tf_op jit(solution)/shard_map/ppermute | solution.py:18
  27.0 0.1 fusion.37
  27.1 2.4 %collective-permute-done.7 = s16[16,4224]{1,0:T(8,128)(2,1)S(1)} collective-permute-done((s16[16,4224]{1,0:T(8,128)(2,1)S(1)}, s16[16,4224]{1,0:T(8,128)(2,1)S(1)}, u32[]{:S(2)}, u32[]{:S(2)}) %collective-permute-start.7) | collective-permute-done | bytes 135200 | tf_op jit(solution)/shard_map/ppermute | solution.py:18
  29.5 0.1 fusion.34
  29.6 1.5 %collective-permute-done.5 = s16[16,4224]{1,0:T(8,128)(2,1)S(1)} collective-permute-done((s16[16,4224]{1,0:T(8,128)(2,1)S(1)}, s16[16,4224]{1,0:T(8,128)(2,1)S(1)}, u32[]{:S(2)}, u32[]{:S(2)}) %collective-permute-start.5) | collective-permute-done | bytes 135200 | tf_op jit(solution)/shard_map/ppermute | solution.py:18
  31.2 0.1 fusion.40
  31.3 0.3 abs_reduce_fusion
  31.6 0.1 clamp_convert_fusion
  31.7 0.1 broadcast_in_dim.16
  31.8 3.5 %collective-permute-start.8 = (s16[16,4224]{1,0:T(8,128)(2,1)S(1)}, s16[16,4224]{1,0:T(8,128)(2,1)S(1)}, u32[]{:S(2)}, u32[]{:S(2)}) collective-permute-start(s16[16,4224]{1,0:T(8,128)(2,1)S(1)} %pad_add_fusion.3), channel_id=1, source_target_pairs={{0,4},{1,5},{2,6},{3,7},{4,0},{5,1},{6,2},{7,3},{8,12},{9,13},{10,... | collective-permute-start | bytes 405512 | tf_op jit(solution)/shard_map/ppermute | solution.py:18
  35.4 5.8 %collective-permute-done.8 = s16[16,4224]{1,0:T(8,128)(2,1)S(1)} collective-permute-done((s16[16,4224]{1,0:T(8,128)(2,1)S(1)}, s16[16,4224]{1,0:T(8,128)(2,1)S(1)}, u32[]{:S(2)}, u32[]{:S(2)}) %collective-permute-start.8) | collective-permute-done | bytes 135200 | tf_op jit(solution)/shard_map/ppermute | solution.py:18
  41.3 0.1 fusion.31
  41.4 0.1 fusion.18
  41.5 0.5 collective-permute-start.11
  42.1 1.3 %collective-permute-start.10 = (bf16[16,4096]{1,0:T(8,128)(2,1)S(1)}, bf16[16,4096]{1,0:T(8,128)(2,1)S(1)}, u32[]{:S(2)}, u32[]{:S(2)}) collective-permute-start(bf16[16,4096]{1,0:T(8,128)(2,1)S(1)} %fusion.23), channel_id=1, source_target_pairs={{0,2},{1,3},{2,0},{3,1},{4,6},{5,7},{6,4},{7,5},{8,10},{9,11},{10,... | collective-permute-start | bytes 393224 | tf_op jit(solution)/shard_map/ppermute | solution.py:18
  43.4 1.7 %collective-permute-start.9 = (bf16[16,4096]{1,0:T(8,128)(2,1)S(1)}, bf16[16,4096]{1,0:T(8,128)(2,1)S(1)}, u32[]{:S(2)}, u32[]{:S(2)}) collective-permute-start(bf16[16,4096]{1,0:T(8,128)(2,1)S(1)} %fusion.23), channel_id=1, source_target_pairs={{0,1},{1,0},{2,3},{3,2},{4,5},{5,4},{6,7},{7,6},{8,9},{9,8},{10,11... | collective-permute-start | bytes 393224 | tf_op jit(solution)/shard_map/ppermute | solution.py:18
  45.1 3.1 %collective-permute-done.11 = bf16[16,4096]{1,0:T(8,128)(2,1)S(1)} collective-permute-done((bf16[16,4096]{1,0:T(8,128)(2,1)S(1)}, bf16[16,4096]{1,0:T(8,128)(2,1)S(1)}, u32[]{:S(2)}, u32[]{:S(2)}) %collective-permute-start.11) | collective-permute-done | bytes 131104 | tf_op jit(solution)/shard_map/ppermute | solution.py:18
  48.2 0.4 collective-permute-done.10
  48.6 0.9 %collective-permute-done.9 = bf16[16,4096]{1,0:T(8,128)(2,1)S(1)} collective-permute-done((bf16[16,4096]{1,0:T(8,128)(2,1)S(1)}, bf16[16,4096]{1,0:T(8,128)(2,1)S(1)}, u32[]{:S(2)}, u32[]{:S(2)}) %collective-permute-start.9) | collective-permute-done | bytes 131104 | tf_op jit(solution)/shard_map/ppermute | solution.py:18
  49.5 0.5 fusion.12
  50.1 2.6 %multiply_reduce_fusion = (f32[]{:T(128)}, f32[128,4096]{1,0:T(8,128)S(1)}) fusion(bf16[1,128,4096]{2,1,0:T(8,128)(2,1)S(1)} %copy-done.3, bf16[1,128,4096]{2,1,0:T(8,128)(2,1)S(1)} %copy-done.1, f32[128]{0:T(128)S(1)} %get-tuple-element.12, bf16[64,128]{1,0:T(8,128)(2,1)S(1)} %get-tuple-element.6, bf16[16,4096]{1,0:T(8,128)(2,1)S(1)} %collective-permute-done.11, ...), kind=kOutput, calls=%fused_computation.20 | convolution fusion | flops 78118912 | bytes 5784068 | tf_op jit(solution)/shard_map/dot_general | solution.py:90
  52.7 3.5 %multiply_reduce_fusion.1 = (f32[]{:T(128)}, f32[4096,128]{1,0:T(8,128)}) fusion(bf16[1,4096,128]{2,1,0:T(8,128)(2,1)S(1)} %copy-done.5, bf16[64,4096]{1,0:T(8,128)(2,1)S(1)} %constant_dynamic-update-slice_fusion, f32[64,128]{1,0:T(8,128)S(1)} %fusion.12, f32[64,128]{1,0:T(8,128)S(1)} %collective-permute-done.12, f32[128]{0:T(128)S(1)} %get-tuple-element.13, ...), kind=kOutput, calls=%fused_computation.21 | convolution fusion | flops 73981952 | bytes 4850180 | tf_op jit(solution)/shard_map/dot_general | solution.py:102
  57.6 1.3 %collective-permute-start.14 = (f32[1,1]{1,0:T(1,128)}, f32[1,1]{1,0:T(1,128)}, u32[]{:S(2)}, u32[]{:S(2)}) collective-permute-start(f32[1,1]{1,0:T(1,128)} %bitcast.9), channel_id=1, source_target_pairs={{0,8},{8,0},{1,9},{9,1},{2,10},{10,2},{3,11},{11,3},{4,12},{12,4},... | collective-permute-start | bytes 20 | tf_op jit(solution)/shard_map/ppermute | solution.py:18
  59.5 2.0 %collective-permute-start.15 = (f32[1,1]{1,0:T(1,128)}, f32[1,1]{1,0:T(1,128)}, u32[]{:S(2)}, u32[]{:S(2)}) collective-permute-start(f32[1,1]{1,0:T(1,128)} %add.102), channel_id=1, source_target_pairs={{0,1},{1,0},{2,3},{3,2},{4,5},{5,4},{6,7},{7,6},{8,9},{9,8},{10,11... | collective-permute-start | bytes 20 | tf_op jit(solution)/shard_map/ppermute | solution.py:18
  61.5 1.6 %collective-permute-done.15 = f32[1,1]{1,0:T(1,128)} collective-permute-done((f32[1,1]{1,0:T(1,128)}, f32[1,1]{1,0:T(1,128)}, u32[]{:S(2)}, u32[]{:S(2)}) %collective-permute-start.15) | collective-permute-done | bytes 36 | tf_op jit(solution)/shard_map/ppermute | solution.py:18
  63.7 3.1 %collective-permute-start.16 = (f32[1,1]{1,0:T(1,128)}, f32[1,1]{1,0:T(1,128)}, u32[]{:S(2)}, u32[]{:S(2)}) collective-permute-start(f32[1,1]{1,0:T(1,128)} %add.103), channel_id=1, source_target_pairs={{0,2},{1,3},{2,0},{3,1},{4,6},{5,7},{6,4},{7,5},{8,10},{9,11},{10,... | collective-permute-start | bytes 20 | tf_op jit(solution)/shard_map/ppermute | solution.py:18
  66.8 0.5 collective-permute-done.16
  67.9 4.5 %collective-permute-start.17 = (f32[1,1]{1,0:T(1,128)}, f32[1,1]{1,0:T(1,128)}, u32[]{:S(2)}, u32[]{:S(2)}) collective-permute-start(f32[1,1]{1,0:T(1,128)} %add.104), channel_id=1, source_target_pairs={{0,4},{1,5},{2,6},{3,7},{4,0},{5,1},{6,2},{7,3},{8,12},{9,13},{10,... | collective-permute-start | bytes 20 | tf_op jit(solution)/shard_map/ppermute | solution.py:18
  72.3 0.2 collective-permute-done.17
  73.2 1.1 %fusion.11 = bf16[1,128,4096]{2,1,0:T(8,128)(2,1)} fusion(f32[128,4096]{1,0:T(8,128)S(1)} %get-tuple-element.27, f32[]{:T(128)} %bitcast.10), kind=kLoop, calls=%fused_computation.23 | loop fusion | flops 1048576 | bytes 3145732 | tf_op jit(solution)/shard_map/broadcast_in_dim | solution.py:115
  74.3 1.1 %fusion.10 = bf16[1,4096,128]{2,1,0:T(8,128)(2,1)} fusion(f32[4096,128]{1,0:T(8,128)S(1)} %copy-done.2, f32[]{:T(128)} %bitcast.10), kind=kLoop, calls=%fused_computation.22 | loop fusion | flops 1048576 | bytes 3145732 | tf_op jit(solution)/shard_map/broadcast_in_dim | solution.py:115
  (44 shorter events, 0.8 us)
Async XLA Ops:
  0.6 17.4 %copy-start = (bf16[1,4096,128]{2,1,0:T(8,128)(2,1)S(1)}, bf16[1,4096,128]{2,1,0:T(8,128)(2,1)}, u32[]{:S(2)}) copy-start(bf16[1,4096,128]{2,1,0:T(8,128)(2,1)} %param.10) | copy-start | bytes 3145732
  0.6 17.8 %copy-start.1 = (bf16[1,128,4096]{2,1,0:T(8,128)(2,1)S(1)}, bf16[1,128,4096]{2,1,0:T(8,128)(2,1)}, u32[]{:S(2)}) copy-start(bf16[1,128,4096]{2,1,0:T(8,128)(2,1)} %param.11) | copy-start | bytes 3145732
  1.9 7.7 %collective-permute-start = (bf16[8,4096]{1,0:T(8,128)(2,1)S(1)}, bf16[8,4096]{1,0:T(8,128)(2,1)S(1)}, u32[]{:S(2)}, u32[]{:S(2)}) collective-permute-start(bf16[8,4096]{1,0:T(8,128)(2,1)S(1)} %get-tuple-element.23), channel_id=1, source_target_pairs={{0,4},{1,5},{2,6},{3,7},{4,0},{5,1},{6,2},{7,3},{8,12},{9,13},{10,... | collective-permute-start | bytes 196616 | tf_op jit(solution)/shard_map/ppermute | solution.py:18
  9.7 8.3 %collective-permute-start.3 = (bf16[16,4096]{1,0:T(8,128)(2,1)S(1)}, bf16[16,4096]{1,0:T(8,128)(2,1)S(1)}, u32[]{:S(2)}, u32[]{:S(2)}) collective-permute-start(bf16[16,4096]{1,0:T(8,128)(2,1)S(1)} %pad_maximum_fusion.1), channel_id=1, source_target_pairs={{0,3},{1,2},{2,1},{3,0},{4,7},{5,6},{6,5},{7,4},{8,11},{9,10},{10,... | collective-permute-start | bytes 393224 | tf_op jit(solution)/shard_map/ppermute | solution.py:18
  11.3 6.7 %collective-permute-start.2 = (bf16[16,4096]{1,0:T(8,128)(2,1)S(1)}, bf16[16,4096]{1,0:T(8,128)(2,1)S(1)}, u32[]{:S(2)}, u32[]{:S(2)}) collective-permute-start(bf16[16,4096]{1,0:T(8,128)(2,1)S(1)} %pad_maximum_fusion.1), channel_id=1, source_target_pairs={{0,2},{1,3},{2,0},{3,1},{4,6},{5,7},{6,4},{7,5},{8,10},{9,11},{10,... | collective-permute-start | bytes 393224 | tf_op jit(solution)/shard_map/ppermute | solution.py:18
  12.9 5.0 %collective-permute-start.1 = (bf16[16,4096]{1,0:T(8,128)(2,1)S(1)}, bf16[16,4096]{1,0:T(8,128)(2,1)S(1)}, u32[]{:S(2)}, u32[]{:S(2)}) collective-permute-start(bf16[16,4096]{1,0:T(8,128)(2,1)S(1)} %pad_maximum_fusion.1), channel_id=1, source_target_pairs={{0,1},{1,0},{2,3},{3,2},{4,5},{5,4},{6,7},{7,6},{8,9},{9,8},{10,11... | collective-permute-start | bytes 393224 | tf_op jit(solution)/shard_map/ppermute | solution.py:18
  18.3 1.3 %collective-permute-start.4 = (f32[64,128]{1,0:T(8,128)S(1)}, f32[64,128]{1,0:T(8,128)S(1)}, u32[]{:S(2)}, u32[]{:S(2)}) collective-permute-start(f32[64,128]{1,0:T(8,128)S(1)} %fusion.16), channel_id=1, source_target_pairs={{0,8},{8,0},{1,9},{9,1},{2,10},{10,2},{3,11},{11,3},{4,12},{12,4},... | collective-permute-start | bytes 98312 | tf_op jit(solution)/shard_map/ppermute | solution.py:18
  20.4 6.5 %collective-permute-start.6 = (s16[16,4224]{1,0:T(8,128)(2,1)S(1)}, s16[16,4224]{1,0:T(8,128)(2,1)S(1)}, u32[]{:S(2)}, u32[]{:S(2)}) collective-permute-start(s16[16,4224]{1,0:T(8,128)(2,1)S(1)} %pad_add_fusion.1), channel_id=1, source_target_pairs={{0,2},{1,3},{2,0},{3,1},{4,6},{5,7},{6,4},{7,5},{8,10},{9,11},{10,... | collective-permute-start | bytes 405512 | tf_op jit(solution)/shard_map/ppermute | solution.py:18
  21.7 7.7 %collective-permute-start.7 = (s16[16,4224]{1,0:T(8,128)(2,1)S(1)}, s16[16,4224]{1,0:T(8,128)(2,1)S(1)}, u32[]{:S(2)}, u32[]{:S(2)}) collective-permute-start(s16[16,4224]{1,0:T(8,128)(2,1)S(1)} %pad_add_fusion.2), channel_id=1, source_target_pairs={{0,3},{1,2},{2,1},{3,0},{4,7},{5,6},{6,5},{7,4},{8,11},{9,10},{10,... | collective-permute-start | bytes 405512 | tf_op jit(solution)/shard_map/ppermute | solution.py:18
  23.1 8.1 %collective-permute-start.5 = (s16[16,4224]{1,0:T(8,128)(2,1)S(1)}, s16[16,4224]{1,0:T(8,128)(2,1)S(1)}, u32[]{:S(2)}, u32[]{:S(2)}) collective-permute-start(s16[16,4224]{1,0:T(8,128)(2,1)S(1)} %pad_add_fusion), channel_id=1, source_target_pairs={{0,1},{1,0},{2,3},{3,2},{4,5},{5,4},{6,7},{7,6},{8,9},{9,8},{10,11... | collective-permute-start | bytes 405512 | tf_op jit(solution)/shard_map/ppermute | solution.py:18
  31.8 9.4 %collective-permute-start.8 = (s16[16,4224]{1,0:T(8,128)(2,1)S(1)}, s16[16,4224]{1,0:T(8,128)(2,1)S(1)}, u32[]{:S(2)}, u32[]{:S(2)}) collective-permute-start(s16[16,4224]{1,0:T(8,128)(2,1)S(1)} %pad_add_fusion.3), channel_id=1, source_target_pairs={{0,4},{1,5},{2,6},{3,7},{4,0},{5,1},{6,2},{7,3},{8,12},{9,13},{10,... | collective-permute-start | bytes 405512 | tf_op jit(solution)/shard_map/ppermute | solution.py:18
  35.3 14.7 %copy-start.3 = (bf16[1,128,4096]{2,1,0:T(8,128)(2,1)S(1)}, bf16[1,128,4096]{2,1,0:T(8,128)(2,1)}, u32[]{:S(2)}) copy-start(bf16[1,128,4096]{2,1,0:T(8,128)(2,1)} %param.15) | copy-start | bytes 3145732
  35.3 14.7 %copy-start.4 = (bf16[1,128,4096]{2,1,0:T(8,128)(2,1)S(1)}, bf16[1,128,4096]{2,1,0:T(8,128)(2,1)}, u32[]{:S(2)}) copy-start(bf16[1,128,4096]{2,1,0:T(8,128)(2,1)} %param.14) | copy-start | bytes 3145732
  35.3 9.7 %collective-permute-start.13 = (f32[128]{0:T(128)S(1)}, f32[128]{0:T(128)S(1)}, u32[]{:S(2)}, u32[]{:S(2)}) collective-permute-start(f32[128]{0:T(128)S(1)} %add_sqrt_fusion), channel_id=1, source_target_pairs={{0,8},{8,0},{1,9},{9,1},{2,10},{10,2},{3,11},{11,3},{4,12},{12,4},... | collective-permute-start | bytes 1544 | tf_op jit(solution)/shard_map/ppermute | solution.py:18
  41.5 6.7 %collective-permute-start.11 = (bf16[16,4096]{1,0:T(8,128)(2,1)S(1)}, bf16[16,4096]{1,0:T(8,128)(2,1)S(1)}, u32[]{:S(2)}, u32[]{:S(2)}) collective-permute-start(bf16[16,4096]{1,0:T(8,128)(2,1)S(1)} %fusion.23), channel_id=1, source_target_pairs={{0,3},{1,2},{2,1},{3,0},{4,7},{5,6},{6,5},{7,4},{8,11},{9,10},{10,... | collective-permute-start | bytes 393224 | tf_op jit(solution)/shard_map/ppermute | solution.py:18
  42.1 6.5 %collective-permute-start.10 = (bf16[16,4096]{1,0:T(8,128)(2,1)S(1)}, bf16[16,4096]{1,0:T(8,128)(2,1)S(1)}, u32[]{:S(2)}, u32[]{:S(2)}) collective-permute-start(bf16[16,4096]{1,0:T(8,128)(2,1)S(1)} %fusion.23), channel_id=1, source_target_pairs={{0,2},{1,3},{2,0},{3,1},{4,6},{5,7},{6,4},{7,5},{8,10},{9,11},{10,... | collective-permute-start | bytes 393224 | tf_op jit(solution)/shard_map/ppermute | solution.py:18
  43.4 6.1 %collective-permute-start.9 = (bf16[16,4096]{1,0:T(8,128)(2,1)S(1)}, bf16[16,4096]{1,0:T(8,128)(2,1)S(1)}, u32[]{:S(2)}, u32[]{:S(2)}) collective-permute-start(bf16[16,4096]{1,0:T(8,128)(2,1)S(1)} %fusion.23), channel_id=1, source_target_pairs={{0,1},{1,0},{2,3},{3,2},{4,5},{5,4},{6,7},{7,6},{8,9},{9,8},{10,11... | collective-permute-start | bytes 393224 | tf_op jit(solution)/shard_map/ppermute | solution.py:18
  50.0 2.7 %collective-permute-start.12 = (f32[64,128]{1,0:T(8,128)S(1)}, f32[64,128]{1,0:T(8,128)S(1)}, u32[]{:S(2)}, u32[]{:S(2)}) collective-permute-start(f32[64,128]{1,0:T(8,128)S(1)} %fusion.12), channel_id=1, source_target_pairs={{0,8},{8,0},{1,9},{9,1},{2,10},{10,2},{3,11},{11,3},{4,12},{12,4},... | collective-permute-start | bytes 98312 | tf_op jit(solution)/shard_map/ppermute | solution.py:18
  50.1 2.6 %copy-start.5 = (bf16[1,4096,128]{2,1,0:T(8,128)(2,1)S(1)}, bf16[1,4096,128]{2,1,0:T(8,128)(2,1)}, u32[]{:S(2)}) copy-start(bf16[1,4096,128]{2,1,0:T(8,128)(2,1)} %param.13) | copy-start | bytes 3145732
  50.1 2.6 %copy-start.6 = (bf16[1,4096,128]{2,1,0:T(8,128)(2,1)S(1)}, bf16[1,4096,128]{2,1,0:T(8,128)(2,1)}, u32[]{:S(2)}) copy-start(bf16[1,4096,128]{2,1,0:T(8,128)(2,1)} %param.12) | copy-start | bytes 3145732
  57.6 16.8 %copy-start.2 = (f32[4096,128]{1,0:T(8,128)S(1)}, f32[4096,128]{1,0:T(8,128)}, u32[]{:S(2)}) copy-start(f32[4096,128]{1,0:T(8,128)} %get-tuple-element.25) | copy-start | bytes 6291460
  57.6 1.4 %collective-permute-start.14 = (f32[1,1]{1,0:T(1,128)}, f32[1,1]{1,0:T(1,128)}, u32[]{:S(2)}, u32[]{:S(2)}) collective-permute-start(f32[1,1]{1,0:T(1,128)} %bitcast.9), channel_id=1, source_target_pairs={{0,8},{8,0},{1,9},{9,1},{2,10},{10,2},{3,11},{11,3},{4,12},{12,4},... | collective-permute-start | bytes 20 | tf_op jit(solution)/shard_map/ppermute | solution.py:18
  59.5 3.6 %collective-permute-start.15 = (f32[1,1]{1,0:T(1,128)}, f32[1,1]{1,0:T(1,128)}, u32[]{:S(2)}, u32[]{:S(2)}) collective-permute-start(f32[1,1]{1,0:T(1,128)} %add.102), channel_id=1, source_target_pairs={{0,1},{1,0},{2,3},{3,2},{4,5},{5,4},{6,7},{7,6},{8,9},{9,8},{10,11... | collective-permute-start | bytes 20 | tf_op jit(solution)/shard_map/ppermute | solution.py:18
  63.7 3.6 %collective-permute-start.16 = (f32[1,1]{1,0:T(1,128)}, f32[1,1]{1,0:T(1,128)}, u32[]{:S(2)}, u32[]{:S(2)}) collective-permute-start(f32[1,1]{1,0:T(1,128)} %add.103), channel_id=1, source_target_pairs={{0,2},{1,3},{2,0},{3,1},{4,6},{5,7},{6,4},{7,5},{8,10},{9,11},{10,... | collective-permute-start | bytes 20 | tf_op jit(solution)/shard_map/ppermute | solution.py:18
  67.9 4.6 %collective-permute-start.17 = (f32[1,1]{1,0:T(1,128)}, f32[1,1]{1,0:T(1,128)}, u32[]{:S(2)}, u32[]{:S(2)}) collective-permute-start(f32[1,1]{1,0:T(1,128)} %add.104), channel_id=1, source_target_pairs={{0,4},{1,5},{2,6},{3,7},{4,0},{5,1},{6,2},{7,3},{8,12},{9,13},{10,... | collective-permute-start | bytes 20 | tf_op jit(solution)/shard_map/ppermute | solution.py:18

commit v2 on v1

--- a/solution.py
+++ b/solution.py
@@ -23,21 +23,27 @@
     second_wide = moment_two.astype(f32)
     new_first = beta_one * first_wide + (1.0 - beta_one) * gradient
     new_second = beta_two * second_wide + (1.0 - beta_two) * gradient * gradient
-    return new_first / (jnp.sqrt(new_second) + adam_eps)
+    size = new_second * lax.rsqrt(new_second) + adam_eps
+    return new_first * lax.rsqrt(size * size)
 
 
 def pack(value):
     top = jnp.max(jnp.abs(value), axis=-1, keepdims=True)
     level = jnp.ceil(16.0 * jnp.log2(jnp.maximum(top, 1e-30)))
-    scaled = jnp.round(value * (32767.0 * jnp.exp2(level * -0.0625)))
-    scaled = jnp.clip(scaled, -32767.0, 32767.0)
-    level = jnp.broadcast_to(level, value.shape[:-1] + (128,))
-    return jnp.concatenate([scaled, level], axis=-1).astype(jnp.int16)
+    scaled = jnp.round(value * (32766.0 * jnp.exp2(level * -0.0625)))
+    scaled = jnp.clip(scaled, -32766.0, 32766.0).astype(jnp.int32)
+    column = lax.broadcasted_iota(jnp.int32, value.shape, value.ndim - 1)
+    code = level.astype(jnp.int32) + 4096
+    bit = (code >> jnp.minimum(column, 15)) & 1
+    return jnp.where(column < 16, (scaled & -2) | bit, scaled).astype(jnp.int16)
 
 
 def unpack(packed):
-    wide = packed.astype(f32)
-    return wide[..., :-128] * (jnp.exp2(wide[..., -128:-127] * 0.0625) * (1.0 / 32767.0))
+    head = packed[..., :128].astype(jnp.int32) & 1
+    column = lax.broadcasted_iota(jnp.int32, head.shape, head.ndim - 1)
+    code = jnp.sum(jnp.where(column < 16, head << jnp.minimum(column, 15), 0), axis=-1, keepdims=True)
+    step = jnp.exp2((code - 4096).astype(f32) * 0.0625) * (1.0 / 32766.0)
+    return packed.astype(f32) * step
 
 
 def quad_gather(quarter):
@@ -103,13 +109,14 @@
         batch_rows, pre_grad, (((0,), (0,)), ((), ())), preferred_element_type=f32
     )
     enc_dir = adam_direction(grad_enc, m_enc, v_enc)
-    squares = jnp.sum(enc_dir * enc_dir) + jnp.sum(dec_dir * dec_dir)
-    squares = squares.reshape(1, 1)
+    squares = jnp.sum((enc_dir * enc_dir).reshape(-1, 8, 128), axis=0)
+    squares = squares + jnp.sum((dec_dir * dec_dir).reshape(latents // 8, 8, -1, 128), axis=(0, 2))
     squares = squares + swap(squares, "src", 1)
     bit = 1
     while bit < lat_count:
         squares = squares + swap(squares, "lat", bit)
         bit *= 2
+    squares = jnp.sum(squares)
     update_rms = jnp.sqrt(squares / float(2 * source_count * features * latents * lat_count))
     factor = 1.0 / jnp.maximum(1.0, update_rms / clip_rms)
     return ((enc_dir * factor).astype(bf16)[None], (dec_dir * factor).astype(bf16)[None])

time: 75.6 us -> 71.7 us (0.948)
  starting transfers between devices: 29.5 us -> 21.1 us
  waiting for transfers between devices: 28.1 us -> 35.1 us
  between operations: 4.71 us -> 1.64 us
  matrix products: 8.5 us -> 6.8 us
  other arithmetic: 4.15 us -> 5.85 us
    ppermute x18, starting transfers between devices: 29.5 us -> 21.1 us  [swap(): return lax.ppermute(value, axis, [(i, i ^ bits) for i in range(count)])]
    ppermute x18, waiting for transfers between devices: 28.1 us -> 35.1 us  [swap(): return lax.ppermute(value, axis, [(i, i ^ bits) for i in range(count)])]
    reduce_sum x1, other arithmetic: 0.28 us -> 1.52 us  [body(): dec_norm = jnp.sqrt(jnp.sum(dec_wide * dec_wide, axis=1) + norm_eps)]
    reduce_sum x0 -> x3, other arithmetic: none -> 0.87 us  [the longest x1 0.6 us: body(): squares = jnp.sum(squares)]
    dot_general x1, matrix products: 2.58 us -> 1.72 us  [body(): lax.dot_general(feature_codes, error_rows, (((0,), (0,)), ((), ())), pref...]
    unnamed x17, local copies, waits for them, and re-layouts: 0.06 us -> 0.91 us
    dot_general x1, matrix products: 3.55 us -> 2.71 us  [body(): lax.dot_general(batch_rows, pre_grad, (((0,), (0,)), ((), ())), preferred...]
where the time goes in v2:
time: 71.7 us; the launch traced here: 71.4 us
  waiting for transfers between devices  35.1 us (49%)
  starting transfers between devices  21.1 us (29%)
  matrix products  6.8 us (9%)
  other arithmetic  5.85 us (8%)
  between operations  1.64 us (2%)
  local copies, waits for them, and re-layouts  0.92 us (1%)
    ppermute x18, waiting for transfers between devices, swap(): return lax.ppermute(value, axis, [(i, i ^ bits) for i in range(count)])  35.1 us
    ppermute x18, starting transfers between devices, swap(): return lax.ppermute(value, axis, [(i, i ^ bits) for i in range(count)])  21.1 us
    dot_general x1, matrix products, body(): lax.dot_general(batch_rows, pre_grad, (((0,), (0,)), ((), ())), preferred...  2.71 us
    dot_general x1, matrix products, body(): lax.dot_general(feature_codes, error_rows, (((0,), (0,)), ((), ())), pref...  1.72 us
    reduce_sum x1, other arithmetic, body(): dec_norm = jnp.sqrt(jnp.sum(dec_wide * dec_wide, axis=1) + norm_eps)  1.52 us
  transfers between devices with their start and end apart: 18, of which 13 were waited for; matrix products, arithmetic and copies ran while one was open for 5% of the time, Pallas kernels for 0%

profile of v2, /device:TPU:0, one launch (start us, length us, event | category | flops | bytes accessed | tf_op | source)
XLA Modules:
  0.0 71.4 jit_solution(4930536055477061923)
XLA Ops:
  0.7 1.3 %constant_dynamic-update-slice_fusion.4 = (bf16[64,4096]{1,0:T(8,128)(2,1)S(1)}, bf16[8,4096]{1,0:T(8,128)(2,1)S(1)}) fusion(bf16[16,1,4096]{2,0,1:T(8,128)(2,1)} %param.8, s32[8]{0:T(128)} %param.9), kind=kOutput, calls=%fused_computation.65 | convolution fusion | flops 1081471 | bytes 262176 | tf_op jit(solution)/shard_map/dot_general | solution.py:69
  1.9 4.1 %collective-permute-start = (bf16[8,4096]{1,0:T(8,128)(2,1)S(1)}, bf16[8,4096]{1,0:T(8,128)(2,1)S(1)}, u32[]{:S(2)}, u32[]{:S(2)}) collective-permute-start(bf16[8,4096]{1,0:T(8,128)(2,1)S(1)} %get-tuple-element.18), channel_id=1, source_target_pairs={{0,4},{1,5},{2,6},{3,7},{4,0},{5,1},{6,2},{7,3},{8,12},{9,13},{10,... | collective-permute-start | bytes 196616 | tf_op jit(solution)/shard_map/ppermute | solution.py:18
  6.0 1.5 %fusion.1 = f32[128]{0:T(128)S(1)} fusion(bf16[1,128,4096]{2,1,0:T(8,128)(2,1)} %param.11), kind=kLoop, calls=%fused_computation.9 | loop fusion | flops 1572736 | bytes 1049088 | tf_op jit(solution)/shard_map/reduce_sum | solution.py:78
  7.5 2.1 %collective-permute-done = bf16[8,4096]{1,0:T(8,128)(2,1)S(1)} collective-permute-done((bf16[8,4096]{1,0:T(8,128)(2,1)S(1)}, bf16[8,4096]{1,0:T(8,128)(2,1)S(1)}, u32[]{:S(2)}, u32[]{:S(2)}) %collective-permute-start) | collective-permute-done | bytes 65568 | tf_op jit(solution)/shard_map/ppermute | solution.py:18
  9.7 1.6 %collective-permute-start.3 = (bf16[16,4096]{1,0:T(8,128)(2,1)S(1)}, bf16[16,4096]{1,0:T(8,128)(2,1)S(1)}, u32[]{:S(2)}, u32[]{:S(2)}) collective-permute-start(bf16[16,4096]{1,0:T(8,128)(2,1)S(1)} %pad_maximum_fusion.1), channel_id=1, source_target_pairs={{0,3},{1,2},{2,1},{3,0},{4,7},{5,6},{6,5},{7,4},{8,11},{9,10},{10,... | collective-permute-start | bytes 393224 | tf_op jit(solution)/shard_map/ppermute | solution.py:18
  11.3 1.7 %collective-permute-start.2 = (bf16[16,4096]{1,0:T(8,128)(2,1)S(1)}, bf16[16,4096]{1,0:T(8,128)(2,1)S(1)}, u32[]{:S(2)}, u32[]{:S(2)}) collective-permute-start(bf16[16,4096]{1,0:T(8,128)(2,1)S(1)} %pad_maximum_fusion.1), channel_id=1, source_target_pairs={{0,2},{1,3},{2,0},{3,1},{4,6},{5,7},{6,4},{7,5},{8,10},{9,11},{10,... | collective-permute-start | bytes 393224 | tf_op jit(solution)/shard_map/ppermute | solution.py:18
  12.9 0.3 collective-permute-start.1
  13.3 4.7 %collective-permute-done.1 = bf16[16,4096]{1,0:T(8,128)(2,1)S(1)} collective-permute-done((bf16[16,4096]{1,0:T(8,128)(2,1)S(1)}, bf16[16,4096]{1,0:T(8,128)(2,1)S(1)}, u32[]{:S(2)}, u32[]{:S(2)}) %collective-permute-start.1) | collective-permute-done | bytes 131104 | tf_op jit(solution)/shard_map/ppermute | solution.py:18
  18.0 0.3 fusion.18
  18.3 0.1 collective-permute-start.4
  18.4 1.2 %collective-permute-done.4 = f32[64,128]{1,0:T(8,128)S(1)} collective-permute-done((f32[64,128]{1,0:T(8,128)S(1)}, f32[64,128]{1,0:T(8,128)S(1)}, u32[]{:S(2)}, u32[]{:S(2)}) %collective-permute-start.4) | collective-permute-done | bytes 32800 | tf_op jit(solution)/shard_map/ppermute | solution.py:18
  19.6 0.3 fusion.16
  19.9 0.2 abs_reduce_fusion.3
  20.2 0.3 select_convert_fusion.1
  20.5 2.1 %collective-permute-start.7 = (s16[16,4096]{1,0:T(8,128)(2,1)S(1)}, s16[16,4096]{1,0:T(8,128)(2,1)S(1)}, u32[]{:S(2)}, u32[]{:S(2)}) collective-permute-start(s16[16,4096]{1,0:T(8,128)(2,1)S(1)} %get-tuple-element.12), channel_id=1, source_target_pairs={{0,3},{1,2},{2,1},{3,0},{4,7},{5,6},{6,5},{7,4},{8,11},{9,10},{10,... | collective-permute-start | bytes 393224 | tf_op jit(solution)/shard_map/ppermute | solution.py:18
  22.6 0.6 collective-permute-start.5
  23.2 0.9 %collective-permute-start.6 = (s16[16,4096]{1,0:T(8,128)(2,1)S(1)}, s16[16,4096]{1,0:T(8,128)(2,1)S(1)}, u32[]{:S(2)}, u32[]{:S(2)}) collective-permute-start(s16[16,4096]{1,0:T(8,128)(2,1)S(1)} %get-tuple-element.14), channel_id=1, source_target_pairs={{0,2},{1,3},{2,0},{3,1},{4,6},{5,7},{6,4},{7,5},{8,10},{9,11},{10,... | collective-permute-start | bytes 393224 | tf_op jit(solution)/shard_map/ppermute | solution.py:18
  24.1 3.7 %collective-permute-done.7 = s16[16,4096]{1,0:T(8,128)(2,1)S(1)} collective-permute-done((s16[16,4096]{1,0:T(8,128)(2,1)S(1)}, s16[16,4096]{1,0:T(8,128)(2,1)S(1)}, u32[]{:S(2)}, u32[]{:S(2)}) %collective-permute-start.7) | collective-permute-done | bytes 131104 | tf_op jit(solution)/shard_map/ppermute | solution.py:18
  27.8 2.0 %collective-permute-done.5 = s16[16,4096]{1,0:T(8,128)(2,1)S(1)} collective-permute-done((s16[16,4096]{1,0:T(8,128)(2,1)S(1)}, s16[16,4096]{1,0:T(8,128)(2,1)S(1)}, u32[]{:S(2)}, u32[]{:S(2)}) %collective-permute-start.5) | collective-permute-done | bytes 131104 | tf_op jit(solution)/shard_map/ppermute | solution.py:18
  29.8 0.2 select_reduce_fusion.3
  30.0 0.3 abs_reduce_fusion
  30.4 0.1 select_convert_fusion
  30.5 3.0 %collective-permute-start.8 = (s16[16,4096]{1,0:T(8,128)(2,1)S(1)}, s16[16,4096]{1,0:T(8,128)(2,1)S(1)}, u32[]{:S(2)}, u32[]{:S(2)}) collective-permute-start(s16[16,4096]{1,0:T(8,128)(2,1)S(1)} %select_convert_fusion), channel_id=1, source_target_pairs={{0,4},{1,5},{2,6},{3,7},{4,0},{5,1},{6,2},{7,3},{8,12},{9,13},{10,... | collective-permute-start | bytes 393224 | tf_op jit(solution)/shard_map/ppermute | solution.py:18
  33.5 6.5 %collective-permute-done.8 = s16[16,4096]{1,0:T(8,128)(2,1)S(1)} collective-permute-done((s16[16,4096]{1,0:T(8,128)(2,1)S(1)}, s16[16,4096]{1,0:T(8,128)(2,1)S(1)}, u32[]{:S(2)}, u32[]{:S(2)}) %collective-permute-start.8) | collective-permute-done | bytes 131104 | tf_op jit(solution)/shard_map/ppermute | solution.py:18
  40.0 0.1 select_reduce_fusion
  40.1 0.1 multiply_bitcast_fusion
  40.3 0.4 collective-permute-start.11
  40.6 1.8 %collective-permute-start.10 = (bf16[16,4096]{1,0:T(8,128)(2,1)S(1)}, bf16[16,4096]{1,0:T(8,128)(2,1)S(1)}, u32[]{:S(2)}, u32[]{:S(2)}) collective-permute-start(bf16[16,4096]{1,0:T(8,128)(2,1)S(1)} %fusion.23), channel_id=1, source_target_pairs={{0,2},{1,3},{2,0},{3,1},{4,6},{5,7},{6,4},{7,5},{8,10},{9,11},{10,... | collective-permute-start | bytes 393224 | tf_op jit(solution)/shard_map/ppermute | solution.py:18
  42.4 1.4 %collective-permute-start.9 = (bf16[16,4096]{1,0:T(8,128)(2,1)S(1)}, bf16[16,4096]{1,0:T(8,128)(2,1)S(1)}, u32[]{:S(2)}, u32[]{:S(2)}) collective-permute-start(bf16[16,4096]{1,0:T(8,128)(2,1)S(1)} %fusion.23), channel_id=1, source_target_pairs={{0,1},{1,0},{2,3},{3,2},{4,5},{5,4},{6,7},{7,6},{8,9},{9,8},{10,11... | collective-permute-start | bytes 393224 | tf_op jit(solution)/shard_map/ppermute | solution.py:18
  43.8 3.7 %collective-permute-done.11 = bf16[16,4096]{1,0:T(8,128)(2,1)S(1)} collective-permute-done((bf16[16,4096]{1,0:T(8,128)(2,1)S(1)}, bf16[16,4096]{1,0:T(8,128)(2,1)S(1)}, u32[]{:S(2)}, u32[]{:S(2)}) %collective-permute-start.11) | collective-permute-done | bytes 131104 | tf_op jit(solution)/shard_map/ppermute | solution.py:18
  47.6 0.5 collective-permute-done.10
  48.1 0.9 %collective-permute-done.9 = bf16[16,4096]{1,0:T(8,128)(2,1)S(1)} collective-permute-done((bf16[16,4096]{1,0:T(8,128)(2,1)S(1)}, bf16[16,4096]{1,0:T(8,128)(2,1)S(1)}, u32[]{:S(2)}, u32[]{:S(2)}) %collective-permute-start.9) | collective-permute-done | bytes 131104 | tf_op jit(solution)/shard_map/ppermute | solution.py:18
  49.0 0.5 fusion.14
  49.4 0.1 collective-permute-start.12
  49.6 1.7 %bitcast_reduce_fusion = (f32[8,128]{1,0:T(8,128)S(1)}, f32[128,4096]{1,0:T(8,128)S(1)}) fusion(bf16[1,128,4096]{2,1,0:T(8,128)(2,1)S(1)} %copy-done.3, bf16[1,128,4096]{2,1,0:T(8,128)(2,1)S(1)} %copy-done.1, f32[128]{0:T(128)S(1)} %get-tuple-element.15, bf16[64,128]{1,0:T(8,128)(2,1)S(1)} %get-tuple-element.9, ...), kind=kOutput, calls=%fused_computation.20 | convolution fusion | flops 79166464 | bytes 5788160 | tf_op jit(solution)/shard_map/dot_general | solution.py:96
  51.3 2.7 %bitcast_reduce_fusion.1 = (f32[8,128]{1,0:T(8,128)S(1)}, f32[4096,128]{1,0:T(8,128)}) fusion(bf16[1,4096,128]{2,1,0:T(8,128)(2,1)S(1)} %copy-done.5, bf16[64,4096]{1,0:T(8,128)(2,1)S(1)} %constant_dynamic-update-slice_fusion, f32[64,128]{1,0:T(8,128)S(1)} %fusion.14, f32[64,128]{1,0:T(8,128)S(1)} %collective-permute-done.12, ...), kind=kOutput, calls=%fused_computation.22 | convolution fusion | flops 75029504 | bytes 4854272 | tf_op jit(solution)/shard_map/dot_general | solution.py:108
  54.0 0.5 collective-permute-start.14
  54.5 0.8 %collective-permute-done.14 = f32[8,128]{1,0:T(8,128)S(1)} collective-permute-done((f32[8,128]{1,0:T(8,128)S(1)}, f32[8,128]{1,0:T(8,128)S(1)}, u32[]{:S(2)}, u32[]{:S(2)}) %collective-permute-start.14) | collective-permute-done | bytes 4128 | tf_op jit(solution)/shard_map/ppermute | solution.py:18
  55.3 0.6 collective-permute-start.15
  56.0 3.0 %collective-permute-done.15 = f32[8,128]{1,0:T(8,128)S(1)} collective-permute-done((f32[8,128]{1,0:T(8,128)S(1)}, f32[8,128]{1,0:T(8,128)S(1)}, u32[]{:S(2)}, u32[]{:S(2)}) %collective-permute-start.15) | collective-permute-done | bytes 4128 | tf_op jit(solution)/shard_map/ppermute | solution.py:18
  58.9 0.4 collective-permute-start.16
  59.3 3.2 %collective-permute-done.16 = f32[8,128]{1,0:T(8,128)S(1)} collective-permute-done((f32[8,128]{1,0:T(8,128)S(1)}, f32[8,128]{1,0:T(8,128)S(1)}, u32[]{:S(2)}, u32[]{:S(2)}) %collective-permute-start.16) | collective-permute-done | bytes 4128 | tf_op jit(solution)/shard_map/ppermute | solution.py:18
  62.5 1.8 %collective-permute-start.17 = (f32[8,128]{1,0:T(8,128)S(1)}, f32[8,128]{1,0:T(8,128)S(1)}, u32[]{:S(2)}, u32[]{:S(2)}) collective-permute-start(f32[8,128]{1,0:T(8,128)S(1)} %add.164), channel_id=1, source_target_pairs={{0,4},{1,5},{2,6},{3,7},{4,0},{5,1},{6,2},{7,3},{8,12},{9,13},{10,... | collective-permute-start | bytes 12296 | tf_op jit(solution)/shard_map/ppermute | solution.py:18
  64.3 2.8 %collective-permute-done.17 = f32[8,128]{1,0:T(8,128)S(1)} collective-permute-done((f32[8,128]{1,0:T(8,128)S(1)}, f32[8,128]{1,0:T(8,128)S(1)}, u32[]{:S(2)}, u32[]{:S(2)}) %collective-permute-start.17) | collective-permute-done | bytes 4128 | tf_op jit(solution)/shard_map/ppermute | solution.py:18
  67.1 0.6 add_reduce_fusion
  68.4 1.1 %fusion.13 = bf16[1,128,4096]{2,1,0:T(8,128)(2,1)} fusion(f32[128,4096]{1,0:T(8,128)S(1)} %get-tuple-element.22, f32[]{:T(128)S(6)} %div.13), kind=kLoop, calls=%fused_computation.27 | loop fusion | flops 1048576 | bytes 3145732 | tf_op jit(solution)/shard_map/broadcast_in_dim | solution.py:122
  69.5 0.8 %copy-done.2 = f32[4096,128]{1,0:T(8,128)S(1)} copy-done((f32[4096,128]{1,0:T(8,128)S(1)}, f32[4096,128]{1,0:T(8,128)}, u32[]{:S(2)}) %copy-start.2) | copy-done | bytes 2097176
  70.4 1.1 %fusion.12 = bf16[1,4096,128]{2,1,0:T(8,128)(2,1)} fusion(f32[4096,128]{1,0:T(8,128)S(1)} %copy-done.2, f32[]{:T(128)S(6)} %div.13), kind=kLoop, calls=%fused_computation.26 | loop fusion | flops 1048576 | bytes 3145732 | tf_op jit(solution)/shard_map/broadcast_in_dim | solution.py:122
  (46 shorter events, 0.3 us)
Async XLA Ops:
  0.6 17.4 %copy-start = (bf16[1,4096,128]{2,1,0:T(8,128)(2,1)S(1)}, bf16[1,4096,128]{2,1,0:T(8,128)(2,1)}, u32[]{:S(2)}) copy-start(bf16[1,4096,128]{2,1,0:T(8,128)(2,1)} %param.10) | copy-start | bytes 3145732
  0.6 19.0 %copy-start.1 = (bf16[1,128,4096]{2,1,0:T(8,128)(2,1)S(1)}, bf16[1,128,4096]{2,1,0:T(8,128)(2,1)}, u32[]{:S(2)}) copy-start(bf16[1,128,4096]{2,1,0:T(8,128)(2,1)} %param.11) | copy-start | bytes 3145732
  1.9 7.7 %collective-permute-start = (bf16[8,4096]{1,0:T(8,128)(2,1)S(1)}, bf16[8,4096]{1,0:T(8,128)(2,1)S(1)}, u32[]{:S(2)}, u32[]{:S(2)}) collective-permute-start(bf16[8,4096]{1,0:T(8,128)(2,1)S(1)} %get-tuple-element.18), channel_id=1, source_target_pairs={{0,4},{1,5},{2,6},{3,7},{4,0},{5,1},{6,2},{7,3},{8,12},{9,13},{10,... | collective-permute-start | bytes 196616 | tf_op jit(solution)/shard_map/ppermute | solution.py:18
  9.7 8.3 %collective-permute-start.3 = (bf16[16,4096]{1,0:T(8,128)(2,1)S(1)}, bf16[16,4096]{1,0:T(8,128)(2,1)S(1)}, u32[]{:S(2)}, u32[]{:S(2)}) collective-permute-start(bf16[16,4096]{1,0:T(8,128)(2,1)S(1)} %pad_maximum_fusion.1), channel_id=1, source_target_pairs={{0,3},{1,2},{2,1},{3,0},{4,7},{5,6},{6,5},{7,4},{8,11},{9,10},{10,... | collective-permute-start | bytes 393224 | tf_op jit(solution)/shard_map/ppermute | solution.py:18
  11.3 6.7 %collective-permute-start.2 = (bf16[16,4096]{1,0:T(8,128)(2,1)S(1)}, bf16[16,4096]{1,0:T(8,128)(2,1)S(1)}, u32[]{:S(2)}, u32[]{:S(2)}) collective-permute-start(bf16[16,4096]{1,0:T(8,128)(2,1)S(1)} %pad_maximum_fusion.1), channel_id=1, source_target_pairs={{0,2},{1,3},{2,0},{3,1},{4,6},{5,7},{6,4},{7,5},{8,10},{9,11},{10,... | collective-permute-start | bytes 393224 | tf_op jit(solution)/shard_map/ppermute | solution.py:18
  12.9 5.0 %collective-permute-start.1 = (bf16[16,4096]{1,0:T(8,128)(2,1)S(1)}, bf16[16,4096]{1,0:T(8,128)(2,1)S(1)}, u32[]{:S(2)}, u32[]{:S(2)}) collective-permute-start(bf16[16,4096]{1,0:T(8,128)(2,1)S(1)} %pad_maximum_fusion.1), channel_id=1, source_target_pairs={{0,1},{1,0},{2,3},{3,2},{4,5},{5,4},{6,7},{7,6},{8,9},{9,8},{10,11... | collective-permute-start | bytes 393224 | tf_op jit(solution)/shard_map/ppermute | solution.py:18
  18.3 1.3 %collective-permute-start.4 = (f32[64,128]{1,0:T(8,128)S(1)}, f32[64,128]{1,0:T(8,128)S(1)}, u32[]{:S(2)}, u32[]{:S(2)}) collective-permute-start(f32[64,128]{1,0:T(8,128)S(1)} %fusion.18), channel_id=1, source_target_pairs={{0,8},{8,0},{1,9},{9,1},{2,10},{10,2},{3,11},{11,3},{4,12},{12,4},... | collective-permute-start | bytes 98312 | tf_op jit(solution)/shard_map/ppermute | solution.py:18
  20.5 7.3 %collective-permute-start.7 = (s16[16,4096]{1,0:T(8,128)(2,1)S(1)}, s16[16,4096]{1,0:T(8,128)(2,1)S(1)}, u32[]{:S(2)}, u32[]{:S(2)}) collective-permute-start(s16[16,4096]{1,0:T(8,128)(2,1)S(1)} %get-tuple-element.12), channel_id=1, source_target_pairs={{0,3},{1,2},{2,1},{3,0},{4,7},{5,6},{6,5},{7,4},{8,11},{9,10},{10,... | collective-permute-start | bytes 393224 | tf_op jit(solution)/shard_map/ppermute | solution.py:18
  22.6 7.3 %collective-permute-start.5 = (s16[16,4096]{1,0:T(8,128)(2,1)S(1)}, s16[16,4096]{1,0:T(8,128)(2,1)S(1)}, u32[]{:S(2)}, u32[]{:S(2)}) collective-permute-start(s16[16,4096]{1,0:T(8,128)(2,1)S(1)} %get-tuple-element.13), channel_id=1, source_target_pairs={{0,1},{1,0},{2,3},{3,2},{4,5},{5,4},{6,7},{7,6},{8,9},{9,8},{10,11... | collective-permute-start | bytes 393224 | tf_op jit(solution)/shard_map/ppermute | solution.py:18
  23.2 6.7 %collective-permute-start.6 = (s16[16,4096]{1,0:T(8,128)(2,1)S(1)}, s16[16,4096]{1,0:T(8,128)(2,1)S(1)}, u32[]{:S(2)}, u32[]{:S(2)}) collective-permute-start(s16[16,4096]{1,0:T(8,128)(2,1)S(1)} %get-tuple-element.14), channel_id=1, source_target_pairs={{0,2},{1,3},{2,0},{3,1},{4,6},{5,7},{6,4},{7,5},{8,10},{9,11},{10,... | collective-permute-start | bytes 393224 | tf_op jit(solution)/shard_map/ppermute | solution.py:18
  30.4 19.2 %copy-start.3 = (bf16[1,128,4096]{2,1,0:T(8,128)(2,1)S(1)}, bf16[1,128,4096]{2,1,0:T(8,128)(2,1)}, u32[]{:S(2)}) copy-start(bf16[1,128,4096]{2,1,0:T(8,128)(2,1)} %param.15) | copy-start | bytes 3145732
  30.4 19.2 %copy-start.4 = (bf16[1,128,4096]{2,1,0:T(8,128)(2,1)S(1)}, bf16[1,128,4096]{2,1,0:T(8,128)(2,1)}, u32[]{:S(2)}) copy-start(bf16[1,128,4096]{2,1,0:T(8,128)(2,1)} %param.14) | copy-start | bytes 3145732
  30.5 9.4 %collective-permute-start.8 = (s16[16,4096]{1,0:T(8,128)(2,1)S(1)}, s16[16,4096]{1,0:T(8,128)(2,1)S(1)}, u32[]{:S(2)}, u32[]{:S(2)}) collective-permute-start(s16[16,4096]{1,0:T(8,128)(2,1)S(1)} %select_convert_fusion), channel_id=1, source_target_pairs={{0,4},{1,5},{2,6},{3,7},{4,0},{5,1},{6,2},{7,3},{8,12},{9,13},{10,... | collective-permute-start | bytes 393224 | tf_op jit(solution)/shard_map/ppermute | solution.py:18
  33.5 10.3 %collective-permute-start.13 = (f32[128]{0:T(128)S(1)}, f32[128]{0:T(128)S(1)}, u32[]{:S(2)}, u32[]{:S(2)}) collective-permute-start(f32[128]{0:T(128)S(1)} %add_sqrt_fusion), channel_id=1, source_target_pairs={{0,8},{8,0},{1,9},{9,1},{2,10},{10,2},{3,11},{11,3},{4,12},{12,4},... | collective-permute-start | bytes 1544 | tf_op jit(solution)/shard_map/ppermute | solution.py:18
  40.3 7.3 %collective-permute-start.11 = (bf16[16,4096]{1,0:T(8,128)(2,1)S(1)}, bf16[16,4096]{1,0:T(8,128)(2,1)S(1)}, u32[]{:S(2)}, u32[]{:S(2)}) collective-permute-start(bf16[16,4096]{1,0:T(8,128)(2,1)S(1)} %fusion.23), channel_id=1, source_target_pairs={{0,3},{1,2},{2,1},{3,0},{4,7},{5,6},{6,5},{7,4},{8,11},{9,10},{10,... | collective-permute-start | bytes 393224 | tf_op jit(solution)/shard_map/ppermute | solution.py:18
  40.6 7.5 %collective-permute-start.10 = (bf16[16,4096]{1,0:T(8,128)(2,1)S(1)}, bf16[16,4096]{1,0:T(8,128)(2,1)S(1)}, u32[]{:S(2)}, u32[]{:S(2)}) collective-permute-start(bf16[16,4096]{1,0:T(8,128)(2,1)S(1)} %fusion.23), channel_id=1, source_target_pairs={{0,2},{1,3},{2,0},{3,1},{4,6},{5,7},{6,4},{7,5},{8,10},{9,11},{10,... | collective-permute-start | bytes 393224 | tf_op jit(solution)/shard_map/ppermute | solution.py:18
  42.4 6.5 %collective-permute-start.9 = (bf16[16,4096]{1,0:T(8,128)(2,1)S(1)}, bf16[16,4096]{1,0:T(8,128)(2,1)S(1)}, u32[]{:S(2)}, u32[]{:S(2)}) collective-permute-start(bf16[16,4096]{1,0:T(8,128)(2,1)S(1)} %fusion.23), channel_id=1, source_target_pairs={{0,1},{1,0},{2,3},{3,2},{4,5},{5,4},{6,7},{7,6},{8,9},{9,8},{10,11... | collective-permute-start | bytes 393224 | tf_op jit(solution)/shard_map/ppermute | solution.py:18
  49.4 1.9 %collective-permute-start.12 = (f32[64,128]{1,0:T(8,128)S(1)}, f32[64,128]{1,0:T(8,128)S(1)}, u32[]{:S(2)}, u32[]{:S(2)}) collective-permute-start(f32[64,128]{1,0:T(8,128)S(1)} %fusion.14), channel_id=1, source_target_pairs={{0,8},{8,0},{1,9},{9,1},{2,10},{10,2},{3,11},{11,3},{4,12},{12,4},... | collective-permute-start | bytes 98312 | tf_op jit(solution)/shard_map/ppermute | solution.py:18
  49.5 1.8 %copy-start.5 = (bf16[1,4096,128]{2,1,0:T(8,128)(2,1)S(1)}, bf16[1,4096,128]{2,1,0:T(8,128)(2,1)}, u32[]{:S(2)}) copy-start(bf16[1,4096,128]{2,1,0:T(8,128)(2,1)} %param.13) | copy-start | bytes 3145732
  49.6 1.8 %copy-start.6 = (bf16[1,4096,128]{2,1,0:T(8,128)(2,1)S(1)}, bf16[1,4096,128]{2,1,0:T(8,128)(2,1)}, u32[]{:S(2)}) copy-start(bf16[1,4096,128]{2,1,0:T(8,128)(2,1)} %param.12) | copy-start | bytes 3145732
  54.0 1.3 %collective-permute-start.14 = (f32[8,128]{1,0:T(8,128)S(1)}, f32[8,128]{1,0:T(8,128)S(1)}, u32[]{:S(2)}, u32[]{:S(2)}) collective-permute-start(f32[8,128]{1,0:T(8,128)S(1)} %add.161), channel_id=1, source_target_pairs={{0,8},{8,0},{1,9},{9,1},{2,10},{10,2},{3,11},{11,3},{4,12},{12,4},... | collective-permute-start | bytes 12296 | tf_op jit(solution)/shard_map/ppermute | solution.py:18
  55.3 3.6 %collective-permute-start.15 = (f32[8,128]{1,0:T(8,128)S(1)}, f32[8,128]{1,0:T(8,128)S(1)}, u32[]{:S(2)}, u32[]{:S(2)}) collective-permute-start(f32[8,128]{1,0:T(8,128)S(1)} %add.162), channel_id=1, source_target_pairs={{0,1},{1,0},{2,3},{3,2},{4,5},{5,4},{6,7},{7,6},{8,9},{9,8},{10,11... | collective-permute-start | bytes 12296 | tf_op jit(solution)/shard_map/ppermute | solution.py:18
  58.9 3.6 %collective-permute-start.16 = (f32[8,128]{1,0:T(8,128)S(1)}, f32[8,128]{1,0:T(8,128)S(1)}, u32[]{:S(2)}, u32[]{:S(2)}) collective-permute-start(f32[8,128]{1,0:T(8,128)S(1)} %add.163), channel_id=1, source_target_pairs={{0,2},{1,3},{2,0},{3,1},{4,6},{5,7},{6,4},{7,5},{8,10},{9,11},{10,... | collective-permute-start | bytes 12296 | tf_op jit(solution)/shard_map/ppermute | solution.py:18
  62.5 4.5 %collective-permute-start.17 = (f32[8,128]{1,0:T(8,128)S(1)}, f32[8,128]{1,0:T(8,128)S(1)}, u32[]{:S(2)}, u32[]{:S(2)}) collective-permute-start(f32[8,128]{1,0:T(8,128)S(1)} %add.164), channel_id=1, source_target_pairs={{0,4},{1,5},{2,6},{3,7},{4,0},{5,1},{6,2},{7,3},{8,12},{9,13},{10,... | collective-permute-start | bytes 12296 | tf_op jit(solution)/shard_map/ppermute | solution.py:18
  68.4 2.0 %copy-start.2 = (f32[4096,128]{1,0:T(8,128)S(1)}, f32[4096,128]{1,0:T(8,128)}, u32[]{:S(2)}) copy-start(f32[4096,128]{1,0:T(8,128)} %get-tuple-element.20) | copy-start | bytes 6291460

commit v3 on v2

--- a/solution.py
+++ b/solution.py
@@ -1,6 +1,10 @@
+import functools
+
 import jax
 import jax.numpy as jnp
 from jax import lax
+from jax.experimental import pallas as pl
+from jax.experimental.pallas import tpu as pltpu
 from jax.sharding import PartitionSpec as P
 
 sparsity = 0.5
@@ -18,13 +22,45 @@
     return lax.ppermute(value, axis, [(i, i ^ bits) for i in range(count)])
 
 
-def adam_direction(gradient, moment_one, moment_two):
-    first_wide = moment_one.astype(f32)
-    second_wide = moment_two.astype(f32)
-    new_first = beta_one * first_wide + (1.0 - beta_one) * gradient
-    new_second = beta_two * second_wide + (1.0 - beta_two) * gradient * gradient
+def adam_direction(gradient, first_part, second_part):
+    new_first = first_part + (1.0 - beta_one) * gradient
+    new_second = second_part + (1.0 - beta_two) * gradient * gradient
     size = new_second * lax.rsqrt(new_second) + adam_eps
     return new_first * lax.rsqrt(size * size)
+
+
+def scale_kernel(count, squares_ref, enc_ref, dec_ref, enc_out, dec_out, enc_buf, dec_buf, sems):
+    total = jnp.sum(squares_ref[...], keepdims=True)
+    update_rms = jnp.sqrt(total / count)
+    factor = 1.0 / jnp.maximum(1.0, update_rms / clip_rms)
+    steps = 4
+    copies = []
+    for i in range(steps):
+        for j, (src, buf, out) in enumerate(((enc_ref, enc_buf, enc_out), (dec_ref, dec_buf, dec_out))):
+            rows = src.shape[0] // steps
+            part = pl.ds(i * rows, rows)
+            buf[part, :] = (src[part, :] * factor).astype(bf16)
+            copy = pltpu.make_async_copy(buf.at[part, :], out.at[part, :], sems.at[i, j])
+            copy.start()
+            copies.append(copy)
+    for copy in copies:
+        copy.wait()
+
+
+def scale(squares, enc_dir, dec_dir, count):
+    return pl.pallas_call(
+        functools.partial(scale_kernel, count),
+        out_shape=(jax.ShapeDtypeStruct(enc_dir.shape, bf16), jax.ShapeDtypeStruct(dec_dir.shape, bf16)),
+        in_specs=[pl.BlockSpec(memory_space=pltpu.VMEM)] * 3,
+        out_specs=[pl.BlockSpec(memory_space=pl.ANY)] * 2,
+        scratch_shapes=[
+            pltpu.VMEM(enc_dir.shape, bf16),
+            pltpu.VMEM(dec_dir.shape, bf16),
+            pltpu.SemaphoreType.DMA((4, 2)),
+        ],
+        compiler_params=pltpu.CompilerParams(vmem_limit_bytes=24 << 20),
+        name="scale_directions",
+    )(squares, enc_dir, dec_dir)
 
 
 def pack(value):
@@ -72,6 +108,15 @@
         quarter = jnp.concatenate([quarter, swap(quarter, "lat", bit)])
     quarter_count = quarter.shape[0]
     batch_rows = jnp.concatenate(quad_gather(quarter))
+    batch_rows, m_enc, v_enc, m_dec, v_dec = lax.optimization_barrier(
+        (
+            batch_rows,
+            beta_one * m_enc.astype(f32),
+            beta_two * v_enc.astype(f32),
+            beta_one * m_dec.astype(f32),
+            beta_two * v_dec.astype(f32),
+        )
+    )
 
     partial_value = jnp.dot(batch_rows, w_enc, preferred_element_type=f32)
     dec_wide = decoder_matrix.astype(f32)
@@ -116,10 +161,10 @@
     while bit < lat_count:
         squares = squares + swap(squares, "lat", bit)
         bit *= 2
-    squares = jnp.sum(squares)
-    update_rms = jnp.sqrt(squares / float(2 * source_count * features * latents * lat_count))
-    factor = 1.0 / jnp.maximum(1.0, update_rms / clip_rms)
-    return ((enc_dir * factor).astype(bf16)[None], (dec_dir * factor).astype(bf16)[None])
+    enc_step, dec_step = scale(
+        squares, enc_dir, dec_dir, float(2 * source_count * features * latents * lat_count)
+    )
+    return enc_step[None], dec_step[None]
 
 
 def solution(mesh):

time: 71.7 us -> 67.9 us (0.947)
  matrix products: 6.8 us -> 3.25 us
  waiting for transfers between devices: 35.1 us -> 32 us
  Pallas kernels: 0 us -> 1.56 us
  other arithmetic: 5.85 us -> 7.4 us
  starting transfers between devices: 21.1 us -> 22.5 us
  local copies, waits for them, and re-layouts: 0.92 us -> 0.06 us
  between operations: 1.64 us -> 0.92 us
    ppermute x18, waiting for transfers between devices: 35.1 us -> 32 us  [swap(): return lax.ppermute(value, axis, [(i, i ^ bits) for i in range(count)])]
    mul x0 -> x2, other arithmetic: none -> 2.51 us  [the longest x1 2.19 us: body(): beta_two * v_dec.astype(f32)]
    dot_general x1, matrix products: 2.71 us -> 0.49 us  [body(): lax.dot_general(batch_rows, pre_grad, (((0,), (0,)), ((), ())), preferred...]
    broadcast_in_dim x2 -> x0, other arithmetic: 2.2 us -> none  [the longest x1 1.12 us: body(): (dec_dir * factor).astype(bf16)[None]]
    pallas_call x0 -> x1, Pallas kernels: none -> 1.56 us  [scale(): pl.pallas_call(functools.partial(scale_kernel, count), out_shape=(jax.Sha...]
    ppermute x18, starting transfers between devices: 21.1 us -> 22.5 us  [swap(): return lax.ppermute(value, axis, [(i, i ^ bits) for i in range(count)])]
    dot_general x1, matrix products: 1.72 us -> 0.46 us  [body(): lax.dot_general(feature_codes, error_rows, (((0,), (0,)), ((), ())), pref...]
    reduce_sum x1 -> x2, other arithmetic: 0.6 us -> 1.79 us  [the longest x1 0.9 us: body(): jnp.sum((dec_dir * dec_dir).reshape(latents // 8, 8, -1, 128), axis=(0, 2))]
  transfers between devices with their start and end apart: 18 -> 18, of which waited for: 13 -> 15; matrix products, arithmetic and copies ran while one was open for 5% -> 8% of each run, Pallas kernels for 0% -> 0%
where the time goes in v3:
time: 67.9 us; the launch traced here: 67.7 us
  waiting for transfers between devices  32 us (47%)
  starting transfers between devices  22.5 us (33%)
  other arithmetic  7.4 us (11%)
  matrix products  3.25 us (5%)
  Pallas kernels  1.56 us (2%)
  between operations  0.92 us (1%)
    ppermute x18, waiting for transfers between devices, swap(): return lax.ppermute(value, axis, [(i, i ^ bits) for i in range(count)])  32 us
    ppermute x18, starting transfers between devices, swap(): return lax.ppermute(value, axis, [(i, i ^ bits) for i in range(count)])  22.5 us
    mul x1, other arithmetic, body(): beta_two * v_dec.astype(f32)  2.19 us
    pallas_call x1, Pallas kernels, scale(): pl.pallas_call(functools.partial(scale_kernel, count), out_shape=(jax.Sha...  1.56 us
    reduce_sum x1, other arithmetic, body(): dec_norm = jnp.sqrt(jnp.sum(dec_wide * dec_wide, axis=1) + norm_eps)  1.52 us
  transfers between devices with their start and end apart: 18, of which 15 were waited for; matrix products, arithmetic and copies ran while one was open for 8% of the time, Pallas kernels for 0%

profile of v3, /device:TPU:0, one launch (start us, length us, event | category | flops | bytes accessed | tf_op | source)
XLA Modules:
  0.0 67.7 jit_solution(5758953437680096114)
XLA Ops:
  0.6 1.2 %constant_dynamic-update-slice_fusion.4 = (bf16[64,4096]{1,0:T(8,128)(2,1)S(1)}, bf16[8,4096]{1,0:T(8,128)(2,1)S(1)}) fusion(bf16[16,1,4096]{2,0,1:T(8,128)(2,1)} %param.8, s32[8]{0:T(128)} %param.9), kind=kOutput, calls=%fused_computation.64 | convolution fusion | flops 1081471 | bytes 262176 | tf_op jit(solution)/shard_map/dot_general | solution.py:105
  1.9 4.1 %collective-permute-start = (bf16[8,4096]{1,0:T(8,128)(2,1)S(1)}, bf16[8,4096]{1,0:T(8,128)(2,1)S(1)}, u32[]{:S(2)}, u32[]{:S(2)}) collective-permute-start(bf16[8,4096]{1,0:T(8,128)(2,1)S(1)} %get-tuple-element.36), channel_id=1, source_target_pairs={{0,4},{1,5},{2,6},{3,7},{4,0},{5,1},{6,2},{7,3},{8,12},{9,13},{10,... | collective-permute-start | bytes 196616 | tf_op jit(solution)/shard_map/ppermute | solution.py:22
  6.0 1.5 %fusion.1 = f32[128]{0:T(128)S(1)} fusion(bf16[1,128,4096]{2,1,0:T(8,128)(2,1)} %param.11), kind=kLoop, calls=%fused_computation.9 | loop fusion | flops 1572736 | bytes 1049088 | tf_op jit(solution)/shard_map/reduce_sum | solution.py:123
  7.5 2.2 %multiply_bitcast_fusion = (f32[128,4096]{1,0:T(8,128)S(1)}, f32[128,4096]{1,0:T(8,128)S(1)}) fusion(bf16[1,128,4096]{2,1,0:T(8,128)(2,1)} %param.15, bf16[1,128,4096]{2,1,0:T(8,128)(2,1)} %param.14), kind=kLoop, calls=%fused_computation.22 | loop fusion | flops 2097152 | bytes 6291456 | tf_op jit(solution)/shard_map/mul | solution.py:117
  9.7 0.3 multiply_bitcast_fusion.2
  10.1 1.6 %collective-permute-start.1 = (bf16[16,4096]{1,0:T(8,128)(2,1)S(1)}, bf16[16,4096]{1,0:T(8,128)(2,1)S(1)}, u32[]{:S(2)}, u32[]{:S(2)}) collective-permute-start(bf16[16,4096]{1,0:T(8,128)(2,1)S(1)} %pad_maximum_fusion.1), channel_id=1, source_target_pairs={{0,1},{1,0},{2,3},{3,2},{4,5},{5,4},{6,7},{7,6},{8,9},{9,8},{10,11... | collective-permute-start | bytes 393224 | tf_op jit(solution)/shard_map/ppermute | solution.py:22
  11.7 1.6 %collective-permute-start.2 = (bf16[16,4096]{1,0:T(8,128)(2,1)S(1)}, bf16[16,4096]{1,0:T(8,128)(2,1)S(1)}, u32[]{:S(2)}, u32[]{:S(2)}) collective-permute-start(bf16[16,4096]{1,0:T(8,128)(2,1)S(1)} %pad_maximum_fusion.1), channel_id=1, source_target_pairs={{0,2},{1,3},{2,0},{3,1},{4,6},{5,7},{6,4},{7,5},{8,10},{9,11},{10,... | collective-permute-start | bytes 393224 | tf_op jit(solution)/shard_map/ppermute | solution.py:22
  13.2 0.4 collective-permute-start.3
  13.6 1.5 %collective-permute-done.1 = bf16[16,4096]{1,0:T(8,128)(2,1)S(1)} collective-permute-done((bf16[16,4096]{1,0:T(8,128)(2,1)S(1)}, bf16[16,4096]{1,0:T(8,128)(2,1)S(1)}, u32[]{:S(2)}, u32[]{:S(2)}) %collective-permute-start.1) | collective-permute-done | bytes 131104 | tf_op jit(solution)/shard_map/ppermute | solution.py:22
  15.1 2.6 %collective-permute-done.2 = bf16[16,4096]{1,0:T(8,128)(2,1)S(1)} collective-permute-done((bf16[16,4096]{1,0:T(8,128)(2,1)S(1)}, bf16[16,4096]{1,0:T(8,128)(2,1)S(1)}, u32[]{:S(2)}, u32[]{:S(2)}) %collective-permute-start.2) | collective-permute-done | bytes 131104 | tf_op jit(solution)/shard_map/ppermute | solution.py:22
  17.8 1.6 %collective-permute-done.3 = bf16[16,4096]{1,0:T(8,128)(2,1)S(1)} collective-permute-done((bf16[16,4096]{1,0:T(8,128)(2,1)S(1)}, bf16[16,4096]{1,0:T(8,128)(2,1)S(1)}, u32[]{:S(2)}, u32[]{:S(2)}) %collective-permute-start.3) | collective-permute-done | bytes 131104 | tf_op jit(solution)/shard_map/ppermute | solution.py:22
  19.4 0.3 fusion.16
  19.8 1.2 %collective-permute-done.4 = f32[64,128]{1,0:T(8,128)S(1)} collective-permute-done((f32[64,128]{1,0:T(8,128)S(1)}, f32[64,128]{1,0:T(8,128)S(1)}, u32[]{:S(2)}, u32[]{:S(2)}) %collective-permute-start.4) | collective-permute-done | bytes 32800 | tf_op jit(solution)/shard_map/ppermute | solution.py:22
  21.1 0.3 fusion.14
  21.3 0.2 abs_reduce_fusion.3
  21.6 0.3 select_convert_fusion.1
  22.0 1.3 %collective-permute-start.5 = (s16[16,4096]{1,0:T(8,128)(2,1)S(1)}, s16[16,4096]{1,0:T(8,128)(2,1)S(1)}, u32[]{:S(2)}, u32[]{:S(2)}) collective-permute-start(s16[16,4096]{1,0:T(8,128)(2,1)S(1)} %get-tuple-element.31), channel_id=1, source_target_pairs={{0,1},{1,0},{2,3},{3,2},{4,5},{5,4},{6,7},{7,6},{8,9},{9,8},{10,11... | collective-permute-start | bytes 393224 | tf_op jit(solution)/shard_map/ppermute | solution.py:22
  23.2 1.6 %collective-permute-start.6 = (s16[16,4096]{1,0:T(8,128)(2,1)S(1)}, s16[16,4096]{1,0:T(8,128)(2,1)S(1)}, u32[]{:S(2)}, u32[]{:S(2)}) collective-permute-start(s16[16,4096]{1,0:T(8,128)(2,1)S(1)} %get-tuple-element.32), channel_id=1, source_target_pairs={{0,2},{1,3},{2,0},{3,1},{4,6},{5,7},{6,4},{7,5},{8,10},{9,11},{10,... | collective-permute-start | bytes 393224 | tf_op jit(solution)/shard_map/ppermute | solution.py:22
  24.8 0.7 %collective-permute-start.7 = (s16[16,4096]{1,0:T(8,128)(2,1)S(1)}, s16[16,4096]{1,0:T(8,128)(2,1)S(1)}, u32[]{:S(2)}, u32[]{:S(2)}) collective-permute-start(s16[16,4096]{1,0:T(8,128)(2,1)S(1)} %get-tuple-element.30), channel_id=1, source_target_pairs={{0,3},{1,2},{2,1},{3,0},{4,7},{5,6},{6,5},{7,4},{8,11},{9,10},{10,... | collective-permute-start | bytes 393224 | tf_op jit(solution)/shard_map/ppermute | solution.py:22
  25.5 2.1 %collective-permute-done.5 = s16[16,4096]{1,0:T(8,128)(2,1)S(1)} collective-permute-done((s16[16,4096]{1,0:T(8,128)(2,1)S(1)}, s16[16,4096]{1,0:T(8,128)(2,1)S(1)}, u32[]{:S(2)}, u32[]{:S(2)}) %collective-permute-start.5) | collective-permute-done | bytes 131104 | tf_op jit(solution)/shard_map/ppermute | solution.py:22
  27.6 2.0 %collective-permute-done.6 = s16[16,4096]{1,0:T(8,128)(2,1)S(1)} collective-permute-done((s16[16,4096]{1,0:T(8,128)(2,1)S(1)}, s16[16,4096]{1,0:T(8,128)(2,1)S(1)}, u32[]{:S(2)}, u32[]{:S(2)}) %collective-permute-start.6) | collective-permute-done | bytes 131104 | tf_op jit(solution)/shard_map/ppermute | solution.py:22
  29.6 1.9 %collective-permute-done.7 = s16[16,4096]{1,0:T(8,128)(2,1)S(1)} collective-permute-done((s16[16,4096]{1,0:T(8,128)(2,1)S(1)}, s16[16,4096]{1,0:T(8,128)(2,1)S(1)}, u32[]{:S(2)}, u32[]{:S(2)}) %collective-permute-start.7) | collective-permute-done | bytes 131104 | tf_op jit(solution)/shard_map/ppermute | solution.py:22
  31.6 0.1 select_reduce_fusion.3
  31.8 0.3 abs_reduce_fusion
  32.1 0.2 select_convert_fusion
  32.3 1.7 %collective-permute-start.8 = (s16[16,4096]{1,0:T(8,128)(2,1)S(1)}, s16[16,4096]{1,0:T(8,128)(2,1)S(1)}, u32[]{:S(2)}, u32[]{:S(2)}) collective-permute-start(s16[16,4096]{1,0:T(8,128)(2,1)S(1)} %select_convert_fusion), channel_id=1, source_target_pairs={{0,4},{1,5},{2,6},{3,7},{4,0},{5,1},{6,2},{7,3},{8,12},{9,13},{10,... | collective-permute-start | bytes 393224 | tf_op jit(solution)/shard_map/ppermute | solution.py:22
  34.0 6.7 %collective-permute-done.8 = s16[16,4096]{1,0:T(8,128)(2,1)S(1)} collective-permute-done((s16[16,4096]{1,0:T(8,128)(2,1)S(1)}, s16[16,4096]{1,0:T(8,128)(2,1)S(1)}, u32[]{:S(2)}, u32[]{:S(2)}) %collective-permute-start.8) | collective-permute-done | bytes 131104 | tf_op jit(solution)/shard_map/ppermute | solution.py:22
  40.7 0.1 select_reduce_fusion
  40.8 0.1 multiply_bitcast_fusion.4
  41.0 2.4 %collective-permute-start.11 = (bf16[16,4096]{1,0:T(8,128)(2,1)S(1)}, bf16[16,4096]{1,0:T(8,128)(2,1)S(1)}, u32[]{:S(2)}, u32[]{:S(2)}) collective-permute-start(bf16[16,4096]{1,0:T(8,128)(2,1)S(1)} %fusion.21), channel_id=1, source_target_pairs={{0,3},{1,2},{2,1},{3,0},{4,7},{5,6},{6,5},{7,4},{8,11},{9,10},{10,... | collective-permute-start | bytes 393224 | tf_op jit(solution)/shard_map/ppermute | solution.py:22
  43.5 1.0 %collective-permute-start.9 = (bf16[16,4096]{1,0:T(8,128)(2,1)S(1)}, bf16[16,4096]{1,0:T(8,128)(2,1)S(1)}, u32[]{:S(2)}, u32[]{:S(2)}) collective-permute-start(bf16[16,4096]{1,0:T(8,128)(2,1)S(1)} %fusion.21), channel_id=1, source_target_pairs={{0,1},{1,0},{2,3},{3,2},{4,5},{5,4},{6,7},{7,6},{8,9},{9,8},{10,11... | collective-permute-start | bytes 393224 | tf_op jit(solution)/shard_map/ppermute | solution.py:22
  44.5 2.8 %collective-permute-done.10 = bf16[16,4096]{1,0:T(8,128)(2,1)S(1)} collective-permute-done((bf16[16,4096]{1,0:T(8,128)(2,1)S(1)}, bf16[16,4096]{1,0:T(8,128)(2,1)S(1)}, u32[]{:S(2)}, u32[]{:S(2)}) %collective-permute-start.10) | collective-permute-done | bytes 131104 | tf_op jit(solution)/shard_map/ppermute | solution.py:22
  47.3 1.1 %collective-permute-done.11 = bf16[16,4096]{1,0:T(8,128)(2,1)S(1)} collective-permute-done((bf16[16,4096]{1,0:T(8,128)(2,1)S(1)}, bf16[16,4096]{1,0:T(8,128)(2,1)S(1)}, u32[]{:S(2)}, u32[]{:S(2)}) %collective-permute-start.11) | collective-permute-done | bytes 131104 | tf_op jit(solution)/shard_map/ppermute | solution.py:22
  48.4 1.3 %collective-permute-done.9 = bf16[16,4096]{1,0:T(8,128)(2,1)S(1)} collective-permute-done((bf16[16,4096]{1,0:T(8,128)(2,1)S(1)}, bf16[16,4096]{1,0:T(8,128)(2,1)S(1)}, u32[]{:S(2)}, u32[]{:S(2)}) %collective-permute-start.9) | collective-permute-done | bytes 131104 | tf_op jit(solution)/shard_map/ppermute | solution.py:22
  49.7 0.5 fusion.12
  50.2 0.5 fusion
  50.7 0.9 %bitcast_reduce_fusion = (f32[8,128]{1,0:T(8,128)S(1)}, f32[128,4096]{1,0:T(8,128)S(1)}) fusion(f32[128,4096]{1,0:T(8,128)S(1)} %get-tuple-element.13, f32[128,4096]{1,0:T(8,128)S(1)} %fusion, f32[128,4096]{1,0:T(8,128)S(1)} %get-tuple-element.12), kind=kLoop, calls=%fused_computation.20 | loop fusion | flops 5766144 | bytes 8392704 | tf_op jit(solution)/shard_map/reduce_sum | solution.py:158
  51.6 0.5 fusion.23
  52.1 0.9 %bitcast_reduce_fusion.1 = (f32[8,128]{1,0:T(8,128)S(1)}, f32[4096,128]{1,0:T(8,128)S(1)}) fusion(f32[4096,128]{1,0:T(8,128)S(1)} %get-tuple-element.11, f32[4096,128]{1,0:T(8,128)S(1)} %fusion.23, f32[4096,128]{1,0:T(8,128)S(1)} %get-tuple-element.9), kind=kLoop, calls=%fused_computation.21 | loop fusion | flops 5766144 | bytes 8392704 | tf_op jit(solution)/shard_map/reduce_sum | solution.py:157
  53.0 0.6 collective-permute-start.14
  53.6 0.8 %collective-permute-done.14 = f32[8,128]{1,0:T(8,128)S(1)} collective-permute-done((f32[8,128]{1,0:T(8,128)S(1)}, f32[8,128]{1,0:T(8,128)S(1)}, u32[]{:S(2)}, u32[]{:S(2)}) %collective-permute-start.14) | collective-permute-done | bytes 4128 | tf_op jit(solution)/shard_map/ppermute | solution.py:22
  54.4 1.9 %collective-permute-start.15 = (f32[8,128]{1,0:T(8,128)S(1)}, f32[8,128]{1,0:T(8,128)S(1)}, u32[]{:S(2)}, u32[]{:S(2)}) collective-permute-start(f32[8,128]{1,0:T(8,128)S(1)} %add.162), channel_id=1, source_target_pairs={{0,1},{1,0},{2,3},{3,2},{4,5},{5,4},{6,7},{7,6},{8,9},{9,8},{10,11... | collective-permute-start | bytes 12296 | tf_op jit(solution)/shard_map/ppermute | solution.py:22
  56.3 1.7 %collective-permute-done.15 = f32[8,128]{1,0:T(8,128)S(1)} collective-permute-done((f32[8,128]{1,0:T(8,128)S(1)}, f32[8,128]{1,0:T(8,128)S(1)}, u32[]{:S(2)}, u32[]{:S(2)}) %collective-permute-start.15) | collective-permute-done | bytes 4128 | tf_op jit(solution)/shard_map/ppermute | solution.py:22
  58.0 0.9 %collective-permute-start.16 = (f32[8,128]{1,0:T(8,128)S(1)}, f32[8,128]{1,0:T(8,128)S(1)}, u32[]{:S(2)}, u32[]{:S(2)}) collective-permute-start(f32[8,128]{1,0:T(8,128)S(1)} %add.163), channel_id=1, source_target_pairs={{0,2},{1,3},{2,0},{3,1},{4,6},{5,7},{6,4},{7,5},{8,10},{9,11},{10,... | collective-permute-start | bytes 12296 | tf_op jit(solution)/shard_map/ppermute | solution.py:22
  59.0 2.7 %collective-permute-done.16 = f32[8,128]{1,0:T(8,128)S(1)} collective-permute-done((f32[8,128]{1,0:T(8,128)S(1)}, f32[8,128]{1,0:T(8,128)S(1)}, u32[]{:S(2)}, u32[]{:S(2)}) %collective-permute-start.16) | collective-permute-done | bytes 4128 | tf_op jit(solution)/shard_map/ppermute | solution.py:22
  61.6 2.5 %collective-permute-start.17 = (f32[8,128]{1,0:T(8,128)S(1)}, f32[8,128]{1,0:T(8,128)S(1)}, u32[]{:S(2)}, u32[]{:S(2)}) collective-permute-start(f32[8,128]{1,0:T(8,128)S(1)} %add.164), channel_id=1, source_target_pairs={{0,4},{1,5},{2,6},{3,7},{4,0},{5,1},{6,2},{7,3},{8,12},{9,13},{10,... | collective-permute-start | bytes 12296 | tf_op jit(solution)/shard_map/ppermute | solution.py:22
  64.1 2.0 %collective-permute-done.17 = f32[8,128]{1,0:T(8,128)S(1)} collective-permute-done((f32[8,128]{1,0:T(8,128)S(1)}, f32[8,128]{1,0:T(8,128)S(1)}, u32[]{:S(2)}, u32[]{:S(2)}) %collective-permute-start.17) | collective-permute-done | bytes 4128 | tf_op jit(solution)/shard_map/ppermute | solution.py:22
  66.1 1.6 %scale_directions.1 = (bf16[4096,128]{1,0:T(8,128)(2,1)}, bf16[128,4096]{1,0:T(8,128)(2,1)}) custom-call(f32[8,128]{1,0:T(8,128)S(1)} %add.165.squares_ref, f32[4096,128]{1,0:T(8,128)S(1)} %get-tuple-element.27.enc_ref, f32[128,4096]{1,0:T(8,128)S(1)} %get-tuple-element.23.dec_ref), custom_call_target="tpu_custom_call" | custom-call | tf_op jit(solution)/shard_map/scale_directions/pallas_call | solution.py:51
  (45 shorter events, 0.6 us)
Async XLA Ops:
  0.6 18.8 %copy-start = (bf16[1,4096,128]{2,1,0:T(8,128)(2,1)S(1)}, bf16[1,4096,128]{2,1,0:T(8,128)(2,1)}, u32[]{:S(2)}) copy-start(bf16[1,4096,128]{2,1,0:T(8,128)(2,1)} %param.10) | copy-start | bytes 3145732
  1.9 8.2 %collective-permute-start = (bf16[8,4096]{1,0:T(8,128)(2,1)S(1)}, bf16[8,4096]{1,0:T(8,128)(2,1)S(1)}, u32[]{:S(2)}, u32[]{:S(2)}) collective-permute-start(bf16[8,4096]{1,0:T(8,128)(2,1)S(1)} %get-tuple-element.36), channel_id=1, source_target_pairs={{0,4},{1,5},{2,6},{3,7},{4,0},{5,1},{6,2},{7,3},{8,12},{9,13},{10,... | collective-permute-start | bytes 196616 | tf_op jit(solution)/shard_map/ppermute | solution.py:22
  7.5 2.2 %copy-start.2 = (bf16[1,4096,128]{2,1,0:T(8,128)(2,1)S(1)}, bf16[1,4096,128]{2,1,0:T(8,128)(2,1)}, u32[]{:S(2)}) copy-start(bf16[1,4096,128]{2,1,0:T(8,128)(2,1)} %param.13) | copy-start | bytes 3145732
  7.5 2.2 %copy-start.3 = (bf16[1,4096,128]{2,1,0:T(8,128)(2,1)S(1)}, bf16[1,4096,128]{2,1,0:T(8,128)(2,1)}, u32[]{:S(2)}) copy-start(bf16[1,4096,128]{2,1,0:T(8,128)(2,1)} %param.12) | copy-start | bytes 3145732
  10.0 11.0 %copy-start.1 = (bf16[1,128,4096]{2,1,0:T(8,128)(2,1)S(1)}, bf16[1,128,4096]{2,1,0:T(8,128)(2,1)}, u32[]{:S(2)}) copy-start(bf16[1,128,4096]{2,1,0:T(8,128)(2,1)} %param.11) | copy-start | bytes 3145732
  10.1 5.0 %collective-permute-start.1 = (bf16[16,4096]{1,0:T(8,128)(2,1)S(1)}, bf16[16,4096]{1,0:T(8,128)(2,1)S(1)}, u32[]{:S(2)}, u32[]{:S(2)}) collective-permute-start(bf16[16,4096]{1,0:T(8,128)(2,1)S(1)} %pad_maximum_fusion.1), channel_id=1, source_target_pairs={{0,1},{1,0},{2,3},{3,2},{4,5},{5,4},{6,7},{7,6},{8,9},{9,8},{10,11... | collective-permute-start | bytes 393224 | tf_op jit(solution)/shard_map/ppermute | solution.py:22
  11.7 6.1 %collective-permute-start.2 = (bf16[16,4096]{1,0:T(8,128)(2,1)S(1)}, bf16[16,4096]{1,0:T(8,128)(2,1)S(1)}, u32[]{:S(2)}, u32[]{:S(2)}) collective-permute-start(bf16[16,4096]{1,0:T(8,128)(2,1)S(1)} %pad_maximum_fusion.1), channel_id=1, source_target_pairs={{0,2},{1,3},{2,0},{3,1},{4,6},{5,7},{6,4},{7,5},{8,10},{9,11},{10,... | collective-permute-start | bytes 393224 | tf_op jit(solution)/shard_map/ppermute | solution.py:22
  13.2 6.1 %collective-permute-start.3 = (bf16[16,4096]{1,0:T(8,128)(2,1)S(1)}, bf16[16,4096]{1,0:T(8,128)(2,1)S(1)}, u32[]{:S(2)}, u32[]{:S(2)}) collective-permute-start(bf16[16,4096]{1,0:T(8,128)(2,1)S(1)} %pad_maximum_fusion.1), channel_id=1, source_target_pairs={{0,3},{1,2},{2,1},{3,0},{4,7},{5,6},{6,5},{7,4},{8,11},{9,10},{10,... | collective-permute-start | bytes 393224 | tf_op jit(solution)/shard_map/ppermute | solution.py:22
  19.7 1.3 %collective-permute-start.4 = (f32[64,128]{1,0:T(8,128)S(1)}, f32[64,128]{1,0:T(8,128)S(1)}, u32[]{:S(2)}, u32[]{:S(2)}) collective-permute-start(f32[64,128]{1,0:T(8,128)S(1)} %fusion.16), channel_id=1, source_target_pairs={{0,8},{8,0},{1,9},{9,1},{2,10},{10,2},{3,11},{11,3},{4,12},{12,4},... | collective-permute-start | bytes 98312 | tf_op jit(solution)/shard_map/ppermute | solution.py:22
  22.0 5.6 %collective-permute-start.5 = (s16[16,4096]{1,0:T(8,128)(2,1)S(1)}, s16[16,4096]{1,0:T(8,128)(2,1)S(1)}, u32[]{:S(2)}, u32[]{:S(2)}) collective-permute-start(s16[16,4096]{1,0:T(8,128)(2,1)S(1)} %get-tuple-element.31), channel_id=1, source_target_pairs={{0,1},{1,0},{2,3},{3,2},{4,5},{5,4},{6,7},{7,6},{8,9},{9,8},{10,11... | collective-permute-start | bytes 393224 | tf_op jit(solution)/shard_map/ppermute | solution.py:22
  23.2 6.4 %collective-permute-start.6 = (s16[16,4096]{1,0:T(8,128)(2,1)S(1)}, s16[16,4096]{1,0:T(8,128)(2,1)S(1)}, u32[]{:S(2)}, u32[]{:S(2)}) collective-permute-start(s16[16,4096]{1,0:T(8,128)(2,1)S(1)} %get-tuple-element.32), channel_id=1, source_target_pairs={{0,2},{1,3},{2,0},{3,1},{4,6},{5,7},{6,4},{7,5},{8,10},{9,11},{10,... | collective-permute-start | bytes 393224 | tf_op jit(solution)/shard_map/ppermute | solution.py:22
  24.8 6.7 %collective-permute-start.7 = (s16[16,4096]{1,0:T(8,128)(2,1)S(1)}, s16[16,4096]{1,0:T(8,128)(2,1)S(1)}, u32[]{:S(2)}, u32[]{:S(2)}) collective-permute-start(s16[16,4096]{1,0:T(8,128)(2,1)S(1)} %get-tuple-element.30), channel_id=1, source_target_pairs={{0,3},{1,2},{2,1},{3,0},{4,7},{5,6},{6,5},{7,4},{8,11},{9,10},{10,... | collective-permute-start | bytes 393224 | tf_op jit(solution)/shard_map/ppermute | solution.py:22
  32.3 8.4 %collective-permute-start.8 = (s16[16,4096]{1,0:T(8,128)(2,1)S(1)}, s16[16,4096]{1,0:T(8,128)(2,1)S(1)}, u32[]{:S(2)}, u32[]{:S(2)}) collective-permute-start(s16[16,4096]{1,0:T(8,128)(2,1)S(1)} %select_convert_fusion), channel_id=1, source_target_pairs={{0,4},{1,5},{2,6},{3,7},{4,0},{5,1},{6,2},{7,3},{8,12},{9,13},{10,... | collective-permute-start | bytes 393224 | tf_op jit(solution)/shard_map/ppermute | solution.py:22
  34.0 10.6 %collective-permute-start.13 = (f32[128]{0:T(128)S(1)}, f32[128]{0:T(128)S(1)}, u32[]{:S(2)}, u32[]{:S(2)}) collective-permute-start(f32[128]{0:T(128)S(1)} %add_sqrt_fusion), channel_id=1, source_target_pairs={{0,8},{8,0},{1,9},{9,1},{2,10},{10,2},{3,11},{11,3},{4,12},{12,4},... | collective-permute-start | bytes 1544 | tf_op jit(solution)/shard_map/ppermute | solution.py:22
  41.0 6.3 %collective-permute-start.10 = (bf16[16,4096]{1,0:T(8,128)(2,1)S(1)}, bf16[16,4096]{1,0:T(8,128)(2,1)S(1)}, u32[]{:S(2)}, u32[]{:S(2)}) collective-permute-start(bf16[16,4096]{1,0:T(8,128)(2,1)S(1)} %fusion.21), channel_id=1, source_target_pairs={{0,2},{1,3},{2,0},{3,1},{4,6},{5,7},{6,4},{7,5},{8,10},{9,11},{10,... | collective-permute-start | bytes 393224 | tf_op jit(solution)/shard_map/ppermute | solution.py:22
  41.0 7.3 %collective-permute-start.11 = (bf16[16,4096]{1,0:T(8,128)(2,1)S(1)}, bf16[16,4096]{1,0:T(8,128)(2,1)S(1)}, u32[]{:S(2)}, u32[]{:S(2)}) collective-permute-start(bf16[16,4096]{1,0:T(8,128)(2,1)S(1)} %fusion.21), channel_id=1, source_target_pairs={{0,3},{1,2},{2,1},{3,0},{4,7},{5,6},{6,5},{7,4},{8,11},{9,10},{10,... | collective-permute-start | bytes 393224 | tf_op jit(solution)/shard_map/ppermute | solution.py:22
  43.5 6.2 %collective-permute-start.9 = (bf16[16,4096]{1,0:T(8,128)(2,1)S(1)}, bf16[16,4096]{1,0:T(8,128)(2,1)S(1)}, u32[]{:S(2)}, u32[]{:S(2)}) collective-permute-start(bf16[16,4096]{1,0:T(8,128)(2,1)S(1)} %fusion.21), channel_id=1, source_target_pairs={{0,1},{1,0},{2,3},{3,2},{4,5},{5,4},{6,7},{7,6},{8,9},{9,8},{10,11... | collective-permute-start | bytes 393224 | tf_op jit(solution)/shard_map/ppermute | solution.py:22
  50.1 1.5 %collective-permute-start.12 = (f32[64,128]{1,0:T(8,128)S(1)}, f32[64,128]{1,0:T(8,128)S(1)}, u32[]{:S(2)}, u32[]{:S(2)}) collective-permute-start(f32[64,128]{1,0:T(8,128)S(1)} %fusion.12), channel_id=1, source_target_pairs={{0,8},{8,0},{1,9},{9,1},{2,10},{10,2},{3,11},{11,3},{4,12},{12,4},... | collective-permute-start | bytes 98312 | tf_op jit(solution)/shard_map/ppermute | solution.py:22
  53.0 1.4 %collective-permute-start.14 = (f32[8,128]{1,0:T(8,128)S(1)}, f32[8,128]{1,0:T(8,128)S(1)}, u32[]{:S(2)}, u32[]{:S(2)}) collective-permute-start(f32[8,128]{1,0:T(8,128)S(1)} %add.161), channel_id=1, source_target_pairs={{0,8},{8,0},{1,9},{9,1},{2,10},{10,2},{3,11},{11,3},{4,12},{12,4},... | collective-permute-start | bytes 12296 | tf_op jit(solution)/shard_map/ppermute | solution.py:22
  54.4 3.6 %collective-permute-start.15 = (f32[8,128]{1,0:T(8,128)S(1)}, f32[8,128]{1,0:T(8,128)S(1)}, u32[]{:S(2)}, u32[]{:S(2)}) collective-permute-start(f32[8,128]{1,0:T(8,128)S(1)} %add.162), channel_id=1, source_target_pairs={{0,1},{1,0},{2,3},{3,2},{4,5},{5,4},{6,7},{7,6},{8,9},{9,8},{10,11... | collective-permute-start | bytes 12296 | tf_op jit(solution)/shard_map/ppermute | solution.py:22
  58.0 3.6 %collective-permute-start.16 = (f32[8,128]{1,0:T(8,128)S(1)}, f32[8,128]{1,0:T(8,128)S(1)}, u32[]{:S(2)}, u32[]{:S(2)}) collective-permute-start(f32[8,128]{1,0:T(8,128)S(1)} %add.163), channel_id=1, source_target_pairs={{0,2},{1,3},{2,0},{3,1},{4,6},{5,7},{6,4},{7,5},{8,10},{9,11},{10,... | collective-permute-start | bytes 12296 | tf_op jit(solution)/shard_map/ppermute | solution.py:22
  61.6 4.5 %collective-permute-start.17 = (f32[8,128]{1,0:T(8,128)S(1)}, f32[8,128]{1,0:T(8,128)S(1)}, u32[]{:S(2)}, u32[]{:S(2)}) collective-permute-start(f32[8,128]{1,0:T(8,128)S(1)} %add.164), channel_id=1, source_target_pairs={{0,4},{1,5},{2,6},{3,7},{4,0},{5,1},{6,2},{7,3},{8,12},{9,13},{10,... | collective-permute-start | bytes 12296 | tf_op jit(solution)/shard_map/ppermute | solution.py:22

commit v4 on v3

--- a/solution.py
+++ b/solution.py
@@ -108,27 +108,29 @@
         quarter = jnp.concatenate([quarter, swap(quarter, "lat", bit)])
     quarter_count = quarter.shape[0]
     batch_rows = jnp.concatenate(quad_gather(quarter))
-    batch_rows, m_enc, v_enc, m_dec, v_dec = lax.optimization_barrier(
+    partial_value = jnp.dot(batch_rows, w_enc, preferred_element_type=f32)
+    dec_wide = decoder_matrix.astype(f32)
+    dec_norm = jnp.sqrt(jnp.sum(dec_wide * dec_wide, axis=1) + norm_eps)
+    preact = partial_value + swap(partial_value, "src", 1)
+    norm_total = dec_norm + swap(dec_norm, "src", 1)
+    feature_codes = jnp.maximum(preact, 0.0).astype(bf16)
+    feature_codes, m_enc, v_enc, m_dec, v_dec = lax.optimization_barrier(
+        (feature_codes, m_enc, v_enc, m_dec, v_dec)
+    )
+    parts = jnp.dot(feature_codes, decoder_matrix, preferred_element_type=f32)
+    parts = parts.reshape(4, quarter_count, features)
+    total = parts[0]
+    for k in (1, 2, 3):
+        total = total + unpack(swap(pack(parts[k]), "lat", k))
+    total, m_enc, v_enc, m_dec, v_dec = lax.optimization_barrier(
         (
-            batch_rows,
+            total,
             beta_one * m_enc.astype(f32),
             beta_two * v_enc.astype(f32),
             beta_one * m_dec.astype(f32),
             beta_two * v_dec.astype(f32),
         )
     )
-
-    partial_value = jnp.dot(batch_rows, w_enc, preferred_element_type=f32)
-    dec_wide = decoder_matrix.astype(f32)
-    dec_norm = jnp.sqrt(jnp.sum(dec_wide * dec_wide, axis=1) + norm_eps)
-    preact = partial_value + swap(partial_value, "src", 1)
-    norm_total = dec_norm + swap(dec_norm, "src", 1)
-    feature_codes = jnp.maximum(preact, 0.0).astype(bf16)
-    parts = jnp.dot(feature_codes, decoder_matrix, preferred_element_type=f32)
-    parts = parts.reshape(4, quarter_count, features)
-    total = parts[0]
-    for k in (1, 2, 3):
-        total = total + unpack(swap(pack(parts[k]), "lat", k))
     for at, bit in enumerate(high_bits):
         other = unpack(swap(pack(total), "lat", bit))
         span = own_count << at

time: 67.9 us -> 65.7 us (0.968)
  other arithmetic: 7.4 us -> 3.74 us
  waiting for transfers between devices: 32 us -> 30.2 us
  matrix products: 3.25 us -> 5 us
  starting transfers between devices: 22.5 us -> 23.6 us
    mul x1, other arithmetic: 2.19 us -> 0.36 us  [body(): beta_two * v_dec.astype(f32)]
    reduce_sum x2 -> x0, other arithmetic: 1.79 us -> none  [the longest x1 0.9 us: body(): jnp.sum((dec_dir * dec_dir).reshape(latents // 8, 8, -1, 128), axis=(0, 2))]
    ppermute x18, waiting for transfers between devices: 32 us -> 30.2 us  [swap(): return lax.ppermute(value, axis, [(i, i ^ bits) for i in range(count)])]
    ppermute x18, starting transfers between devices: 22.5 us -> 23.6 us  [swap(): return lax.ppermute(value, axis, [(i, i ^ bits) for i in range(count)])]
    dot_general x1, matrix products: 0.46 us -> 1.49 us  [body(): lax.dot_general(feature_codes, error_rows, (((0,), (0,)), ((), ())), pref...]
  transfers between devices with their start and end apart: 18 -> 18, of which waited for: 15 -> 13; matrix products, arithmetic and copies ran while one was open for 8% -> 6% of each run, Pallas kernels for 0% -> 0%
where the time goes in v4:
time: 65.7 us; the launch traced here: 65.5 us
  waiting for transfers between devices  30.2 us (46%)
  starting transfers between devices  23.6 us (36%)
  matrix products  5 us (8%)
  other arithmetic  3.74 us (6%)
  Pallas kernels  1.56 us (2%)
  between operations  0.9 us (1%)
    ppermute x18, waiting for transfers between devices, swap(): return lax.ppermute(value, axis, [(i, i ^ bits) for i in range(count)])  30.2 us
    ppermute x18, starting transfers between devices, swap(): return lax.ppermute(value, axis, [(i, i ^ bits) for i in range(count)])  23.6 us
    pallas_call x1, Pallas kernels, scale(): pl.pallas_call(functools.partial(scale_kernel, count), out_shape=(jax.Sha...  1.56 us
    reduce_sum x1, other arithmetic, body(): dec_norm = jnp.sqrt(jnp.sum(dec_wide * dec_wide, axis=1) + norm_eps)  1.52 us
    dot_general x1, matrix products, body(): lax.dot_general(feature_codes, error_rows, (((0,), (0,)), ((), ())), pref...  1.49 us
  transfers between devices with their start and end apart: 18, of which 13 were waited for; matrix products, arithmetic and copies ran while one was open for 6% of the time, Pallas kernels for 0%

profile of v4, /device:TPU:0, one launch (start us, length us, event | category | flops | bytes accessed | tf_op | source)
XLA Modules:
  0.0 65.5 jit_solution(7690652449148905674)
XLA Ops:
  0.7 1.3 %constant_dynamic-update-slice_fusion.4 = (bf16[64,4096]{1,0:T(8,128)(2,1)S(1)}, bf16[8,4096]{1,0:T(8,128)(2,1)S(1)}) fusion(bf16[16,1,4096]{2,0,1:T(8,128)(2,1)} %param.8, s32[8]{0:T(128)} %param.9), kind=kOutput, calls=%fused_computation.63 | convolution fusion | flops 1081471 | bytes 262176 | tf_op jit(solution)/shard_map/dot_general | solution.py:105
  1.9 4.1 %collective-permute-start = (bf16[8,4096]{1,0:T(8,128)(2,1)S(1)}, bf16[8,4096]{1,0:T(8,128)(2,1)S(1)}, u32[]{:S(2)}, u32[]{:S(2)}) collective-permute-start(bf16[8,4096]{1,0:T(8,128)(2,1)S(1)} %get-tuple-element.38), channel_id=1, source_target_pairs={{0,4},{1,5},{2,6},{3,7},{4,0},{5,1},{6,2},{7,3},{8,12},{9,13},{10,... | collective-permute-start | bytes 196616 | tf_op jit(solution)/shard_map/ppermute | solution.py:22
  6.0 1.5 %fusion.1 = f32[128]{0:T(128)S(1)} fusion(bf16[1,128,4096]{2,1,0:T(8,128)(2,1)} %param.11), kind=kLoop, calls=%fused_computation.9 | loop fusion | flops 1572736 | bytes 1049088 | tf_op jit(solution)/shard_map/reduce_sum | solution.py:113
  7.6 2.1 %collective-permute-done = bf16[8,4096]{1,0:T(8,128)(2,1)S(1)} collective-permute-done((bf16[8,4096]{1,0:T(8,128)(2,1)S(1)}, bf16[8,4096]{1,0:T(8,128)(2,1)S(1)}, u32[]{:S(2)}, u32[]{:S(2)}) %collective-permute-start) | collective-permute-done | bytes 65568 | tf_op jit(solution)/shard_map/ppermute | solution.py:22
  9.7 1.6 %collective-permute-start.3 = (bf16[16,4096]{1,0:T(8,128)(2,1)S(1)}, bf16[16,4096]{1,0:T(8,128)(2,1)S(1)}, u32[]{:S(2)}, u32[]{:S(2)}) collective-permute-start(bf16[16,4096]{1,0:T(8,128)(2,1)S(1)} %pad_maximum_fusion.1), channel_id=1, source_target_pairs={{0,3},{1,2},{2,1},{3,0},{4,7},{5,6},{6,5},{7,4},{8,11},{9,10},{10,... | collective-permute-start | bytes 393224 | tf_op jit(solution)/shard_map/ppermute | solution.py:22
  11.3 1.7 %collective-permute-start.2 = (bf16[16,4096]{1,0:T(8,128)(2,1)S(1)}, bf16[16,4096]{1,0:T(8,128)(2,1)S(1)}, u32[]{:S(2)}, u32[]{:S(2)}) collective-permute-start(bf16[16,4096]{1,0:T(8,128)(2,1)S(1)} %pad_maximum_fusion.1), channel_id=1, source_target_pairs={{0,2},{1,3},{2,0},{3,1},{4,6},{5,7},{6,4},{7,5},{8,10},{9,11},{10,... | collective-permute-start | bytes 393224 | tf_op jit(solution)/shard_map/ppermute | solution.py:22
  12.9 0.3 collective-permute-start.1
  13.3 4.7 %collective-permute-done.1 = bf16[16,4096]{1,0:T(8,128)(2,1)S(1)} collective-permute-done((bf16[16,4096]{1,0:T(8,128)(2,1)S(1)}, bf16[16,4096]{1,0:T(8,128)(2,1)S(1)}, u32[]{:S(2)}, u32[]{:S(2)}) %collective-permute-start.1) | collective-permute-done | bytes 131104 | tf_op jit(solution)/shard_map/ppermute | solution.py:22
  18.0 0.3 fusion.16
  18.3 0.1 collective-permute-start.4
  18.4 1.2 %collective-permute-done.4 = f32[64,128]{1,0:T(8,128)S(1)} collective-permute-done((f32[64,128]{1,0:T(8,128)S(1)}, f32[64,128]{1,0:T(8,128)S(1)}, u32[]{:S(2)}, u32[]{:S(2)}) %collective-permute-start.4) | collective-permute-done | bytes 32800 | tf_op jit(solution)/shard_map/ppermute | solution.py:22
  19.6 0.3 fusion.14
  19.9 0.2 abs_reduce_fusion.3
  20.2 0.3 select_convert_fusion.3
  20.5 0.9 %collective-permute-start.5 = (s16[16,4096]{1,0:T(8,128)(2,1)S(1)}, s16[16,4096]{1,0:T(8,128)(2,1)S(1)}, u32[]{:S(2)}, u32[]{:S(2)}) collective-permute-start(s16[16,4096]{1,0:T(8,128)(2,1)S(1)} %get-tuple-element.32), channel_id=1, source_target_pairs={{0,1},{1,0},{2,3},{3,2},{4,5},{5,4},{6,7},{7,6},{8,9},{9,8},{10,11... | collective-permute-start | bytes 393224 | tf_op jit(solution)/shard_map/ppermute | solution.py:22
  21.4 1.7 %collective-permute-start.7 = (s16[16,4096]{1,0:T(8,128)(2,1)S(1)}, s16[16,4096]{1,0:T(8,128)(2,1)S(1)}, u32[]{:S(2)}, u32[]{:S(2)}) collective-permute-start(s16[16,4096]{1,0:T(8,128)(2,1)S(1)} %get-tuple-element.33), channel_id=1, source_target_pairs={{0,3},{1,2},{2,1},{3,0},{4,7},{5,6},{6,5},{7,4},{8,11},{9,10},{10,... | collective-permute-start | bytes 393224 | tf_op jit(solution)/shard_map/ppermute | solution.py:22
  23.2 0.9 %collective-permute-start.6 = (s16[16,4096]{1,0:T(8,128)(2,1)S(1)}, s16[16,4096]{1,0:T(8,128)(2,1)S(1)}, u32[]{:S(2)}, u32[]{:S(2)}) collective-permute-start(s16[16,4096]{1,0:T(8,128)(2,1)S(1)} %get-tuple-element.34), channel_id=1, source_target_pairs={{0,2},{1,3},{2,0},{3,1},{4,6},{5,7},{6,4},{7,5},{8,10},{9,11},{10,... | collective-permute-start | bytes 393224 | tf_op jit(solution)/shard_map/ppermute | solution.py:22
  24.1 0.3 convert_multiply_fusion.4
  24.4 0.3 copy-done.5
  24.7 0.4 convert_multiply_fusion.2
  25.1 3.8 %collective-permute-done.5 = s16[16,4096]{1,0:T(8,128)(2,1)S(1)} collective-permute-done((s16[16,4096]{1,0:T(8,128)(2,1)S(1)}, s16[16,4096]{1,0:T(8,128)(2,1)S(1)}, u32[]{:S(2)}, u32[]{:S(2)}) %collective-permute-start.5) | collective-permute-done | bytes 131104 | tf_op jit(solution)/shard_map/ppermute | solution.py:22
  28.9 1.2 %collective-permute-done.6 = s16[16,4096]{1,0:T(8,128)(2,1)S(1)} collective-permute-done((s16[16,4096]{1,0:T(8,128)(2,1)S(1)}, s16[16,4096]{1,0:T(8,128)(2,1)S(1)}, u32[]{:S(2)}, u32[]{:S(2)}) %collective-permute-start.6) | collective-permute-done | bytes 131104 | tf_op jit(solution)/shard_map/ppermute | solution.py:22
  30.2 0.1 select_reduce_fusion.3
  30.3 0.2 fusion.19
  30.5 0.1 abs_reduce_fusion
  30.7 0.2 select_convert_fusion
  30.8 3.0 %collective-permute-start.8 = (s16[16,4096]{1,0:T(8,128)(2,1)S(1)}, s16[16,4096]{1,0:T(8,128)(2,1)S(1)}, u32[]{:S(2)}, u32[]{:S(2)}) collective-permute-start(s16[16,4096]{1,0:T(8,128)(2,1)S(1)} %select_convert_fusion), channel_id=1, source_target_pairs={{0,4},{1,5},{2,6},{3,7},{4,0},{5,1},{6,2},{7,3},{8,12},{9,13},{10,... | collective-permute-start | bytes 393224 | tf_op jit(solution)/shard_map/ppermute | solution.py:22
  33.8 5.5 %collective-permute-done.8 = s16[16,4096]{1,0:T(8,128)(2,1)S(1)} collective-permute-done((s16[16,4096]{1,0:T(8,128)(2,1)S(1)}, s16[16,4096]{1,0:T(8,128)(2,1)S(1)}, u32[]{:S(2)}, u32[]{:S(2)}) %collective-permute-start.8) | collective-permute-done | bytes 131104 | tf_op jit(solution)/shard_map/ppermute | solution.py:22
  39.3 0.1 select_reduce_fusion
  39.5 0.1 multiply_bitcast_fusion
  39.6 1.1 %collective-permute-start.11 = (bf16[16,4096]{1,0:T(8,128)(2,1)S(1)}, bf16[16,4096]{1,0:T(8,128)(2,1)S(1)}, u32[]{:S(2)}, u32[]{:S(2)}) collective-permute-start(bf16[16,4096]{1,0:T(8,128)(2,1)S(1)} %fusion.21), channel_id=1, source_target_pairs={{0,3},{1,2},{2,1},{3,0},{4,7},{5,6},{6,5},{7,4},{8,11},{9,10},{10,... | collective-permute-start | bytes 393224 | tf_op jit(solution)/shard_map/ppermute | solution.py:22
  40.7 1.5 %collective-permute-start.10 = (bf16[16,4096]{1,0:T(8,128)(2,1)S(1)}, bf16[16,4096]{1,0:T(8,128)(2,1)S(1)}, u32[]{:S(2)}, u32[]{:S(2)}) collective-permute-start(bf16[16,4096]{1,0:T(8,128)(2,1)S(1)} %fusion.21), channel_id=1, source_target_pairs={{0,2},{1,3},{2,0},{3,1},{4,6},{5,7},{6,4},{7,5},{8,10},{9,11},{10,... | collective-permute-start | bytes 393224 | tf_op jit(solution)/shard_map/ppermute | solution.py:22
  42.3 0.9 %collective-permute-start.9 = (bf16[16,4096]{1,0:T(8,128)(2,1)S(1)}, bf16[16,4096]{1,0:T(8,128)(2,1)S(1)}, u32[]{:S(2)}, u32[]{:S(2)}) collective-permute-start(bf16[16,4096]{1,0:T(8,128)(2,1)S(1)} %fusion.21), channel_id=1, source_target_pairs={{0,1},{1,0},{2,3},{3,2},{4,5},{5,4},{6,7},{7,6},{8,9},{9,8},{10,11... | collective-permute-start | bytes 393224 | tf_op jit(solution)/shard_map/ppermute | solution.py:22
  43.2 3.0 %collective-permute-done.11 = bf16[16,4096]{1,0:T(8,128)(2,1)S(1)} collective-permute-done((bf16[16,4096]{1,0:T(8,128)(2,1)S(1)}, bf16[16,4096]{1,0:T(8,128)(2,1)S(1)}, u32[]{:S(2)}, u32[]{:S(2)}) %collective-permute-start.11) | collective-permute-done | bytes 131104 | tf_op jit(solution)/shard_map/ppermute | solution.py:22
  46.2 0.8 %collective-permute-done.10 = bf16[16,4096]{1,0:T(8,128)(2,1)S(1)} collective-permute-done((bf16[16,4096]{1,0:T(8,128)(2,1)S(1)}, bf16[16,4096]{1,0:T(8,128)(2,1)S(1)}, u32[]{:S(2)}, u32[]{:S(2)}) %collective-permute-start.10) | collective-permute-done | bytes 131104 | tf_op jit(solution)/shard_map/ppermute | solution.py:22
  47.0 0.5 collective-permute-done.9
  47.6 0.5 fusion.12
  48.1 1.5 %bitcast_reduce_fusion = (f32[8,128]{1,0:T(8,128)S(1)}, f32[128,4096]{1,0:T(8,128)S(1)}) fusion(f32[128,4096]{1,0:T(8,128)S(1)} %get-tuple-element.23, f32[128,4096]{1,0:T(8,128)S(1)} %get-tuple-element.22, bf16[1,128,4096]{2,1,0:T(8,128)(2,1)S(1)} %copy-done.1, f32[128]{0:T(128)S(1)} %get-tuple-element.35, bf16[64,128]{1,0:T(8,128)(2,1)S(1)} %maximum_convert_fusion, ...), kind=kOutput, calls=%fused_computation.20 | convolution fusion | flops 77069312 | bytes 7885312 | tf_op jit(solution)/shard_map/dot_general | solution.py:143
  49.6 1.1 %bitcast_reduce_fusion.1 = (f32[8,128]{1,0:T(8,128)S(1)}, f32[4096,128]{1,0:T(8,128)S(1)}) fusion(f32[4096,128]{1,0:T(8,128)S(1)} %get-tuple-element.21, f32[4096,128]{1,0:T(8,128)S(1)} %get-tuple-element.19, bf16[64,4096]{1,0:T(8,128)(2,1)S(1)} %constant_dynamic-update-slice_fusion, f32[64,128]{1,0:T(8,128)S(1)} %fusion.12, ...), kind=kOutput, calls=%fused_computation.21 | convolution fusion | flops 72932352 | bytes 6951424 | tf_op jit(solution)/shard_map/dot_general | solution.py:155
  50.8 0.6 collective-permute-start.14
  51.4 0.8 %collective-permute-done.14 = f32[8,128]{1,0:T(8,128)S(1)} collective-permute-done((f32[8,128]{1,0:T(8,128)S(1)}, f32[8,128]{1,0:T(8,128)S(1)}, u32[]{:S(2)}, u32[]{:S(2)}) %collective-permute-start.14) | collective-permute-done | bytes 4128 | tf_op jit(solution)/shard_map/ppermute | solution.py:22
  52.2 0.9 %collective-permute-start.15 = (f32[8,128]{1,0:T(8,128)S(1)}, f32[8,128]{1,0:T(8,128)S(1)}, u32[]{:S(2)}, u32[]{:S(2)}) collective-permute-start(f32[8,128]{1,0:T(8,128)S(1)} %add.162), channel_id=1, source_target_pairs={{0,1},{1,0},{2,3},{3,2},{4,5},{5,4},{6,7},{7,6},{8,9},{9,8},{10,11... | collective-permute-start | bytes 12296 | tf_op jit(solution)/shard_map/ppermute | solution.py:22
  53.1 2.7 %collective-permute-done.15 = f32[8,128]{1,0:T(8,128)S(1)} collective-permute-done((f32[8,128]{1,0:T(8,128)S(1)}, f32[8,128]{1,0:T(8,128)S(1)}, u32[]{:S(2)}, u32[]{:S(2)}) %collective-permute-start.15) | collective-permute-done | bytes 4128 | tf_op jit(solution)/shard_map/ppermute | solution.py:22
  55.8 1.5 %collective-permute-start.16 = (f32[8,128]{1,0:T(8,128)S(1)}, f32[8,128]{1,0:T(8,128)S(1)}, u32[]{:S(2)}, u32[]{:S(2)}) collective-permute-start(f32[8,128]{1,0:T(8,128)S(1)} %add.163), channel_id=1, source_target_pairs={{0,2},{1,3},{2,0},{3,1},{4,6},{5,7},{6,4},{7,5},{8,10},{9,11},{10,... | collective-permute-start | bytes 12296 | tf_op jit(solution)/shard_map/ppermute | solution.py:22
  57.3 2.1 %collective-permute-done.16 = f32[8,128]{1,0:T(8,128)S(1)} collective-permute-done((f32[8,128]{1,0:T(8,128)S(1)}, f32[8,128]{1,0:T(8,128)S(1)}, u32[]{:S(2)}, u32[]{:S(2)}) %collective-permute-start.16) | collective-permute-done | bytes 4128 | tf_op jit(solution)/shard_map/ppermute | solution.py:22
  59.4 2.8 %collective-permute-start.17 = (f32[8,128]{1,0:T(8,128)S(1)}, f32[8,128]{1,0:T(8,128)S(1)}, u32[]{:S(2)}, u32[]{:S(2)}) collective-permute-start(f32[8,128]{1,0:T(8,128)S(1)} %add.164), channel_id=1, source_target_pairs={{0,4},{1,5},{2,6},{3,7},{4,0},{5,1},{6,2},{7,3},{8,12},{9,13},{10,... | collective-permute-start | bytes 12296 | tf_op jit(solution)/shard_map/ppermute | solution.py:22
  62.2 1.7 %collective-permute-done.17 = f32[8,128]{1,0:T(8,128)S(1)} collective-permute-done((f32[8,128]{1,0:T(8,128)S(1)}, f32[8,128]{1,0:T(8,128)S(1)}, u32[]{:S(2)}, u32[]{:S(2)}) %collective-permute-start.17) | collective-permute-done | bytes 4128 | tf_op jit(solution)/shard_map/ppermute | solution.py:22
  63.9 1.6 %scale_directions.1 = (bf16[4096,128]{1,0:T(8,128)(2,1)}, bf16[128,4096]{1,0:T(8,128)(2,1)}) custom-call(f32[8,128]{1,0:T(8,128)S(1)} %add.165.squares_ref, f32[4096,128]{1,0:T(8,128)S(1)} %get-tuple-element.40.enc_ref, f32[128,4096]{1,0:T(8,128)S(1)} %get-tuple-element.42.dec_ref), custom_call_target="tpu_custom_call" | custom-call | tf_op jit(solution)/shard_map/scale_directions/pallas_call | solution.py:51
  (47 shorter events, 0.4 us)
Async XLA Ops:
  0.6 17.4 %copy-start = (bf16[1,4096,128]{2,1,0:T(8,128)(2,1)S(1)}, bf16[1,4096,128]{2,1,0:T(8,128)(2,1)}, u32[]{:S(2)}) copy-start(bf16[1,4096,128]{2,1,0:T(8,128)(2,1)} %param.10) | copy-start | bytes 3145732
  0.6 19.0 %copy-start.1 = (bf16[1,128,4096]{2,1,0:T(8,128)(2,1)S(1)}, bf16[1,128,4096]{2,1,0:T(8,128)(2,1)}, u32[]{:S(2)}) copy-start(bf16[1,128,4096]{2,1,0:T(8,128)(2,1)} %param.11) | copy-start | bytes 3145732
  1.9 7.7 %collective-permute-start = (bf16[8,4096]{1,0:T(8,128)(2,1)S(1)}, bf16[8,4096]{1,0:T(8,128)(2,1)S(1)}, u32[]{:S(2)}, u32[]{:S(2)}) collective-permute-start(bf16[8,4096]{1,0:T(8,128)(2,1)S(1)} %get-tuple-element.38), channel_id=1, source_target_pairs={{0,4},{1,5},{2,6},{3,7},{4,0},{5,1},{6,2},{7,3},{8,12},{9,13},{10,... | collective-permute-start | bytes 196616 | tf_op jit(solution)/shard_map/ppermute | solution.py:22
  9.7 8.3 %collective-permute-start.3 = (bf16[16,4096]{1,0:T(8,128)(2,1)S(1)}, bf16[16,4096]{1,0:T(8,128)(2,1)S(1)}, u32[]{:S(2)}, u32[]{:S(2)}) collective-permute-start(bf16[16,4096]{1,0:T(8,128)(2,1)S(1)} %pad_maximum_fusion.1), channel_id=1, source_target_pairs={{0,3},{1,2},{2,1},{3,0},{4,7},{5,6},{6,5},{7,4},{8,11},{9,10},{10,... | collective-permute-start | bytes 393224 | tf_op jit(solution)/shard_map/ppermute | solution.py:22
  11.3 6.7 %collective-permute-start.2 = (bf16[16,4096]{1,0:T(8,128)(2,1)S(1)}, bf16[16,4096]{1,0:T(8,128)(2,1)S(1)}, u32[]{:S(2)}, u32[]{:S(2)}) collective-permute-start(bf16[16,4096]{1,0:T(8,128)(2,1)S(1)} %pad_maximum_fusion.1), channel_id=1, source_target_pairs={{0,2},{1,3},{2,0},{3,1},{4,6},{5,7},{6,4},{7,5},{8,10},{9,11},{10,... | collective-permute-start | bytes 393224 | tf_op jit(solution)/shard_map/ppermute | solution.py:22
  12.9 5.0 %collective-permute-start.1 = (bf16[16,4096]{1,0:T(8,128)(2,1)S(1)}, bf16[16,4096]{1,0:T(8,128)(2,1)S(1)}, u32[]{:S(2)}, u32[]{:S(2)}) collective-permute-start(bf16[16,4096]{1,0:T(8,128)(2,1)S(1)} %pad_maximum_fusion.1), channel_id=1, source_target_pairs={{0,1},{1,0},{2,3},{3,2},{4,5},{5,4},{6,7},{7,6},{8,9},{9,8},{10,11... | collective-permute-start | bytes 393224 | tf_op jit(solution)/shard_map/ppermute | solution.py:22
  18.3 1.3 %collective-permute-start.4 = (f32[64,128]{1,0:T(8,128)S(1)}, f32[64,128]{1,0:T(8,128)S(1)}, u32[]{:S(2)}, u32[]{:S(2)}) collective-permute-start(f32[64,128]{1,0:T(8,128)S(1)} %fusion.16), channel_id=1, source_target_pairs={{0,8},{8,0},{1,9},{9,1},{2,10},{10,2},{3,11},{11,3},{4,12},{12,4},... | collective-permute-start | bytes 98312 | tf_op jit(solution)/shard_map/ppermute | solution.py:22
  18.4 5.6 %copy-start.2 = (bf16[1,4096,128]{2,1,0:T(8,128)(2,1)S(1)}, bf16[1,4096,128]{2,1,0:T(8,128)(2,1)}, u32[]{:S(2)}) copy-start(bf16[1,4096,128]{2,1,0:T(8,128)(2,1)} %param.13) | copy-start | bytes 3145732
  18.4 5.6 %copy-start.3 = (bf16[1,4096,128]{2,1,0:T(8,128)(2,1)S(1)}, bf16[1,4096,128]{2,1,0:T(8,128)(2,1)}, u32[]{:S(2)}) copy-start(bf16[1,4096,128]{2,1,0:T(8,128)(2,1)} %param.12) | copy-start | bytes 3145732
  20.5 8.4 %collective-permute-start.5 = (s16[16,4096]{1,0:T(8,128)(2,1)S(1)}, s16[16,4096]{1,0:T(8,128)(2,1)S(1)}, u32[]{:S(2)}, u32[]{:S(2)}) collective-permute-start(s16[16,4096]{1,0:T(8,128)(2,1)S(1)} %get-tuple-element.32), channel_id=1, source_target_pairs={{0,1},{1,0},{2,3},{3,2},{4,5},{5,4},{6,7},{7,6},{8,9},{9,8},{10,11... | collective-permute-start | bytes 393224 | tf_op jit(solution)/shard_map/ppermute | solution.py:22
  21.4 7.5 %collective-permute-start.7 = (s16[16,4096]{1,0:T(8,128)(2,1)S(1)}, s16[16,4096]{1,0:T(8,128)(2,1)S(1)}, u32[]{:S(2)}, u32[]{:S(2)}) collective-permute-start(s16[16,4096]{1,0:T(8,128)(2,1)S(1)} %get-tuple-element.33), channel_id=1, source_target_pairs={{0,3},{1,2},{2,1},{3,0},{4,7},{5,6},{6,5},{7,4},{8,11},{9,10},{10,... | collective-permute-start | bytes 393224 | tf_op jit(solution)/shard_map/ppermute | solution.py:22
  23.2 1.2 %copy-start.4 = (bf16[1,128,4096]{2,1,0:T(8,128)(2,1)S(1)}, bf16[1,128,4096]{2,1,0:T(8,128)(2,1)}, u32[]{:S(2)}) copy-start(bf16[1,128,4096]{2,1,0:T(8,128)(2,1)} %param.15) | copy-start | bytes 3145732
  23.2 1.5 %copy-start.5 = (bf16[1,128,4096]{2,1,0:T(8,128)(2,1)S(1)}, bf16[1,128,4096]{2,1,0:T(8,128)(2,1)}, u32[]{:S(2)}) copy-start(bf16[1,128,4096]{2,1,0:T(8,128)(2,1)} %param.14) | copy-start | bytes 3145732
  23.2 7.0 %collective-permute-start.6 = (s16[16,4096]{1,0:T(8,128)(2,1)S(1)}, s16[16,4096]{1,0:T(8,128)(2,1)S(1)}, u32[]{:S(2)}, u32[]{:S(2)}) collective-permute-start(s16[16,4096]{1,0:T(8,128)(2,1)S(1)} %get-tuple-element.34), channel_id=1, source_target_pairs={{0,2},{1,3},{2,0},{3,1},{4,6},{5,7},{6,4},{7,5},{8,10},{9,11},{10,... | collective-permute-start | bytes 393224 | tf_op jit(solution)/shard_map/ppermute | solution.py:22
  30.8 8.5 %collective-permute-start.8 = (s16[16,4096]{1,0:T(8,128)(2,1)S(1)}, s16[16,4096]{1,0:T(8,128)(2,1)S(1)}, u32[]{:S(2)}, u32[]{:S(2)}) collective-permute-start(s16[16,4096]{1,0:T(8,128)(2,1)S(1)} %select_convert_fusion), channel_id=1, source_target_pairs={{0,4},{1,5},{2,6},{3,7},{4,0},{5,1},{6,2},{7,3},{8,12},{9,13},{10,... | collective-permute-start | bytes 393224 | tf_op jit(solution)/shard_map/ppermute | solution.py:22
  33.8 9.4 %collective-permute-start.13 = (f32[128]{0:T(128)S(1)}, f32[128]{0:T(128)S(1)}, u32[]{:S(2)}, u32[]{:S(2)}) collective-permute-start(f32[128]{0:T(128)S(1)} %add_sqrt_fusion), channel_id=1, source_target_pairs={{0,8},{8,0},{1,9},{9,1},{2,10},{10,2},{3,11},{11,3},{4,12},{12,4},... | collective-permute-start | bytes 1544 | tf_op jit(solution)/shard_map/ppermute | solution.py:22
  39.6 6.6 %collective-permute-start.11 = (bf16[16,4096]{1,0:T(8,128)(2,1)S(1)}, bf16[16,4096]{1,0:T(8,128)(2,1)S(1)}, u32[]{:S(2)}, u32[]{:S(2)}) collective-permute-start(bf16[16,4096]{1,0:T(8,128)(2,1)S(1)} %fusion.21), channel_id=1, source_target_pairs={{0,3},{1,2},{2,1},{3,0},{4,7},{5,6},{6,5},{7,4},{8,11},{9,10},{10,... | collective-permute-start | bytes 393224 | tf_op jit(solution)/shard_map/ppermute | solution.py:22
  40.7 6.3 %collective-permute-start.10 = (bf16[16,4096]{1,0:T(8,128)(2,1)S(1)}, bf16[16,4096]{1,0:T(8,128)(2,1)S(1)}, u32[]{:S(2)}, u32[]{:S(2)}) collective-permute-start(bf16[16,4096]{1,0:T(8,128)(2,1)S(1)} %fusion.21), channel_id=1, source_target_pairs={{0,2},{1,3},{2,0},{3,1},{4,6},{5,7},{6,4},{7,5},{8,10},{9,11},{10,... | collective-permute-start | bytes 393224 | tf_op jit(solution)/shard_map/ppermute | solution.py:22
  42.3 5.3 %collective-permute-start.9 = (bf16[16,4096]{1,0:T(8,128)(2,1)S(1)}, bf16[16,4096]{1,0:T(8,128)(2,1)S(1)}, u32[]{:S(2)}, u32[]{:S(2)}) collective-permute-start(bf16[16,4096]{1,0:T(8,128)(2,1)S(1)} %fusion.21), channel_id=1, source_target_pairs={{0,1},{1,0},{2,3},{3,2},{4,5},{5,4},{6,7},{7,6},{8,9},{9,8},{10,11... | collective-permute-start | bytes 393224 | tf_op jit(solution)/shard_map/ppermute | solution.py:22
  48.1 1.6 %collective-permute-start.12 = (f32[64,128]{1,0:T(8,128)S(1)}, f32[64,128]{1,0:T(8,128)S(1)}, u32[]{:S(2)}, u32[]{:S(2)}) collective-permute-start(f32[64,128]{1,0:T(8,128)S(1)} %fusion.12), channel_id=1, source_target_pairs={{0,8},{8,0},{1,9},{9,1},{2,10},{10,2},{3,11},{11,3},{4,12},{12,4},... | collective-permute-start | bytes 98312 | tf_op jit(solution)/shard_map/ppermute | solution.py:22
  50.8 1.4 %collective-permute-start.14 = (f32[8,128]{1,0:T(8,128)S(1)}, f32[8,128]{1,0:T(8,128)S(1)}, u32[]{:S(2)}, u32[]{:S(2)}) collective-permute-start(f32[8,128]{1,0:T(8,128)S(1)} %add.161), channel_id=1, source_target_pairs={{0,8},{8,0},{1,9},{9,1},{2,10},{10,2},{3,11},{11,3},{4,12},{12,4},... | collective-permute-start | bytes 12296 | tf_op jit(solution)/shard_map/ppermute | solution.py:22
  52.2 3.6 %collective-permute-start.15 = (f32[8,128]{1,0:T(8,128)S(1)}, f32[8,128]{1,0:T(8,128)S(1)}, u32[]{:S(2)}, u32[]{:S(2)}) collective-permute-start(f32[8,128]{1,0:T(8,128)S(1)} %add.162), channel_id=1, source_target_pairs={{0,1},{1,0},{2,3},{3,2},{4,5},{5,4},{6,7},{7,6},{8,9},{9,8},{10,11... | collective-permute-start | bytes 12296 | tf_op jit(solution)/shard_map/ppermute | solution.py:22
  55.8 3.6 %collective-permute-start.16 = (f32[8,128]{1,0:T(8,128)S(1)}, f32[8,128]{1,0:T(8,128)S(1)}, u32[]{:S(2)}, u32[]{:S(2)}) collective-permute-start(f32[8,128]{1,0:T(8,128)S(1)} %add.163), channel_id=1, source_target_pairs={{0,2},{1,3},{2,0},{3,1},{4,6},{5,7},{6,4},{7,5},{8,10},{9,11},{10,... | collective-permute-start | bytes 12296 | tf_op jit(solution)/shard_map/ppermute | solution.py:22
  59.4 4.5 %collective-permute-start.17 = (f32[8,128]{1,0:T(8,128)S(1)}, f32[8,128]{1,0:T(8,128)S(1)}, u32[]{:S(2)}, u32[]{:S(2)}) collective-permute-start(f32[8,128]{1,0:T(8,128)S(1)} %add.164), channel_id=1, source_target_pairs={{0,4},{1,5},{2,6},{3,7},{4,0},{5,1},{6,2},{7,3},{8,12},{9,13},{10,... | collective-permute-start | bytes 12296 | tf_op jit(solution)/shard_map/ppermute | solution.py:22

commit v5 on v4

--- a/solution.py
+++ b/solution.py
@@ -15,6 +15,8 @@
 norm_eps = 1e-06
 f32 = jnp.float32
 bf16 = jnp.bfloat16
+CHUNK = 512
+ORDER = (1, 3, 2)
 
 
 def swap(value, axis, bits):
@@ -82,8 +84,115 @@
     return packed.astype(f32) * step
 
 
+def row_level(top):
+    return jnp.ceil(16.0 * jnp.log2(jnp.maximum(top, 1e-30)))
+
+
+def store_packed(out_ref, out_rows, source, rows, level):
+    scale = 32766.0 * jnp.exp2(level * -0.0625)
+    width = source.shape[1]
+    for at in range(0, width, CHUNK):
+        part = pl.ds(at, CHUNK)
+        scaled = jnp.round(source[rows, part] * scale)
+        scaled = jnp.clip(scaled, -32766.0, 32766.0).astype(jnp.int32)
+        if at == 0:
+            column = lax.broadcasted_iota(jnp.int32, scaled.shape, 1)
+            bit = ((level.astype(jnp.int32) + 4096) >> jnp.minimum(column, 15)) & 1
+            scaled = jnp.where(column < 16, (scaled & -2) | bit, scaled)
+        out_ref[out_rows, part] = scaled.astype(jnp.int16)
+
+
+def lane_top(value):
+    top = jnp.abs(value[:, :128])
+    for at in range(128, value.shape[1], 128):
+        top = jnp.maximum(top, jnp.abs(value[:, at : at + 128]))
+    return top
+
+
+def decode_kernel(own_ref, other_ref, dec_ref, codes_ref, first_ref, p1_ref, p2_ref, p3_ref, parts):
+    codes = jnp.maximum(own_ref[...] + other_ref[...], 0.0).astype(bf16)
+    codes_ref[...] = codes
+    quarter = first_ref.shape[0]
+    top = None
+    for at in range(0, dec_ref.shape[1], CHUNK):
+        part = pl.ds(at, CHUNK)
+        value = jnp.dot(codes, dec_ref[:, part], preferred_element_type=f32)
+        first_ref[:, part] = value[:quarter]
+        parts[:, part] = value[quarter:]
+        here = lane_top(value[quarter:])
+        top = here if top is None else jnp.maximum(top, here)
+    level = row_level(jnp.max(top, axis=1, keepdims=True))
+    for k, out_ref in enumerate((p1_ref, p2_ref, p3_ref)):
+        rows = pl.ds(k * quarter, quarter)
+        store_packed(out_ref, pl.ds(0, quarter), parts, rows, level[k * quarter : (k + 1) * quarter])
+
+
+def decode(own, other, dec):
+    batch, latents = own.shape
+    features = dec.shape[1]
+    quarter = batch // 4
+    packed = jax.ShapeDtypeStruct((quarter, features), jnp.int16)
+    return pl.pallas_call(
+        decode_kernel,
+        out_shape=(
+            jax.ShapeDtypeStruct((batch, latents), bf16),
+            jax.ShapeDtypeStruct((quarter, features), f32),
+            packed,
+            packed,
+            packed,
+        ),
+        in_specs=[pl.BlockSpec(memory_space=pltpu.VMEM)] * 3,
+        out_specs=[pl.BlockSpec(memory_space=pltpu.VMEM)] * 5,
+        scratch_shapes=[pltpu.VMEM((3 * quarter, features), f32)],
+        compiler_params=pltpu.CompilerParams(vmem_limit_bytes=32 << 20),
+        cost_estimate=pl.CostEstimate(
+            flops=2 * batch * latents * features, bytes_accessed=2 * latents * features, transcendentals=0
+        ),
+        name="decode_and_pack",
+    )(own, other, dec)
+
+
+def read_step(packed_ref):
+    head = packed_ref[:, :128].astype(jnp.int32) & 1
+    column = lax.broadcasted_iota(jnp.int32, head.shape, 1)
+    weight = jnp.where(column < 16, jnp.int32(1) << jnp.minimum(column, 15), 0)
+    code = jnp.sum((head * weight).astype(f32), axis=1, keepdims=True)
+    return jnp.exp2((code - 4096.0) * 0.0625) * (1.0 / 32766.0)
+
+
+def quad_sum_kernel(first_ref, p1_ref, p2_ref, p3_ref, total_ref, packed_ref):
+    refs = (p1_ref, p2_ref, p3_ref)
+    steps = [read_step(ref) for ref in refs]
+    top = None
+    for at in range(0, first_ref.shape[1], CHUNK):
+        part = pl.ds(at, CHUNK)
+        value = first_ref[:, part]
+        for ref, step in zip(refs, steps):
+            value = value + ref[:, part].astype(f32) * step
+        total_ref[:, part] = value
+        here = lane_top(value)
+        top = here if top is None else jnp.maximum(top, here)
+    level = row_level(jnp.max(top, axis=1, keepdims=True))
+    rows = pl.ds(0, first_ref.shape[0])
+    store_packed(packed_ref, rows, total_ref, rows, level)
+
+
+def quad_sum(first, received):
+    return pl.pallas_call(
+        quad_sum_kernel,
+        out_shape=(
+            jax.ShapeDtypeStruct(first.shape, f32),
+            jax.ShapeDtypeStruct(first.shape, jnp.int16),
+        ),
+        in_specs=[pl.BlockSpec(memory_space=pltpu.VMEM)] * 4,
+        out_specs=[pl.BlockSpec(memory_space=pltpu.VMEM)] * 2,
+        compiler_params=pltpu.CompilerParams(vmem_limit_bytes=32 << 20),
+        name="quad_sum",
+    )(first, *received)
+
+
 def quad_gather(quarter):
-    return [quarter] + [swap(quarter, "lat", k) for k in (1, 2, 3)]
+    return [quarter] + [swap(quarter, "lat", k) for k in ORDER]
 
 
 def body(store, row_index, w_enc, decoder_matrix, m_enc, v_enc, m_dec, v_dec):
@@ -111,28 +220,26 @@
     partial_value = jnp.dot(batch_rows, w_enc, preferred_element_type=f32)
     dec_wide = decoder_matrix.astype(f32)
     dec_norm = jnp.sqrt(jnp.sum(dec_wide * dec_wide, axis=1) + norm_eps)
-    preact = partial_value + swap(partial_value, "src", 1)
-    norm_total = dec_norm + swap(dec_norm, "src", 1)
-    feature_codes = jnp.maximum(preact, 0.0).astype(bf16)
+    other_partial = swap(partial_value, "src", 1)
+    preact = partial_value + other_partial
+    feature_codes, first, *parts = decode(partial_value, other_partial, decoder_matrix)
     feature_codes, m_enc, v_enc, m_dec, v_dec = lax.optimization_barrier(
         (feature_codes, m_enc, v_enc, m_dec, v_dec)
     )
-    parts = jnp.dot(feature_codes, decoder_matrix, preferred_element_type=f32)
-    parts = parts.reshape(4, quarter_count, features)
-    total = parts[0]
-    for k in (1, 2, 3):
-        total = total + unpack(swap(pack(parts[k]), "lat", k))
-    total, m_enc, v_enc, m_dec, v_dec = lax.optimization_barrier(
+    norm_total = dec_norm + swap(dec_norm, "src", 1)
+    received = [swap(part, "lat", k) for part, k in zip(parts, ORDER)]
+    received[0], m_enc, v_enc, m_dec, v_dec = lax.optimization_barrier(
         (
-            total,
+            received[0],
             beta_one * m_enc.astype(f32),
             beta_two * v_enc.astype(f32),
             beta_one * m_dec.astype(f32),
             beta_two * v_dec.astype(f32),
         )
     )
+    total, packed = quad_sum(first, received)
     for at, bit in enumerate(high_bits):
-        other = unpack(swap(pack(total), "lat", bit))
+        other = unpack(swap(packed if at == 0 else pack(total), "lat", bit))
         span = own_count << at
         other = jnp.flip(other.reshape(-1, 2, span, features), 1).reshape(quarter_count, features)
         total = total + other

time: 65.7 us -> 65.4 us (level)
  matrix products: 5 us -> 3 us
  starting transfers between devices: 23.6 us -> 24.6 us
  waiting for transfers between devices: 30.2 us -> 29.3 us
  Pallas kernels: 1.56 us -> 2.33 us
  other arithmetic: 3.74 us -> 4.47 us
    reduce_sum x0 -> x2, other arithmetic: none -> 1.79 us  [the longest x1 0.9 us: body(): jnp.sum((dec_dir * dec_dir).reshape(latents // 8, 8, -1, 128), axis=(0, 2))]
    dot_general x1, matrix products: 1.49 us -> 0.46 us  [body(): lax.dot_general(feature_codes, error_rows, (((0,), (0,)), ((), ())), pref...]
    ppermute x18, starting transfers between devices: 23.6 us -> 24.6 us  [swap(): return lax.ppermute(value, axis, [(i, i ^ bits) for i in range(count)])]
    ppermute x18, waiting for transfers between devices: 30.2 us -> 29.3 us  [swap(): return lax.ppermute(value, axis, [(i, i ^ bits) for i in range(count)])]
    pallas_call x0 -> x2, Pallas kernels: none -> 0.78 us  [the longest x1 0.49 us: decode(): pl.pallas_call(decode_kernel, out_shape=(jax.ShapeDtypeStruct((batch, lat...]
  transfers between devices with their start and end apart: 18 -> 18, of which waited for: 13 -> 16; matrix products, arithmetic and copies ran while one was open for 6% -> 7% of each run, Pallas kernels for 0% -> 1%
where the time goes in v5:
time: 65.4 us; the launch traced here: 65.2 us
  waiting for transfers between devices  29.3 us (45%)
  starting transfers between devices  24.6 us (38%)
  other arithmetic  4.47 us (7%)
  matrix products  3 us (5%)
  Pallas kernels  2.33 us (4%)
  between operations  0.84 us (1%)
    ppermute x18, waiting for transfers between devices, swap(): return lax.ppermute(value, axis, [(i, i ^ bits) for i in range(count)])  29.3 us
    ppermute x18, starting transfers between devices, swap(): return lax.ppermute(value, axis, [(i, i ^ bits) for i in range(count)])  24.6 us
    pallas_call x1, Pallas kernels, scale(): pl.pallas_call(functools.partial(scale_kernel, count), out_shape=(jax.Sha...  1.56 us
    reduce_sum x1, other arithmetic, body(): dec_norm = jnp.sqrt(jnp.sum(dec_wide * dec_wide, axis=1) + norm_eps)  1.52 us
  transfers between devices with their start and end apart: 18, of which 16 were waited for; matrix products, arithmetic and copies ran while one was open for 7% of the time, Pallas kernels for 1%

profile of v5, /device:TPU:0, one launch (start us, length us, event | category | flops | bytes accessed | tf_op | source)
XLA Modules:
  0.0 65.2 jit_solution(12146072224672318265)
XLA Ops:
  0.7 1.3 %constant_dynamic-update-slice_fusion.4 = (bf16[64,4096]{1,0:T(8,128)(2,1)S(1)}, bf16[8,4096]{1,0:T(8,128)(2,1)S(1)}) fusion(bf16[16,1,4096]{2,0,1:T(8,128)(2,1)} %param.8, s32[8]{0:T(128)} %param.9), kind=kOutput, calls=%fused_computation.47 | convolution fusion | flops 1081471 | bytes 262176 | tf_op jit(solution)/shard_map/dot_general | solution.py:214
  1.9 4.1 %collective-permute-start = (bf16[8,4096]{1,0:T(8,128)(2,1)S(1)}, bf16[8,4096]{1,0:T(8,128)(2,1)S(1)}, u32[]{:S(2)}, u32[]{:S(2)}) collective-permute-start(bf16[8,4096]{1,0:T(8,128)(2,1)S(1)} %get-tuple-element.47), channel_id=1, source_target_pairs={{0,4},{1,5},{2,6},{3,7},{4,0},{5,1},{6,2},{7,3},{8,12},{9,13},{10,... | collective-permute-start | bytes 196616 | tf_op jit(solution)/shard_map/ppermute | solution.py:24
  6.0 1.5 %fusion.1 = f32[128]{0:T(128)S(1)} fusion(bf16[1,128,4096]{2,1,0:T(8,128)(2,1)} %param.11), kind=kLoop, calls=%fused_computation.9 | loop fusion | flops 1572736 | bytes 1049088 | tf_op jit(solution)/shard_map/reduce_sum | solution.py:222
  7.7 2.0 %collective-permute-done = bf16[8,4096]{1,0:T(8,128)(2,1)S(1)} collective-permute-done((bf16[8,4096]{1,0:T(8,128)(2,1)S(1)}, bf16[8,4096]{1,0:T(8,128)(2,1)S(1)}, u32[]{:S(2)}, u32[]{:S(2)}) %collective-permute-start) | collective-permute-done | bytes 65568 | tf_op jit(solution)/shard_map/ppermute | solution.py:24
  9.7 1.8 %collective-permute-start.1 = (bf16[16,4096]{1,0:T(8,128)(2,1)S(1)}, bf16[16,4096]{1,0:T(8,128)(2,1)S(1)}, u32[]{:S(2)}, u32[]{:S(2)}) collective-permute-start(bf16[16,4096]{1,0:T(8,128)(2,1)S(1)} %pad_maximum_fusion.1), channel_id=1, source_target_pairs={{0,1},{1,0},{2,3},{3,2},{4,5},{5,4},{6,7},{7,6},{8,9},{9,8},{10,11... | collective-permute-start | bytes 393224 | tf_op jit(solution)/shard_map/ppermute | solution.py:24
  11.5 0.3 collective-permute-start.2
  11.8 1.5 %collective-permute-start.3 = (bf16[16,4096]{1,0:T(8,128)(2,1)S(1)}, bf16[16,4096]{1,0:T(8,128)(2,1)S(1)}, u32[]{:S(2)}, u32[]{:S(2)}) collective-permute-start(bf16[16,4096]{1,0:T(8,128)(2,1)S(1)} %pad_maximum_fusion.1), channel_id=1, source_target_pairs={{0,2},{1,3},{2,0},{3,1},{4,6},{5,7},{6,4},{7,5},{8,10},{9,11},{10,... | collective-permute-start | bytes 393224 | tf_op jit(solution)/shard_map/ppermute | solution.py:24
  13.3 2.5 %collective-permute-done.1 = bf16[16,4096]{1,0:T(8,128)(2,1)S(1)} collective-permute-done((bf16[16,4096]{1,0:T(8,128)(2,1)S(1)}, bf16[16,4096]{1,0:T(8,128)(2,1)S(1)}, u32[]{:S(2)}, u32[]{:S(2)}) %collective-permute-start.1) | collective-permute-done | bytes 131104 | tf_op jit(solution)/shard_map/ppermute | solution.py:24
  15.8 1.6 %collective-permute-done.2 = bf16[16,4096]{1,0:T(8,128)(2,1)S(1)} collective-permute-done((bf16[16,4096]{1,0:T(8,128)(2,1)S(1)}, bf16[16,4096]{1,0:T(8,128)(2,1)S(1)}, u32[]{:S(2)}, u32[]{:S(2)}) %collective-permute-start.2) | collective-permute-done | bytes 131104 | tf_op jit(solution)/shard_map/ppermute | solution.py:24
  17.4 0.4 collective-permute-done.3
  17.7 0.3 fusion.12.own_ref
  18.2 1.2 %collective-permute-done.4.other_ref = f32[64,128]{1,0:T(8,128)S(1)} collective-permute-done((f32[64,128]{1,0:T(8,128)S(1)}, f32[64,128]{1,0:T(8,128)S(1)}, u32[]{:S(2)}, u32[]{:S(2)}) %collective-permute-start.4) | collective-permute-done | bytes 32800 | tf_op jit(solution)/shard_map/ppermute | solution.py:24
  19.3 0.5 decode_and_pack.1
  19.8 1.7 %collective-permute-start.5 = (s16[16,4096]{1,0:T(8,128)(2,1)S(1)}, s16[16,4096]{1,0:T(8,128)(2,1)S(1)}, u32[]{:S(2)}, u32[]{:S(2)}) collective-permute-start(s16[16,4096]{1,0:T(8,128)(2,1)S(1)} %get-tuple-element.21), channel_id=1, source_target_pairs={{0,1},{1,0},{2,3},{3,2},{4,5},{5,4},{6,7},{7,6},{8,9},{9,8},{10,11... | collective-permute-start | bytes 393224 | tf_op jit(solution)/shard_map/ppermute | solution.py:24
  21.5 1.4 %collective-permute-start.6 = (s16[16,4096]{1,0:T(8,128)(2,1)S(1)}, s16[16,4096]{1,0:T(8,128)(2,1)S(1)}, u32[]{:S(2)}, u32[]{:S(2)}) collective-permute-start(s16[16,4096]{1,0:T(8,128)(2,1)S(1)} %get-tuple-element.30), channel_id=1, source_target_pairs={{0,3},{1,2},{2,1},{3,0},{4,7},{5,6},{6,5},{7,4},{8,11},{9,10},{10,... | collective-permute-start | bytes 393224 | tf_op jit(solution)/shard_map/ppermute | solution.py:24
  22.9 0.5 collective-permute-start.7
  23.4 0.5 convert_multiply_fusion.2
  23.9 0.2 copy-done.4
  24.2 0.3 copy-done.5
  24.5 0.3 convert_multiply_fusion.4
  24.8 3.0 %collective-permute-done.5.p1_ref = s16[16,4096]{1,0:T(8,128)(2,1)S(1)} collective-permute-done((s16[16,4096]{1,0:T(8,128)(2,1)S(1)}, s16[16,4096]{1,0:T(8,128)(2,1)S(1)}, u32[]{:S(2)}, u32[]{:S(2)}) %collective-permute-start.5) | collective-permute-done | bytes 131104 | tf_op jit(solution)/shard_map/ppermute | solution.py:24
  27.8 1.0 %collective-permute-done.6.p2_ref = s16[16,4096]{1,0:T(8,128)(2,1)S(1)} collective-permute-done((s16[16,4096]{1,0:T(8,128)(2,1)S(1)}, s16[16,4096]{1,0:T(8,128)(2,1)S(1)}, u32[]{:S(2)}, u32[]{:S(2)}) %collective-permute-start.6) | collective-permute-done | bytes 131104 | tf_op jit(solution)/shard_map/ppermute | solution.py:24
  28.8 0.7 %collective-permute-done.7.p3_ref = s16[16,4096]{1,0:T(8,128)(2,1)S(1)} collective-permute-done((s16[16,4096]{1,0:T(8,128)(2,1)S(1)}, s16[16,4096]{1,0:T(8,128)(2,1)S(1)}, u32[]{:S(2)}, u32[]{:S(2)}) %collective-permute-start.7) | collective-permute-done | bytes 131104 | tf_op jit(solution)/shard_map/ppermute | solution.py:24
  29.5 0.3 quad_sum.1
  29.8 3.5 %collective-permute-start.8 = (s16[16,4096]{1,0:T(8,128)(2,1)S(1)}, s16[16,4096]{1,0:T(8,128)(2,1)S(1)}, u32[]{:S(2)}, u32[]{:S(2)}) collective-permute-start(s16[16,4096]{1,0:T(8,128)(2,1)S(1)} %get-tuple-element.33), channel_id=1, source_target_pairs={{0,4},{1,5},{2,6},{3,7},{4,0},{5,1},{6,2},{7,3},{8,12},{9,13},{10,... | collective-permute-start | bytes 393224 | tf_op jit(solution)/shard_map/ppermute | solution.py:24
  33.3 5.5 %collective-permute-done.8 = s16[16,4096]{1,0:T(8,128)(2,1)S(1)} collective-permute-done((s16[16,4096]{1,0:T(8,128)(2,1)S(1)}, s16[16,4096]{1,0:T(8,128)(2,1)S(1)}, u32[]{:S(2)}, u32[]{:S(2)}) %collective-permute-start.8) | collective-permute-done | bytes 131104 | tf_op jit(solution)/shard_map/ppermute | solution.py:24
  38.8 0.1 select_reduce_fusion
  38.9 0.1 multiply_bitcast_fusion
  39.1 1.3 %collective-permute-start.10 = (bf16[16,4096]{1,0:T(8,128)(2,1)S(1)}, bf16[16,4096]{1,0:T(8,128)(2,1)S(1)}, u32[]{:S(2)}, u32[]{:S(2)}) collective-permute-start(bf16[16,4096]{1,0:T(8,128)(2,1)S(1)} %fusion.15), channel_id=1, source_target_pairs={{0,3},{1,2},{2,1},{3,0},{4,7},{5,6},{6,5},{7,4},{8,11},{9,10},{10,... | collective-permute-start | bytes 393224 | tf_op jit(solution)/shard_map/ppermute | solution.py:24
  40.4 1.4 %collective-permute-start.11 = (bf16[16,4096]{1,0:T(8,128)(2,1)S(1)}, bf16[16,4096]{1,0:T(8,128)(2,1)S(1)}, u32[]{:S(2)}, u32[]{:S(2)}) collective-permute-start(bf16[16,4096]{1,0:T(8,128)(2,1)S(1)} %fusion.15), channel_id=1, source_target_pairs={{0,2},{1,3},{2,0},{3,1},{4,6},{5,7},{6,4},{7,5},{8,10},{9,11},{10,... | collective-permute-start | bytes 393224 | tf_op jit(solution)/shard_map/ppermute | solution.py:24
  41.9 0.8 %collective-permute-start.9 = (bf16[16,4096]{1,0:T(8,128)(2,1)S(1)}, bf16[16,4096]{1,0:T(8,128)(2,1)S(1)}, u32[]{:S(2)}, u32[]{:S(2)}) collective-permute-start(bf16[16,4096]{1,0:T(8,128)(2,1)S(1)} %fusion.15), channel_id=1, source_target_pairs={{0,1},{1,0},{2,3},{3,2},{4,5},{5,4},{6,7},{7,6},{8,9},{9,8},{10,11... | collective-permute-start | bytes 393224 | tf_op jit(solution)/shard_map/ppermute | solution.py:24
  42.6 3.0 %collective-permute-done.10 = bf16[16,4096]{1,0:T(8,128)(2,1)S(1)} collective-permute-done((bf16[16,4096]{1,0:T(8,128)(2,1)S(1)}, bf16[16,4096]{1,0:T(8,128)(2,1)S(1)}, u32[]{:S(2)}, u32[]{:S(2)}) %collective-permute-start.10) | collective-permute-done | bytes 131104 | tf_op jit(solution)/shard_map/ppermute | solution.py:24
  45.7 1.1 %collective-permute-done.11 = bf16[16,4096]{1,0:T(8,128)(2,1)S(1)} collective-permute-done((bf16[16,4096]{1,0:T(8,128)(2,1)S(1)}, bf16[16,4096]{1,0:T(8,128)(2,1)S(1)}, u32[]{:S(2)}, u32[]{:S(2)}) %collective-permute-start.11) | collective-permute-done | bytes 131104 | tf_op jit(solution)/shard_map/ppermute | solution.py:24
  46.8 0.3 collective-permute-done.9
  47.1 0.5 fusion.17
  47.6 0.5 fusion
  48.1 0.9 %bitcast_reduce_fusion = (f32[8,128]{1,0:T(8,128)S(1)}, f32[128,4096]{1,0:T(8,128)S(1)}) fusion(f32[128,4096]{1,0:T(8,128)S(1)} %get-tuple-element.37, f32[128,4096]{1,0:T(8,128)S(1)} %fusion, f32[128,4096]{1,0:T(8,128)S(1)} %get-tuple-element.35), kind=kLoop, calls=%fused_computation.20 | loop fusion | flops 5766144 | bytes 8392704 | tf_op jit(solution)/shard_map/reduce_sum | solution.py:267
  49.0 0.5 fusion.18
  49.5 0.9 %bitcast_reduce_fusion.1 = (f32[8,128]{1,0:T(8,128)S(1)}, f32[4096,128]{1,0:T(8,128)S(1)}) fusion(f32[4096,128]{1,0:T(8,128)S(1)} %get-tuple-element.34, f32[4096,128]{1,0:T(8,128)S(1)} %fusion.18, f32[4096,128]{1,0:T(8,128)S(1)} %get-tuple-element.27), kind=kLoop, calls=%fused_computation.21 | loop fusion | flops 5766144 | bytes 8392704 | tf_op jit(solution)/shard_map/reduce_sum | solution.py:266
  50.4 0.6 collective-permute-start.14
  51.0 0.8 %collective-permute-done.14 = f32[8,128]{1,0:T(8,128)S(1)} collective-permute-done((f32[8,128]{1,0:T(8,128)S(1)}, f32[8,128]{1,0:T(8,128)S(1)}, u32[]{:S(2)}, u32[]{:S(2)}) %collective-permute-start.14) | collective-permute-done | bytes 4128 | tf_op jit(solution)/shard_map/ppermute | solution.py:24
  51.8 1.2 %collective-permute-start.15 = (f32[8,128]{1,0:T(8,128)S(1)}, f32[8,128]{1,0:T(8,128)S(1)}, u32[]{:S(2)}, u32[]{:S(2)}) collective-permute-start(f32[8,128]{1,0:T(8,128)S(1)} %add.96), channel_id=1, source_target_pairs={{0,1},{1,0},{2,3},{3,2},{4,5},{5,4},{6,7},{7,6},{8,9},{9,8},{10,11... | collective-permute-start | bytes 12296 | tf_op jit(solution)/shard_map/ppermute | solution.py:24
  53.0 2.5 %collective-permute-done.15 = f32[8,128]{1,0:T(8,128)S(1)} collective-permute-done((f32[8,128]{1,0:T(8,128)S(1)}, f32[8,128]{1,0:T(8,128)S(1)}, u32[]{:S(2)}, u32[]{:S(2)}) %collective-permute-start.15) | collective-permute-done | bytes 4128 | tf_op jit(solution)/shard_map/ppermute | solution.py:24
  55.4 1.4 %collective-permute-start.16 = (f32[8,128]{1,0:T(8,128)S(1)}, f32[8,128]{1,0:T(8,128)S(1)}, u32[]{:S(2)}, u32[]{:S(2)}) collective-permute-start(f32[8,128]{1,0:T(8,128)S(1)} %add.97), channel_id=1, source_target_pairs={{0,2},{1,3},{2,0},{3,1},{4,6},{5,7},{6,4},{7,5},{8,10},{9,11},{10,... | collective-permute-start | bytes 12296 | tf_op jit(solution)/shard_map/ppermute | solution.py:24
  56.9 2.2 %collective-permute-done.16 = f32[8,128]{1,0:T(8,128)S(1)} collective-permute-done((f32[8,128]{1,0:T(8,128)S(1)}, f32[8,128]{1,0:T(8,128)S(1)}, u32[]{:S(2)}, u32[]{:S(2)}) %collective-permute-start.16) | collective-permute-done | bytes 4128 | tf_op jit(solution)/shard_map/ppermute | solution.py:24
  59.0 3.0 %collective-permute-start.17 = (f32[8,128]{1,0:T(8,128)S(1)}, f32[8,128]{1,0:T(8,128)S(1)}, u32[]{:S(2)}, u32[]{:S(2)}) collective-permute-start(f32[8,128]{1,0:T(8,128)S(1)} %add.98), channel_id=1, source_target_pairs={{0,4},{1,5},{2,6},{3,7},{4,0},{5,1},{6,2},{7,3},{8,12},{9,13},{10,... | collective-permute-start | bytes 12296 | tf_op jit(solution)/shard_map/ppermute | solution.py:24
  62.0 1.6 %collective-permute-done.17 = f32[8,128]{1,0:T(8,128)S(1)} collective-permute-done((f32[8,128]{1,0:T(8,128)S(1)}, f32[8,128]{1,0:T(8,128)S(1)}, u32[]{:S(2)}, u32[]{:S(2)}) %collective-permute-start.17) | collective-permute-done | bytes 4128 | tf_op jit(solution)/shard_map/ppermute | solution.py:24
  63.6 1.6 %scale_directions.1 = (bf16[4096,128]{1,0:T(8,128)(2,1)}, bf16[128,4096]{1,0:T(8,128)(2,1)}) custom-call(f32[8,128]{1,0:T(8,128)S(1)} %add.99.squares_ref, f32[4096,128]{1,0:T(8,128)S(1)} %get-tuple-element.43.enc_ref, f32[128,4096]{1,0:T(8,128)S(1)} %get-tuple-element.41.dec_ref), custom_call_target="tpu_custom_call" | custom-call | tf_op jit(solution)/shard_map/scale_directions/pallas_call | solution.py:53
  (32 shorter events, 0.4 us)
Async XLA Ops:
  0.6 17.1 %copy-start = (bf16[1,4096,128]{2,1,0:T(8,128)(2,1)S(1)}, bf16[1,4096,128]{2,1,0:T(8,128)(2,1)}, u32[]{:S(2)}) copy-start(bf16[1,4096,128]{2,1,0:T(8,128)(2,1)} %param.10) | copy-start | bytes 3145732
  0.6 18.7 %copy-start.1 = (bf16[1,128,4096]{2,1,0:T(8,128)(2,1)S(1)}, bf16[1,128,4096]{2,1,0:T(8,128)(2,1)}, u32[]{:S(2)}) copy-start(bf16[1,128,4096]{2,1,0:T(8,128)(2,1)} %param.11) | copy-start | bytes 3145732
  1.9 7.7 %collective-permute-start = (bf16[8,4096]{1,0:T(8,128)(2,1)S(1)}, bf16[8,4096]{1,0:T(8,128)(2,1)S(1)}, u32[]{:S(2)}, u32[]{:S(2)}) collective-permute-start(bf16[8,4096]{1,0:T(8,128)(2,1)S(1)} %get-tuple-element.47), channel_id=1, source_target_pairs={{0,4},{1,5},{2,6},{3,7},{4,0},{5,1},{6,2},{7,3},{8,12},{9,13},{10,... | collective-permute-start | bytes 196616 | tf_op jit(solution)/shard_map/ppermute | solution.py:24
  7.5 15.9 %copy-start.2 = (bf16[1,128,4096]{2,1,0:T(8,128)(2,1)S(1)}, bf16[1,128,4096]{2,1,0:T(8,128)(2,1)}, u32[]{:S(2)}) copy-start(bf16[1,128,4096]{2,1,0:T(8,128)(2,1)} %param.15) | copy-start | bytes 3145732
  7.6 15.8 %copy-start.3 = (bf16[1,128,4096]{2,1,0:T(8,128)(2,1)S(1)}, bf16[1,128,4096]{2,1,0:T(8,128)(2,1)}, u32[]{:S(2)}) copy-start(bf16[1,128,4096]{2,1,0:T(8,128)(2,1)} %param.14) | copy-start | bytes 3145732
  7.6 35.1 %collective-permute-start.13 = (f32[128]{0:T(128)S(1)}, f32[128]{0:T(128)S(1)}, u32[]{:S(2)}, u32[]{:S(2)}) collective-permute-start(f32[128]{0:T(128)S(1)} %add_sqrt_fusion), channel_id=1, source_target_pairs={{0,8},{8,0},{1,9},{9,1},{2,10},{10,2},{3,11},{11,3},{4,12},{12,4},... | collective-permute-start | bytes 1544 | tf_op jit(solution)/shard_map/ppermute | solution.py:24
  9.7 6.1 %collective-permute-start.1 = (bf16[16,4096]{1,0:T(8,128)(2,1)S(1)}, bf16[16,4096]{1,0:T(8,128)(2,1)S(1)}, u32[]{:S(2)}, u32[]{:S(2)}) collective-permute-start(bf16[16,4096]{1,0:T(8,128)(2,1)S(1)} %pad_maximum_fusion.1), channel_id=1, source_target_pairs={{0,1},{1,0},{2,3},{3,2},{4,5},{5,4},{6,7},{7,6},{8,9},{9,8},{10,11... | collective-permute-start | bytes 393224 | tf_op jit(solution)/shard_map/ppermute | solution.py:24
  11.5 5.9 %collective-permute-start.2 = (bf16[16,4096]{1,0:T(8,128)(2,1)S(1)}, bf16[16,4096]{1,0:T(8,128)(2,1)S(1)}, u32[]{:S(2)}, u32[]{:S(2)}) collective-permute-start(bf16[16,4096]{1,0:T(8,128)(2,1)S(1)} %pad_maximum_fusion.1), channel_id=1, source_target_pairs={{0,3},{1,2},{2,1},{3,0},{4,7},{5,6},{6,5},{7,4},{8,11},{9,10},{10,... | collective-permute-start | bytes 393224 | tf_op jit(solution)/shard_map/ppermute | solution.py:24
  11.8 5.9 %collective-permute-start.3 = (bf16[16,4096]{1,0:T(8,128)(2,1)S(1)}, bf16[16,4096]{1,0:T(8,128)(2,1)S(1)}, u32[]{:S(2)}, u32[]{:S(2)}) collective-permute-start(bf16[16,4096]{1,0:T(8,128)(2,1)S(1)} %pad_maximum_fusion.1), channel_id=1, source_target_pairs={{0,2},{1,3},{2,0},{3,1},{4,6},{5,7},{6,4},{7,5},{8,10},{9,11},{10,... | collective-permute-start | bytes 393224 | tf_op jit(solution)/shard_map/ppermute | solution.py:24
  18.1 1.3 %collective-permute-start.4 = (f32[64,128]{1,0:T(8,128)S(1)}, f32[64,128]{1,0:T(8,128)S(1)}, u32[]{:S(2)}, u32[]{:S(2)}) collective-permute-start(f32[64,128]{1,0:T(8,128)S(1)} %fusion.12.own_ref), channel_id=1, source_target_pairs={{0,8},{8,0},{1,9},{9,1},{2,10},{10,2},{3,11},{11,3},{4,12},{12,4},... | collective-permute-start | bytes 98312 | tf_op jit(solution)/shard_map/ppermute | solution.py:24
  19.8 7.9 %collective-permute-start.5 = (s16[16,4096]{1,0:T(8,128)(2,1)S(1)}, s16[16,4096]{1,0:T(8,128)(2,1)S(1)}, u32[]{:S(2)}, u32[]{:S(2)}) collective-permute-start(s16[16,4096]{1,0:T(8,128)(2,1)S(1)} %get-tuple-element.21), channel_id=1, source_target_pairs={{0,1},{1,0},{2,3},{3,2},{4,5},{5,4},{6,7},{7,6},{8,9},{9,8},{10,11... | collective-permute-start | bytes 393224 | tf_op jit(solution)/shard_map/ppermute | solution.py:24
  21.5 7.3 %collective-permute-start.6 = (s16[16,4096]{1,0:T(8,128)(2,1)S(1)}, s16[16,4096]{1,0:T(8,128)(2,1)S(1)}, u32[]{:S(2)}, u32[]{:S(2)}) collective-permute-start(s16[16,4096]{1,0:T(8,128)(2,1)S(1)} %get-tuple-element.30), channel_id=1, source_target_pairs={{0,3},{1,2},{2,1},{3,0},{4,7},{5,6},{6,5},{7,4},{8,11},{9,10},{10,... | collective-permute-start | bytes 393224 | tf_op jit(solution)/shard_map/ppermute | solution.py:24
  22.9 1.2 %copy-start.4 = (bf16[1,4096,128]{2,1,0:T(8,128)(2,1)S(1)}, bf16[1,4096,128]{2,1,0:T(8,128)(2,1)}, u32[]{:S(2)}) copy-start(bf16[1,4096,128]{2,1,0:T(8,128)(2,1)} %param.13) | copy-start | bytes 3145732
  22.9 1.5 %copy-start.5 = (bf16[1,4096,128]{2,1,0:T(8,128)(2,1)S(1)}, bf16[1,4096,128]{2,1,0:T(8,128)(2,1)}, u32[]{:S(2)}) copy-start(bf16[1,4096,128]{2,1,0:T(8,128)(2,1)} %param.12) | copy-start | bytes 3145732
  22.9 6.6 %collective-permute-start.7 = (s16[16,4096]{1,0:T(8,128)(2,1)S(1)}, s16[16,4096]{1,0:T(8,128)(2,1)S(1)}, u32[]{:S(2)}, u32[]{:S(2)}) collective-permute-start(s16[16,4096]{1,0:T(8,128)(2,1)S(1)} %get-tuple-element.31), channel_id=1, source_target_pairs={{0,2},{1,3},{2,0},{3,1},{4,6},{5,7},{6,4},{7,5},{8,10},{9,11},{10,... | collective-permute-start | bytes 393224 | tf_op jit(solution)/shard_map/ppermute | solution.py:24
  29.8 9.0 %collective-permute-start.8 = (s16[16,4096]{1,0:T(8,128)(2,1)S(1)}, s16[16,4096]{1,0:T(8,128)(2,1)S(1)}, u32[]{:S(2)}, u32[]{:S(2)}) collective-permute-start(s16[16,4096]{1,0:T(8,128)(2,1)S(1)} %get-tuple-element.33), channel_id=1, source_target_pairs={{0,4},{1,5},{2,6},{3,7},{4,0},{5,1},{6,2},{7,3},{8,12},{9,13},{10,... | collective-permute-start | bytes 393224 | tf_op jit(solution)/shard_map/ppermute | solution.py:24
  39.1 6.6 %collective-permute-start.10 = (bf16[16,4096]{1,0:T(8,128)(2,1)S(1)}, bf16[16,4096]{1,0:T(8,128)(2,1)S(1)}, u32[]{:S(2)}, u32[]{:S(2)}) collective-permute-start(bf16[16,4096]{1,0:T(8,128)(2,1)S(1)} %fusion.15), channel_id=1, source_target_pairs={{0,3},{1,2},{2,1},{3,0},{4,7},{5,6},{6,5},{7,4},{8,11},{9,10},{10,... | collective-permute-start | bytes 393224 | tf_op jit(solution)/shard_map/ppermute | solution.py:24
  40.4 6.3 %collective-permute-start.11 = (bf16[16,4096]{1,0:T(8,128)(2,1)S(1)}, bf16[16,4096]{1,0:T(8,128)(2,1)S(1)}, u32[]{:S(2)}, u32[]{:S(2)}) collective-permute-start(bf16[16,4096]{1,0:T(8,128)(2,1)S(1)} %fusion.15), channel_id=1, source_target_pairs={{0,2},{1,3},{2,0},{3,1},{4,6},{5,7},{6,4},{7,5},{8,10},{9,11},{10,... | collective-permute-start | bytes 393224 | tf_op jit(solution)/shard_map/ppermute | solution.py:24
  41.9 5.2 %collective-permute-start.9 = (bf16[16,4096]{1,0:T(8,128)(2,1)S(1)}, bf16[16,4096]{1,0:T(8,128)(2,1)S(1)}, u32[]{:S(2)}, u32[]{:S(2)}) collective-permute-start(bf16[16,4096]{1,0:T(8,128)(2,1)S(1)} %fusion.15), channel_id=1, source_target_pairs={{0,1},{1,0},{2,3},{3,2},{4,5},{5,4},{6,7},{7,6},{8,9},{9,8},{10,11... | collective-permute-start | bytes 393224 | tf_op jit(solution)/shard_map/ppermute | solution.py:24
  47.6 1.5 %collective-permute-start.12 = (f32[64,128]{1,0:T(8,128)S(1)}, f32[64,128]{1,0:T(8,128)S(1)}, u32[]{:S(2)}, u32[]{:S(2)}) collective-permute-start(f32[64,128]{1,0:T(8,128)S(1)} %fusion.17), channel_id=1, source_target_pairs={{0,8},{8,0},{1,9},{9,1},{2,10},{10,2},{3,11},{11,3},{4,12},{12,4},... | collective-permute-start | bytes 98312 | tf_op jit(solution)/shard_map/ppermute | solution.py:24
  50.4 1.4 %collective-permute-start.14 = (f32[8,128]{1,0:T(8,128)S(1)}, f32[8,128]{1,0:T(8,128)S(1)}, u32[]{:S(2)}, u32[]{:S(2)}) collective-permute-start(f32[8,128]{1,0:T(8,128)S(1)} %add.95), channel_id=1, source_target_pairs={{0,8},{8,0},{1,9},{9,1},{2,10},{10,2},{3,11},{11,3},{4,12},{12,4},... | collective-permute-start | bytes 12296 | tf_op jit(solution)/shard_map/ppermute | solution.py:24
  51.8 3.6 %collective-permute-start.15 = (f32[8,128]{1,0:T(8,128)S(1)}, f32[8,128]{1,0:T(8,128)S(1)}, u32[]{:S(2)}, u32[]{:S(2)}) collective-permute-start(f32[8,128]{1,0:T(8,128)S(1)} %add.96), channel_id=1, source_target_pairs={{0,1},{1,0},{2,3},{3,2},{4,5},{5,4},{6,7},{7,6},{8,9},{9,8},{10,11... | collective-permute-start | bytes 12296 | tf_op jit(solution)/shard_map/ppermute | solution.py:24
  55.4 3.6 %collective-permute-start.16 = (f32[8,128]{1,0:T(8,128)S(1)}, f32[8,128]{1,0:T(8,128)S(1)}, u32[]{:S(2)}, u32[]{:S(2)}) collective-permute-start(f32[8,128]{1,0:T(8,128)S(1)} %add.97), channel_id=1, source_target_pairs={{0,2},{1,3},{2,0},{3,1},{4,6},{5,7},{6,4},{7,5},{8,10},{9,11},{10,... | collective-permute-start | bytes 12296 | tf_op jit(solution)/shard_map/ppermute | solution.py:24
  59.0 4.6 %collective-permute-start.17 = (f32[8,128]{1,0:T(8,128)S(1)}, f32[8,128]{1,0:T(8,128)S(1)}, u32[]{:S(2)}, u32[]{:S(2)}) collective-permute-start(f32[8,128]{1,0:T(8,128)S(1)} %add.98), channel_id=1, source_target_pairs={{0,4},{1,5},{2,6},{3,7},{4,0},{5,1},{6,2},{7,3},{8,12},{9,13},{10,... | collective-permute-start | bytes 12296 | tf_op jit(solution)/shard_map/ppermute | solution.py:24

commit v6 on v5

--- a/solution.py
+++ b/solution.py
@@ -265,11 +265,10 @@
     enc_dir = adam_direction(grad_enc, m_enc, v_enc)
     squares = jnp.sum((enc_dir * enc_dir).reshape(-1, 8, 128), axis=0)
     squares = squares + jnp.sum((dec_dir * dec_dir).reshape(latents // 8, 8, -1, 128), axis=(0, 2))
+    for bit in high_bits[::-1]:
+        squares = squares + swap(squares, "lat", bit)
+    squares = sum(swap(squares, "lat", k) for k in (3, 2, 1)) + squares
     squares = squares + swap(squares, "src", 1)
-    bit = 1
-    while bit < lat_count:
-        squares = squares + swap(squares, "lat", bit)
-        bit *= 2
     enc_step, dec_step = scale(
         squares, enc_dir, dec_dir, float(2 * source_count * features * latents * lat_count)
     )

time: 65.4 us -> 64.3 us (0.983)
  waiting for transfers between devices: 29.3 us -> 27.8 us
    ppermute x18 -> x19, waiting for transfers between devices: 29.3 us -> 27.8 us  [swap(): return lax.ppermute(value, axis, [(i, i ^ bits) for i in range(count)])]
    ppermute x18 -> x19, starting transfers between devices: 24.6 us -> 25.1 us  [swap(): return lax.ppermute(value, axis, [(i, i ^ bits) for i in range(count)])]
  transfers between devices with their start and end apart: 18 -> 19, of which waited for: 16 -> 16; matrix products, arithmetic and copies ran while one was open for 7% -> 7% of each run, Pallas kernels for 1% -> 1%
where the time goes in v6:
time: 64.3 us; the launch traced here: 64.1 us
  waiting for transfers between devices  27.8 us (43%)
  starting transfers between devices  25.1 us (39%)
  other arithmetic  4.47 us (7%)
  matrix products  3 us (5%)
  Pallas kernels  2.33 us (4%)
  between operations  0.85 us (1%)
    ppermute x19, waiting for transfers between devices, swap(): return lax.ppermute(value, axis, [(i, i ^ bits) for i in range(count)])  27.8 us
    ppermute x19, starting transfers between devices, swap(): return lax.ppermute(value, axis, [(i, i ^ bits) for i in range(count)])  25.1 us
    pallas_call x1, Pallas kernels, scale(): pl.pallas_call(functools.partial(scale_kernel, count), out_shape=(jax.Sha...  1.56 us
    reduce_sum x1, other arithmetic, body(): dec_norm = jnp.sqrt(jnp.sum(dec_wide * dec_wide, axis=1) + norm_eps)  1.52 us
  transfers between devices with their start and end apart: 19, of which 16 were waited for; matrix products, arithmetic and copies ran while one was open for 7% of the time, Pallas kernels for 1%

profile of v6, /device:TPU:0, one launch (start us, length us, event | category | flops | bytes accessed | tf_op | source)
XLA Modules:
  0.0 64.1 jit_solution(12892503766343043808)
XLA Ops:
  0.7 1.3 %constant_dynamic-update-slice_fusion.4 = (bf16[64,4096]{1,0:T(8,128)(2,1)S(1)}, bf16[8,4096]{1,0:T(8,128)(2,1)S(1)}) fusion(bf16[16,1,4096]{2,0,1:T(8,128)(2,1)} %param.8, s32[8]{0:T(128)} %param.9), kind=kOutput, calls=%fused_computation.47 | convolution fusion | flops 1081471 | bytes 262176 | tf_op jit(solution)/shard_map/dot_general | solution.py:214
  1.9 4.1 %collective-permute-start = (bf16[8,4096]{1,0:T(8,128)(2,1)S(1)}, bf16[8,4096]{1,0:T(8,128)(2,1)S(1)}, u32[]{:S(2)}, u32[]{:S(2)}) collective-permute-start(bf16[8,4096]{1,0:T(8,128)(2,1)S(1)} %get-tuple-element.47), channel_id=1, source_target_pairs={{0,4},{1,5},{2,6},{3,7},{4,0},{5,1},{6,2},{7,3},{8,12},{9,13},{10,... | collective-permute-start | bytes 196616 | tf_op jit(solution)/shard_map/ppermute | solution.py:24
  6.0 1.5 %fusion.1 = f32[128]{0:T(128)S(1)} fusion(bf16[1,128,4096]{2,1,0:T(8,128)(2,1)} %param.11), kind=kLoop, calls=%fused_computation.9 | loop fusion | flops 1572736 | bytes 1049088 | tf_op jit(solution)/shard_map/reduce_sum | solution.py:222
  7.7 2.0 %collective-permute-done = bf16[8,4096]{1,0:T(8,128)(2,1)S(1)} collective-permute-done((bf16[8,4096]{1,0:T(8,128)(2,1)S(1)}, bf16[8,4096]{1,0:T(8,128)(2,1)S(1)}, u32[]{:S(2)}, u32[]{:S(2)}) %collective-permute-start) | collective-permute-done | bytes 65568 | tf_op jit(solution)/shard_map/ppermute | solution.py:24
  9.7 1.8 %collective-permute-start.1 = (bf16[16,4096]{1,0:T(8,128)(2,1)S(1)}, bf16[16,4096]{1,0:T(8,128)(2,1)S(1)}, u32[]{:S(2)}, u32[]{:S(2)}) collective-permute-start(bf16[16,4096]{1,0:T(8,128)(2,1)S(1)} %pad_maximum_fusion.1), channel_id=1, source_target_pairs={{0,1},{1,0},{2,3},{3,2},{4,5},{5,4},{6,7},{7,6},{8,9},{9,8},{10,11... | collective-permute-start | bytes 393224 | tf_op jit(solution)/shard_map/ppermute | solution.py:24
  11.5 0.3 collective-permute-start.2
  11.8 1.5 %collective-permute-start.3 = (bf16[16,4096]{1,0:T(8,128)(2,1)S(1)}, bf16[16,4096]{1,0:T(8,128)(2,1)S(1)}, u32[]{:S(2)}, u32[]{:S(2)}) collective-permute-start(bf16[16,4096]{1,0:T(8,128)(2,1)S(1)} %pad_maximum_fusion.1), channel_id=1, source_target_pairs={{0,2},{1,3},{2,0},{3,1},{4,6},{5,7},{6,4},{7,5},{8,10},{9,11},{10,... | collective-permute-start | bytes 393224 | tf_op jit(solution)/shard_map/ppermute | solution.py:24
  13.3 2.5 %collective-permute-done.1 = bf16[16,4096]{1,0:T(8,128)(2,1)S(1)} collective-permute-done((bf16[16,4096]{1,0:T(8,128)(2,1)S(1)}, bf16[16,4096]{1,0:T(8,128)(2,1)S(1)}, u32[]{:S(2)}, u32[]{:S(2)}) %collective-permute-start.1) | collective-permute-done | bytes 131104 | tf_op jit(solution)/shard_map/ppermute | solution.py:24
  15.8 1.6 %collective-permute-done.2 = bf16[16,4096]{1,0:T(8,128)(2,1)S(1)} collective-permute-done((bf16[16,4096]{1,0:T(8,128)(2,1)S(1)}, bf16[16,4096]{1,0:T(8,128)(2,1)S(1)}, u32[]{:S(2)}, u32[]{:S(2)}) %collective-permute-start.2) | collective-permute-done | bytes 131104 | tf_op jit(solution)/shard_map/ppermute | solution.py:24
  17.4 0.4 collective-permute-done.3
  17.7 0.3 fusion.12.own_ref
  18.2 1.2 %collective-permute-done.4.other_ref = f32[64,128]{1,0:T(8,128)S(1)} collective-permute-done((f32[64,128]{1,0:T(8,128)S(1)}, f32[64,128]{1,0:T(8,128)S(1)}, u32[]{:S(2)}, u32[]{:S(2)}) %collective-permute-start.4) | collective-permute-done | bytes 32800 | tf_op jit(solution)/shard_map/ppermute | solution.py:24
  19.3 0.5 decode_and_pack.1
  19.8 1.7 %collective-permute-start.5 = (s16[16,4096]{1,0:T(8,128)(2,1)S(1)}, s16[16,4096]{1,0:T(8,128)(2,1)S(1)}, u32[]{:S(2)}, u32[]{:S(2)}) collective-permute-start(s16[16,4096]{1,0:T(8,128)(2,1)S(1)} %get-tuple-element.21), channel_id=1, source_target_pairs={{0,1},{1,0},{2,3},{3,2},{4,5},{5,4},{6,7},{7,6},{8,9},{9,8},{10,11... | collective-permute-start | bytes 393224 | tf_op jit(solution)/shard_map/ppermute | solution.py:24
  21.5 1.4 %collective-permute-start.6 = (s16[16,4096]{1,0:T(8,128)(2,1)S(1)}, s16[16,4096]{1,0:T(8,128)(2,1)S(1)}, u32[]{:S(2)}, u32[]{:S(2)}) collective-permute-start(s16[16,4096]{1,0:T(8,128)(2,1)S(1)} %get-tuple-element.30), channel_id=1, source_target_pairs={{0,3},{1,2},{2,1},{3,0},{4,7},{5,6},{6,5},{7,4},{8,11},{9,10},{10,... | collective-permute-start | bytes 393224 | tf_op jit(solution)/shard_map/ppermute | solution.py:24
  22.9 0.5 collective-permute-start.7
  23.4 0.5 convert_multiply_fusion.2
  23.9 0.2 copy-done.4
  24.2 0.3 copy-done.5
  24.5 0.3 convert_multiply_fusion.4
  24.8 3.0 %collective-permute-done.5.p1_ref = s16[16,4096]{1,0:T(8,128)(2,1)S(1)} collective-permute-done((s16[16,4096]{1,0:T(8,128)(2,1)S(1)}, s16[16,4096]{1,0:T(8,128)(2,1)S(1)}, u32[]{:S(2)}, u32[]{:S(2)}) %collective-permute-start.5) | collective-permute-done | bytes 131104 | tf_op jit(solution)/shard_map/ppermute | solution.py:24
  27.8 1.0 %collective-permute-done.6.p2_ref = s16[16,4096]{1,0:T(8,128)(2,1)S(1)} collective-permute-done((s16[16,4096]{1,0:T(8,128)(2,1)S(1)}, s16[16,4096]{1,0:T(8,128)(2,1)S(1)}, u32[]{:S(2)}, u32[]{:S(2)}) %collective-permute-start.6) | collective-permute-done | bytes 131104 | tf_op jit(solution)/shard_map/ppermute | solution.py:24
  28.8 0.7 %collective-permute-done.7.p3_ref = s16[16,4096]{1,0:T(8,128)(2,1)S(1)} collective-permute-done((s16[16,4096]{1,0:T(8,128)(2,1)S(1)}, s16[16,4096]{1,0:T(8,128)(2,1)S(1)}, u32[]{:S(2)}, u32[]{:S(2)}) %collective-permute-start.7) | collective-permute-done | bytes 131104 | tf_op jit(solution)/shard_map/ppermute | solution.py:24
  29.5 0.3 quad_sum.1
  29.8 3.5 %collective-permute-start.8 = (s16[16,4096]{1,0:T(8,128)(2,1)S(1)}, s16[16,4096]{1,0:T(8,128)(2,1)S(1)}, u32[]{:S(2)}, u32[]{:S(2)}) collective-permute-start(s16[16,4096]{1,0:T(8,128)(2,1)S(1)} %get-tuple-element.33), channel_id=1, source_target_pairs={{0,4},{1,5},{2,6},{3,7},{4,0},{5,1},{6,2},{7,3},{8,12},{9,13},{10,... | collective-permute-start | bytes 393224 | tf_op jit(solution)/shard_map/ppermute | solution.py:24
  33.3 5.5 %collective-permute-done.8 = s16[16,4096]{1,0:T(8,128)(2,1)S(1)} collective-permute-done((s16[16,4096]{1,0:T(8,128)(2,1)S(1)}, s16[16,4096]{1,0:T(8,128)(2,1)S(1)}, u32[]{:S(2)}, u32[]{:S(2)}) %collective-permute-start.8) | collective-permute-done | bytes 131104 | tf_op jit(solution)/shard_map/ppermute | solution.py:24
  38.8 0.1 select_reduce_fusion
  38.9 0.1 multiply_bitcast_fusion
  39.1 1.3 %collective-permute-start.10 = (bf16[16,4096]{1,0:T(8,128)(2,1)S(1)}, bf16[16,4096]{1,0:T(8,128)(2,1)S(1)}, u32[]{:S(2)}, u32[]{:S(2)}) collective-permute-start(bf16[16,4096]{1,0:T(8,128)(2,1)S(1)} %fusion.15), channel_id=1, source_target_pairs={{0,3},{1,2},{2,1},{3,0},{4,7},{5,6},{6,5},{7,4},{8,11},{9,10},{10,... | collective-permute-start | bytes 393224 | tf_op jit(solution)/shard_map/ppermute | solution.py:24
  40.4 1.4 %collective-permute-start.11 = (bf16[16,4096]{1,0:T(8,128)(2,1)S(1)}, bf16[16,4096]{1,0:T(8,128)(2,1)S(1)}, u32[]{:S(2)}, u32[]{:S(2)}) collective-permute-start(bf16[16,4096]{1,0:T(8,128)(2,1)S(1)} %fusion.15), channel_id=1, source_target_pairs={{0,2},{1,3},{2,0},{3,1},{4,6},{5,7},{6,4},{7,5},{8,10},{9,11},{10,... | collective-permute-start | bytes 393224 | tf_op jit(solution)/shard_map/ppermute | solution.py:24
  41.9 0.8 %collective-permute-start.9 = (bf16[16,4096]{1,0:T(8,128)(2,1)S(1)}, bf16[16,4096]{1,0:T(8,128)(2,1)S(1)}, u32[]{:S(2)}, u32[]{:S(2)}) collective-permute-start(bf16[16,4096]{1,0:T(8,128)(2,1)S(1)} %fusion.15), channel_id=1, source_target_pairs={{0,1},{1,0},{2,3},{3,2},{4,5},{5,4},{6,7},{7,6},{8,9},{9,8},{10,11... | collective-permute-start | bytes 393224 | tf_op jit(solution)/shard_map/ppermute | solution.py:24
  42.6 3.0 %collective-permute-done.10 = bf16[16,4096]{1,0:T(8,128)(2,1)S(1)} collective-permute-done((bf16[16,4096]{1,0:T(8,128)(2,1)S(1)}, bf16[16,4096]{1,0:T(8,128)(2,1)S(1)}, u32[]{:S(2)}, u32[]{:S(2)}) %collective-permute-start.10) | collective-permute-done | bytes 131104 | tf_op jit(solution)/shard_map/ppermute | solution.py:24
  45.7 1.1 %collective-permute-done.11 = bf16[16,4096]{1,0:T(8,128)(2,1)S(1)} collective-permute-done((bf16[16,4096]{1,0:T(8,128)(2,1)S(1)}, bf16[16,4096]{1,0:T(8,128)(2,1)S(1)}, u32[]{:S(2)}, u32[]{:S(2)}) %collective-permute-start.11) | collective-permute-done | bytes 131104 | tf_op jit(solution)/shard_map/ppermute | solution.py:24
  46.8 0.3 collective-permute-done.9
  47.1 0.5 fusion.17
  47.6 0.1 collective-permute-start.12
  47.6 0.5 fusion
  48.1 0.9 %bitcast_reduce_fusion = (f32[8,128]{1,0:T(8,128)S(1)}, f32[128,4096]{1,0:T(8,128)S(1)}) fusion(f32[128,4096]{1,0:T(8,128)S(1)} %get-tuple-element.37, f32[128,4096]{1,0:T(8,128)S(1)} %fusion, f32[128,4096]{1,0:T(8,128)S(1)} %get-tuple-element.35), kind=kLoop, calls=%fused_computation.20 | loop fusion | flops 5766144 | bytes 8392704 | tf_op jit(solution)/shard_map/reduce_sum | solution.py:267
  49.0 0.5 fusion.18
  49.5 0.9 %bitcast_reduce_fusion.1 = (f32[8,128]{1,0:T(8,128)S(1)}, f32[4096,128]{1,0:T(8,128)S(1)}) fusion(f32[4096,128]{1,0:T(8,128)S(1)} %get-tuple-element.34, f32[4096,128]{1,0:T(8,128)S(1)} %fusion.18, f32[4096,128]{1,0:T(8,128)S(1)} %get-tuple-element.27), kind=kLoop, calls=%fused_computation.21 | loop fusion | flops 5766144 | bytes 8392704 | tf_op jit(solution)/shard_map/reduce_sum | solution.py:266
  50.4 3.1 %collective-permute-start.14 = (f32[8,128]{1,0:T(8,128)S(1)}, f32[8,128]{1,0:T(8,128)S(1)}, u32[]{:S(2)}, u32[]{:S(2)}) collective-permute-start(f32[8,128]{1,0:T(8,128)S(1)} %add.98), channel_id=1, source_target_pairs={{0,4},{1,5},{2,6},{3,7},{4,0},{5,1},{6,2},{7,3},{8,12},{9,13},{10,... | collective-permute-start | bytes 12296 | tf_op jit(solution)/shard_map/ppermute | solution.py:24
  53.5 1.6 %collective-permute-done.14 = f32[8,128]{1,0:T(8,128)S(1)} collective-permute-done((f32[8,128]{1,0:T(8,128)S(1)}, f32[8,128]{1,0:T(8,128)S(1)}, u32[]{:S(2)}, u32[]{:S(2)}) %collective-permute-start.14) | collective-permute-done | bytes 4128 | tf_op jit(solution)/shard_map/ppermute | solution.py:24
  55.1 2.6 %collective-permute-start.15 = (f32[8,128]{1,0:T(8,128)S(1)}, f32[8,128]{1,0:T(8,128)S(1)}, u32[]{:S(2)}, u32[]{:S(2)}) collective-permute-start(f32[8,128]{1,0:T(8,128)S(1)} %add.99), channel_id=1, source_target_pairs={{0,3},{1,2},{2,1},{3,0},{4,7},{5,6},{6,5},{7,4},{8,11},{9,10},{10,... | collective-permute-start | bytes 12296 | tf_op jit(solution)/shard_map/ppermute | solution.py:24
  57.7 0.8 %collective-permute-start.17 = (f32[8,128]{1,0:T(8,128)S(1)}, f32[8,128]{1,0:T(8,128)S(1)}, u32[]{:S(2)}, u32[]{:S(2)}) collective-permute-start(f32[8,128]{1,0:T(8,128)S(1)} %add.99), channel_id=1, source_target_pairs={{0,1},{1,0},{2,3},{3,2},{4,5},{5,4},{6,7},{7,6},{8,9},{9,8},{10,11... | collective-permute-start | bytes 12296 | tf_op jit(solution)/shard_map/ppermute | solution.py:24
  58.6 1.0 %collective-permute-done.15 = f32[8,128]{1,0:T(8,128)S(1)} collective-permute-done((f32[8,128]{1,0:T(8,128)S(1)}, f32[8,128]{1,0:T(8,128)S(1)}, u32[]{:S(2)}, u32[]{:S(2)}) %collective-permute-start.15) | collective-permute-done | bytes 4128 | tf_op jit(solution)/shard_map/ppermute | solution.py:24
  59.6 1.7 %collective-permute-done.16 = f32[8,128]{1,0:T(8,128)S(1)} collective-permute-done((f32[8,128]{1,0:T(8,128)S(1)}, f32[8,128]{1,0:T(8,128)S(1)}, u32[]{:S(2)}, u32[]{:S(2)}) %collective-permute-start.16) | collective-permute-done | bytes 4128 | tf_op jit(solution)/shard_map/ppermute | solution.py:24
  61.4 1.2 %collective-permute-done.18 = f32[8,128]{1,0:T(8,128)S(1)} collective-permute-done((f32[8,128]{1,0:T(8,128)S(1)}, f32[8,128]{1,0:T(8,128)S(1)}, u32[]{:S(2)}, u32[]{:S(2)}) %collective-permute-start.18) | collective-permute-done | bytes 4128 | tf_op jit(solution)/shard_map/ppermute | solution.py:24
  62.6 1.6 %scale_directions.1 = (bf16[4096,128]{1,0:T(8,128)(2,1)}, bf16[128,4096]{1,0:T(8,128)(2,1)}) custom-call(f32[8,128]{1,0:T(8,128)S(1)} %add.103.squares_ref, f32[4096,128]{1,0:T(8,128)S(1)} %get-tuple-element.43.enc_ref, f32[128,4096]{1,0:T(8,128)S(1)} %get-tuple-element.41.dec_ref), custom_call_target="tpu_custom_call" | custom-call | tf_op jit(solution)/shard_map/scale_directions/pallas_call | solution.py:53
  (33 shorter events, 0.4 us)
Async XLA Ops:
  0.6 17.1 %copy-start = (bf16[1,4096,128]{2,1,0:T(8,128)(2,1)S(1)}, bf16[1,4096,128]{2,1,0:T(8,128)(2,1)}, u32[]{:S(2)}) copy-start(bf16[1,4096,128]{2,1,0:T(8,128)(2,1)} %param.10) | copy-start | bytes 3145732
  0.6 18.7 %copy-start.1 = (bf16[1,128,4096]{2,1,0:T(8,128)(2,1)S(1)}, bf16[1,128,4096]{2,1,0:T(8,128)(2,1)}, u32[]{:S(2)}) copy-start(bf16[1,128,4096]{2,1,0:T(8,128)(2,1)} %param.11) | copy-start | bytes 3145732
  1.9 7.7 %collective-permute-start = (bf16[8,4096]{1,0:T(8,128)(2,1)S(1)}, bf16[8,4096]{1,0:T(8,128)(2,1)S(1)}, u32[]{:S(2)}, u32[]{:S(2)}) collective-permute-start(bf16[8,4096]{1,0:T(8,128)(2,1)S(1)} %get-tuple-element.47), channel_id=1, source_target_pairs={{0,4},{1,5},{2,6},{3,7},{4,0},{5,1},{6,2},{7,3},{8,12},{9,13},{10,... | collective-permute-start | bytes 196616 | tf_op jit(solution)/shard_map/ppermute | solution.py:24
  7.5 15.9 %copy-start.2 = (bf16[1,128,4096]{2,1,0:T(8,128)(2,1)S(1)}, bf16[1,128,4096]{2,1,0:T(8,128)(2,1)}, u32[]{:S(2)}) copy-start(bf16[1,128,4096]{2,1,0:T(8,128)(2,1)} %param.15) | copy-start | bytes 3145732
  7.6 15.8 %copy-start.3 = (bf16[1,128,4096]{2,1,0:T(8,128)(2,1)S(1)}, bf16[1,128,4096]{2,1,0:T(8,128)(2,1)}, u32[]{:S(2)}) copy-start(bf16[1,128,4096]{2,1,0:T(8,128)(2,1)} %param.14) | copy-start | bytes 3145732
  7.6 35.1 %collective-permute-start.13 = (f32[128]{0:T(128)S(1)}, f32[128]{0:T(128)S(1)}, u32[]{:S(2)}, u32[]{:S(2)}) collective-permute-start(f32[128]{0:T(128)S(1)} %add_sqrt_fusion), channel_id=1, source_target_pairs={{0,8},{8,0},{1,9},{9,1},{2,10},{10,2},{3,11},{11,3},{4,12},{12,4},... | collective-permute-start | bytes 1544 | tf_op jit(solution)/shard_map/ppermute | solution.py:24
  9.7 6.1 %collective-permute-start.1 = (bf16[16,4096]{1,0:T(8,128)(2,1)S(1)}, bf16[16,4096]{1,0:T(8,128)(2,1)S(1)}, u32[]{:S(2)}, u32[]{:S(2)}) collective-permute-start(bf16[16,4096]{1,0:T(8,128)(2,1)S(1)} %pad_maximum_fusion.1), channel_id=1, source_target_pairs={{0,1},{1,0},{2,3},{3,2},{4,5},{5,4},{6,7},{7,6},{8,9},{9,8},{10,11... | collective-permute-start | bytes 393224 | tf_op jit(solution)/shard_map/ppermute | solution.py:24
  11.5 5.9 %collective-permute-start.2 = (bf16[16,4096]{1,0:T(8,128)(2,1)S(1)}, bf16[16,4096]{1,0:T(8,128)(2,1)S(1)}, u32[]{:S(2)}, u32[]{:S(2)}) collective-permute-start(bf16[16,4096]{1,0:T(8,128)(2,1)S(1)} %pad_maximum_fusion.1), channel_id=1, source_target_pairs={{0,3},{1,2},{2,1},{3,0},{4,7},{5,6},{6,5},{7,4},{8,11},{9,10},{10,... | collective-permute-start | bytes 393224 | tf_op jit(solution)/shard_map/ppermute | solution.py:24
  11.8 5.9 %collective-permute-start.3 = (bf16[16,4096]{1,0:T(8,128)(2,1)S(1)}, bf16[16,4096]{1,0:T(8,128)(2,1)S(1)}, u32[]{:S(2)}, u32[]{:S(2)}) collective-permute-start(bf16[16,4096]{1,0:T(8,128)(2,1)S(1)} %pad_maximum_fusion.1), channel_id=1, source_target_pairs={{0,2},{1,3},{2,0},{3,1},{4,6},{5,7},{6,4},{7,5},{8,10},{9,11},{10,... | collective-permute-start | bytes 393224 | tf_op jit(solution)/shard_map/ppermute | solution.py:24
  18.1 1.3 %collective-permute-start.4 = (f32[64,128]{1,0:T(8,128)S(1)}, f32[64,128]{1,0:T(8,128)S(1)}, u32[]{:S(2)}, u32[]{:S(2)}) collective-permute-start(f32[64,128]{1,0:T(8,128)S(1)} %fusion.12.own_ref), channel_id=1, source_target_pairs={{0,8},{8,0},{1,9},{9,1},{2,10},{10,2},{3,11},{11,3},{4,12},{12,4},... | collective-permute-start | bytes 98312 | tf_op jit(solution)/shard_map/ppermute | solution.py:24
  19.8 7.9 %collective-permute-start.5 = (s16[16,4096]{1,0:T(8,128)(2,1)S(1)}, s16[16,4096]{1,0:T(8,128)(2,1)S(1)}, u32[]{:S(2)}, u32[]{:S(2)}) collective-permute-start(s16[16,4096]{1,0:T(8,128)(2,1)S(1)} %get-tuple-element.21), channel_id=1, source_target_pairs={{0,1},{1,0},{2,3},{3,2},{4,5},{5,4},{6,7},{7,6},{8,9},{9,8},{10,11... | collective-permute-start | bytes 393224 | tf_op jit(solution)/shard_map/ppermute | solution.py:24
  21.5 7.3 %collective-permute-start.6 = (s16[16,4096]{1,0:T(8,128)(2,1)S(1)}, s16[16,4096]{1,0:T(8,128)(2,1)S(1)}, u32[]{:S(2)}, u32[]{:S(2)}) collective-permute-start(s16[16,4096]{1,0:T(8,128)(2,1)S(1)} %get-tuple-element.30), channel_id=1, source_target_pairs={{0,3},{1,2},{2,1},{3,0},{4,7},{5,6},{6,5},{7,4},{8,11},{9,10},{10,... | collective-permute-start | bytes 393224 | tf_op jit(solution)/shard_map/ppermute | solution.py:24
  22.9 1.2 %copy-start.4 = (bf16[1,4096,128]{2,1,0:T(8,128)(2,1)S(1)}, bf16[1,4096,128]{2,1,0:T(8,128)(2,1)}, u32[]{:S(2)}) copy-start(bf16[1,4096,128]{2,1,0:T(8,128)(2,1)} %param.13) | copy-start | bytes 3145732
  22.9 1.5 %copy-start.5 = (bf16[1,4096,128]{2,1,0:T(8,128)(2,1)S(1)}, bf16[1,4096,128]{2,1,0:T(8,128)(2,1)}, u32[]{:S(2)}) copy-start(bf16[1,4096,128]{2,1,0:T(8,128)(2,1)} %param.12) | copy-start | bytes 3145732
  22.9 6.6 %collective-permute-start.7 = (s16[16,4096]{1,0:T(8,128)(2,1)S(1)}, s16[16,4096]{1,0:T(8,128)(2,1)S(1)}, u32[]{:S(2)}, u32[]{:S(2)}) collective-permute-start(s16[16,4096]{1,0:T(8,128)(2,1)S(1)} %get-tuple-element.31), channel_id=1, source_target_pairs={{0,2},{1,3},{2,0},{3,1},{4,6},{5,7},{6,4},{7,5},{8,10},{9,11},{10,... | collective-permute-start | bytes 393224 | tf_op jit(solution)/shard_map/ppermute | solution.py:24
  29.8 9.0 %collective-permute-start.8 = (s16[16,4096]{1,0:T(8,128)(2,1)S(1)}, s16[16,4096]{1,0:T(8,128)(2,1)S(1)}, u32[]{:S(2)}, u32[]{:S(2)}) collective-permute-start(s16[16,4096]{1,0:T(8,128)(2,1)S(1)} %get-tuple-element.33), channel_id=1, source_target_pairs={{0,4},{1,5},{2,6},{3,7},{4,0},{5,1},{6,2},{7,3},{8,12},{9,13},{10,... | collective-permute-start | bytes 393224 | tf_op jit(solution)/shard_map/ppermute | solution.py:24
  39.1 6.6 %collective-permute-start.10 = (bf16[16,4096]{1,0:T(8,128)(2,1)S(1)}, bf16[16,4096]{1,0:T(8,128)(2,1)S(1)}, u32[]{:S(2)}, u32[]{:S(2)}) collective-permute-start(bf16[16,4096]{1,0:T(8,128)(2,1)S(1)} %fusion.15), channel_id=1, source_target_pairs={{0,3},{1,2},{2,1},{3,0},{4,7},{5,6},{6,5},{7,4},{8,11},{9,10},{10,... | collective-permute-start | bytes 393224 | tf_op jit(solution)/shard_map/ppermute | solution.py:24
  40.4 6.3 %collective-permute-start.11 = (bf16[16,4096]{1,0:T(8,128)(2,1)S(1)}, bf16[16,4096]{1,0:T(8,128)(2,1)S(1)}, u32[]{:S(2)}, u32[]{:S(2)}) collective-permute-start(bf16[16,4096]{1,0:T(8,128)(2,1)S(1)} %fusion.15), channel_id=1, source_target_pairs={{0,2},{1,3},{2,0},{3,1},{4,6},{5,7},{6,4},{7,5},{8,10},{9,11},{10,... | collective-permute-start | bytes 393224 | tf_op jit(solution)/shard_map/ppermute | solution.py:24
  41.9 5.2 %collective-permute-start.9 = (bf16[16,4096]{1,0:T(8,128)(2,1)S(1)}, bf16[16,4096]{1,0:T(8,128)(2,1)S(1)}, u32[]{:S(2)}, u32[]{:S(2)}) collective-permute-start(bf16[16,4096]{1,0:T(8,128)(2,1)S(1)} %fusion.15), channel_id=1, source_target_pairs={{0,1},{1,0},{2,3},{3,2},{4,5},{5,4},{6,7},{7,6},{8,9},{9,8},{10,11... | collective-permute-start | bytes 393224 | tf_op jit(solution)/shard_map/ppermute | solution.py:24
  47.6 1.5 %collective-permute-start.12 = (f32[64,128]{1,0:T(8,128)S(1)}, f32[64,128]{1,0:T(8,128)S(1)}, u32[]{:S(2)}, u32[]{:S(2)}) collective-permute-start(f32[64,128]{1,0:T(8,128)S(1)} %fusion.17), channel_id=1, source_target_pairs={{0,8},{8,0},{1,9},{9,1},{2,10},{10,2},{3,11},{11,3},{4,12},{12,4},... | collective-permute-start | bytes 98312 | tf_op jit(solution)/shard_map/ppermute | solution.py:24
  50.4 4.7 %collective-permute-start.14 = (f32[8,128]{1,0:T(8,128)S(1)}, f32[8,128]{1,0:T(8,128)S(1)}, u32[]{:S(2)}, u32[]{:S(2)}) collective-permute-start(f32[8,128]{1,0:T(8,128)S(1)} %add.98), channel_id=1, source_target_pairs={{0,4},{1,5},{2,6},{3,7},{4,0},{5,1},{6,2},{7,3},{8,12},{9,13},{10,... | collective-permute-start | bytes 12296 | tf_op jit(solution)/shard_map/ppermute | solution.py:24
  55.1 4.5 %collective-permute-start.15 = (f32[8,128]{1,0:T(8,128)S(1)}, f32[8,128]{1,0:T(8,128)S(1)}, u32[]{:S(2)}, u32[]{:S(2)}) collective-permute-start(f32[8,128]{1,0:T(8,128)S(1)} %add.99), channel_id=1, source_target_pairs={{0,3},{1,2},{2,1},{3,0},{4,7},{5,6},{6,5},{7,4},{8,11},{9,10},{10,... | collective-permute-start | bytes 12296 | tf_op jit(solution)/shard_map/ppermute | solution.py:24
  57.7 3.6 %collective-permute-start.16 = (f32[8,128]{1,0:T(8,128)S(1)}, f32[8,128]{1,0:T(8,128)S(1)}, u32[]{:S(2)}, u32[]{:S(2)}) collective-permute-start(f32[8,128]{1,0:T(8,128)S(1)} %add.99), channel_id=1, source_target_pairs={{0,2},{1,3},{2,0},{3,1},{4,6},{5,7},{6,4},{7,5},{8,10},{9,11},{10,... | collective-permute-start | bytes 12296 | tf_op jit(solution)/shard_map/ppermute | solution.py:24
  57.7 3.6 %collective-permute-start.17 = (f32[8,128]{1,0:T(8,128)S(1)}, f32[8,128]{1,0:T(8,128)S(1)}, u32[]{:S(2)}, u32[]{:S(2)}) collective-permute-start(f32[8,128]{1,0:T(8,128)S(1)} %add.99), channel_id=1, source_target_pairs={{0,1},{1,0},{2,3},{3,2},{4,5},{5,4},{6,7},{7,6},{8,9},{9,8},{10,11... | collective-permute-start | bytes 12296 | tf_op jit(solution)/shard_map/ppermute | solution.py:24
  61.3 1.2 %collective-permute-start.18 = (f32[8,128]{1,0:T(8,128)S(1)}, f32[8,128]{1,0:T(8,128)S(1)}, u32[]{:S(2)}, u32[]{:S(2)}) collective-permute-start(f32[8,128]{1,0:T(8,128)S(1)} %add_add_fusion), channel_id=1, source_target_pairs={{0,8},{8,0},{1,9},{9,1},{2,10},{10,2},{3,11},{11,3},{4,12},{12,4},... | collective-permute-start | bytes 12296 | tf_op jit(solution)/shard_map/ppermute | solution.py:24

commit v7 on v6

--- a/solution.py
+++ b/solution.py
@@ -15,8 +15,8 @@
 norm_eps = 1e-06
 f32 = jnp.float32
 bf16 = jnp.bfloat16
-CHUNK = 512
-ORDER = (1, 3, 2)
+CHUNK = 256
+ORDER = (3, 1, 2)
 
 
 def swap(value, axis, bits):
@@ -31,8 +31,8 @@
     return new_first * lax.rsqrt(size * size)
 
 
-def scale_kernel(count, squares_ref, enc_ref, dec_ref, enc_out, dec_out, enc_buf, dec_buf, sems):
-    total = jnp.sum(squares_ref[...], keepdims=True)
+def scale_kernel(count, squares_ref, other_ref, enc_ref, dec_ref, enc_out, dec_out, enc_buf, dec_buf, sems):
+    total = jnp.sum(squares_ref[...] + other_ref[...], keepdims=True)
     update_rms = jnp.sqrt(total / count)
     factor = 1.0 / jnp.maximum(1.0, update_rms / clip_rms)
     steps = 4
@@ -49,11 +49,11 @@
         copy.wait()
 
 
-def scale(squares, enc_dir, dec_dir, count):
+def scale(squares, other, enc_dir, dec_dir, count):
     return pl.pallas_call(
         functools.partial(scale_kernel, count),
         out_shape=(jax.ShapeDtypeStruct(enc_dir.shape, bf16), jax.ShapeDtypeStruct(dec_dir.shape, bf16)),
-        in_specs=[pl.BlockSpec(memory_space=pltpu.VMEM)] * 3,
+        in_specs=[pl.BlockSpec(memory_space=pltpu.VMEM)] * 4,
         out_specs=[pl.BlockSpec(memory_space=pl.ANY)] * 2,
         scratch_shapes=[
             pltpu.VMEM(enc_dir.shape, bf16),
@@ -62,7 +62,7 @@
         ],
         compiler_params=pltpu.CompilerParams(vmem_limit_bytes=24 << 20),
         name="scale_directions",
-    )(squares, enc_dir, dec_dir)
+    )(squares, other, enc_dir, dec_dir)
 
 
 def pack(value):
@@ -227,7 +227,7 @@
         (feature_codes, m_enc, v_enc, m_dec, v_dec)
     )
     norm_total = dec_norm + swap(dec_norm, "src", 1)
-    received = [swap(part, "lat", k) for part, k in zip(parts, ORDER)]
+    received = [swap(parts[ORDER.index(k)], "lat", k) for k in (1, 3, 2)]
     received[0], m_enc, v_enc, m_dec, v_dec = lax.optimization_barrier(
         (
             received[0],
@@ -268,9 +268,9 @@
     for bit in high_bits[::-1]:
         squares = squares + swap(squares, "lat", bit)
     squares = sum(swap(squares, "lat", k) for k in (3, 2, 1)) + squares
-    squares = squares + swap(squares, "src", 1)
+    other_squares = swap(squares, "src", 1)
     enc_step, dec_step = scale(
-        squares, enc_dir, dec_dir, float(2 * source_count * features * latents * lat_count)
+        squares, other_squares, enc_dir, dec_dir, float(2 * source_count * features * latents * lat_count)
     )
     return enc_step[None], dec_step[None]
 

time: 64.3 us -> 64.2 us (level)
  transfers between devices with their start and end apart: 19 -> 19, of which waited for: 16 -> 17; matrix products, arithmetic and copies ran while one was open for 7% -> 7% of each run, Pallas kernels for 1% -> 1%
where the time goes in v7:
time: 64.2 us; the launch traced here: 64 us
  waiting for transfers between devices  28 us (44%)
  starting transfers between devices  24.9 us (39%)
  other arithmetic  4.46 us (7%)
  matrix products  3 us (5%)
  Pallas kernels  2.33 us (4%)
  between operations  0.84 us (1%)
    ppermute x19, waiting for transfers between devices, swap(): return lax.ppermute(value, axis, [(i, i ^ bits) for i in range(count)])  28 us
    ppermute x19, starting transfers between devices, swap(): return lax.ppermute(value, axis, [(i, i ^ bits) for i in range(count)])  24.9 us
    pallas_call x1, Pallas kernels, scale(): pl.pallas_call(functools.partial(scale_kernel, count), out_shape=(jax.Sha...  1.55 us
    reduce_sum x1, other arithmetic, body(): dec_norm = jnp.sqrt(jnp.sum(dec_wide * dec_wide, axis=1) + norm_eps)  1.52 us
  transfers between devices with their start and end apart: 19, of which 17 were waited for; matrix products, arithmetic and copies ran while one was open for 7% of the time, Pallas kernels for 1%

profile of v7, /device:TPU:0, one launch (start us, length us, event | category | flops | bytes accessed | tf_op | source)
XLA Modules:
  0.0 64.0 jit_solution(11772595817560784539)
XLA Ops:
  0.7 1.3 %constant_dynamic-update-slice_fusion.4 = (bf16[64,4096]{1,0:T(8,128)(2,1)S(1)}, bf16[8,4096]{1,0:T(8,128)(2,1)S(1)}) fusion(bf16[16,1,4096]{2,0,1:T(8,128)(2,1)} %param.8, s32[8]{0:T(128)} %param.9), kind=kOutput, calls=%fused_computation.47 | convolution fusion | flops 1081471 | bytes 262176 | tf_op jit(solution)/shard_map/dot_general | solution.py:214
  1.9 4.1 %collective-permute-start = (bf16[8,4096]{1,0:T(8,128)(2,1)S(1)}, bf16[8,4096]{1,0:T(8,128)(2,1)S(1)}, u32[]{:S(2)}, u32[]{:S(2)}) collective-permute-start(bf16[8,4096]{1,0:T(8,128)(2,1)S(1)} %get-tuple-element.47), channel_id=1, source_target_pairs={{0,4},{1,5},{2,6},{3,7},{4,0},{5,1},{6,2},{7,3},{8,12},{9,13},{10,... | collective-permute-start | bytes 196616 | tf_op jit(solution)/shard_map/ppermute | solution.py:24
  6.0 1.5 %fusion.1 = f32[128]{0:T(128)S(1)} fusion(bf16[1,128,4096]{2,1,0:T(8,128)(2,1)} %param.11), kind=kLoop, calls=%fused_computation.9 | loop fusion | flops 1572736 | bytes 1049088 | tf_op jit(solution)/shard_map/reduce_sum | solution.py:222
  7.7 2.0 %collective-permute-done = bf16[8,4096]{1,0:T(8,128)(2,1)S(1)} collective-permute-done((bf16[8,4096]{1,0:T(8,128)(2,1)S(1)}, bf16[8,4096]{1,0:T(8,128)(2,1)S(1)}, u32[]{:S(2)}, u32[]{:S(2)}) %collective-permute-start) | collective-permute-done | bytes 65568 | tf_op jit(solution)/shard_map/ppermute | solution.py:24
  9.7 1.6 %collective-permute-start.1 = (bf16[16,4096]{1,0:T(8,128)(2,1)S(1)}, bf16[16,4096]{1,0:T(8,128)(2,1)S(1)}, u32[]{:S(2)}, u32[]{:S(2)}) collective-permute-start(bf16[16,4096]{1,0:T(8,128)(2,1)S(1)} %pad_maximum_fusion.1), channel_id=1, source_target_pairs={{0,3},{1,2},{2,1},{3,0},{4,7},{5,6},{6,5},{7,4},{8,11},{9,10},{10,... | collective-permute-start | bytes 393224 | tf_op jit(solution)/shard_map/ppermute | solution.py:24
  11.3 0.5 collective-permute-start.2
  11.8 1.5 %collective-permute-start.3 = (bf16[16,4096]{1,0:T(8,128)(2,1)S(1)}, bf16[16,4096]{1,0:T(8,128)(2,1)S(1)}, u32[]{:S(2)}, u32[]{:S(2)}) collective-permute-start(bf16[16,4096]{1,0:T(8,128)(2,1)S(1)} %pad_maximum_fusion.1), channel_id=1, source_target_pairs={{0,2},{1,3},{2,0},{3,1},{4,6},{5,7},{6,4},{7,5},{8,10},{9,11},{10,... | collective-permute-start | bytes 393224 | tf_op jit(solution)/shard_map/ppermute | solution.py:24
  13.3 3.7 %collective-permute-done.1 = bf16[16,4096]{1,0:T(8,128)(2,1)S(1)} collective-permute-done((bf16[16,4096]{1,0:T(8,128)(2,1)S(1)}, bf16[16,4096]{1,0:T(8,128)(2,1)S(1)}, u32[]{:S(2)}, u32[]{:S(2)}) %collective-permute-start.1) | collective-permute-done | bytes 131104 | tf_op jit(solution)/shard_map/ppermute | solution.py:24
  17.0 0.4 collective-permute-done.2
  17.4 0.2 collective-permute-done.3
  17.6 0.3 fusion.12.own_ref
  18.0 1.2 %collective-permute-done.4.other_ref = f32[64,128]{1,0:T(8,128)S(1)} collective-permute-done((f32[64,128]{1,0:T(8,128)S(1)}, f32[64,128]{1,0:T(8,128)S(1)}, u32[]{:S(2)}, u32[]{:S(2)}) %collective-permute-start.4) | collective-permute-done | bytes 32800 | tf_op jit(solution)/shard_map/ppermute | solution.py:24
  19.2 0.5 decode_and_pack.1
  19.7 1.5 %collective-permute-start.5 = (s16[16,4096]{1,0:T(8,128)(2,1)S(1)}, s16[16,4096]{1,0:T(8,128)(2,1)S(1)}, u32[]{:S(2)}, u32[]{:S(2)}) collective-permute-start(s16[16,4096]{1,0:T(8,128)(2,1)S(1)} %get-tuple-element.21), channel_id=1, source_target_pairs={{0,1},{1,0},{2,3},{3,2},{4,5},{5,4},{6,7},{7,6},{8,9},{9,8},{10,11... | collective-permute-start | bytes 393224 | tf_op jit(solution)/shard_map/ppermute | solution.py:24
  21.2 1.5 %collective-permute-start.6 = (s16[16,4096]{1,0:T(8,128)(2,1)S(1)}, s16[16,4096]{1,0:T(8,128)(2,1)S(1)}, u32[]{:S(2)}, u32[]{:S(2)}) collective-permute-start(s16[16,4096]{1,0:T(8,128)(2,1)S(1)} %get-tuple-element.30), channel_id=1, source_target_pairs={{0,3},{1,2},{2,1},{3,0},{4,7},{5,6},{6,5},{7,4},{8,11},{9,10},{10,... | collective-permute-start | bytes 393224 | tf_op jit(solution)/shard_map/ppermute | solution.py:24
  22.7 0.6 collective-permute-start.7
  23.3 0.5 convert_multiply_fusion.2
  23.8 0.1 copy-done.4
  23.9 0.3 copy-done.5
  24.2 0.3 convert_multiply_fusion.4
  24.6 3.3 %collective-permute-done.5.p1_ref = s16[16,4096]{1,0:T(8,128)(2,1)S(1)} collective-permute-done((s16[16,4096]{1,0:T(8,128)(2,1)S(1)}, s16[16,4096]{1,0:T(8,128)(2,1)S(1)}, u32[]{:S(2)}, u32[]{:S(2)}) %collective-permute-start.5) | collective-permute-done | bytes 131104 | tf_op jit(solution)/shard_map/ppermute | solution.py:24
  27.9 0.6 collective-permute-done.6.p2_ref
  28.5 0.9 %collective-permute-done.7.p3_ref = s16[16,4096]{1,0:T(8,128)(2,1)S(1)} collective-permute-done((s16[16,4096]{1,0:T(8,128)(2,1)S(1)}, s16[16,4096]{1,0:T(8,128)(2,1)S(1)}, u32[]{:S(2)}, u32[]{:S(2)}) %collective-permute-start.7) | collective-permute-done | bytes 131104 | tf_op jit(solution)/shard_map/ppermute | solution.py:24
  29.4 0.3 quad_sum.1
  29.7 3.3 %collective-permute-start.8 = (s16[16,4096]{1,0:T(8,128)(2,1)S(1)}, s16[16,4096]{1,0:T(8,128)(2,1)S(1)}, u32[]{:S(2)}, u32[]{:S(2)}) collective-permute-start(s16[16,4096]{1,0:T(8,128)(2,1)S(1)} %get-tuple-element.33), channel_id=1, source_target_pairs={{0,4},{1,5},{2,6},{3,7},{4,0},{5,1},{6,2},{7,3},{8,12},{9,13},{10,... | collective-permute-start | bytes 393224 | tf_op jit(solution)/shard_map/ppermute | solution.py:24
  33.0 5.5 %collective-permute-done.8 = s16[16,4096]{1,0:T(8,128)(2,1)S(1)} collective-permute-done((s16[16,4096]{1,0:T(8,128)(2,1)S(1)}, s16[16,4096]{1,0:T(8,128)(2,1)S(1)}, u32[]{:S(2)}, u32[]{:S(2)}) %collective-permute-start.8) | collective-permute-done | bytes 131104 | tf_op jit(solution)/shard_map/ppermute | solution.py:24
  38.5 0.1 select_reduce_fusion
  38.8 0.9 %collective-permute-start.10 = (bf16[16,4096]{1,0:T(8,128)(2,1)S(1)}, bf16[16,4096]{1,0:T(8,128)(2,1)S(1)}, u32[]{:S(2)}, u32[]{:S(2)}) collective-permute-start(bf16[16,4096]{1,0:T(8,128)(2,1)S(1)} %fusion.15), channel_id=1, source_target_pairs={{0,1},{1,0},{2,3},{3,2},{4,5},{5,4},{6,7},{7,6},{8,9},{9,8},{10,11... | collective-permute-start | bytes 393224 | tf_op jit(solution)/shard_map/ppermute | solution.py:24
  39.7 0.7 %collective-permute-start.11 = (bf16[16,4096]{1,0:T(8,128)(2,1)S(1)}, bf16[16,4096]{1,0:T(8,128)(2,1)S(1)}, u32[]{:S(2)}, u32[]{:S(2)}) collective-permute-start(bf16[16,4096]{1,0:T(8,128)(2,1)S(1)} %fusion.15), channel_id=1, source_target_pairs={{0,2},{1,3},{2,0},{3,1},{4,6},{5,7},{6,4},{7,5},{8,10},{9,11},{10,... | collective-permute-start | bytes 393224 | tf_op jit(solution)/shard_map/ppermute | solution.py:24
  40.4 1.9 %collective-permute-start.9 = (bf16[16,4096]{1,0:T(8,128)(2,1)S(1)}, bf16[16,4096]{1,0:T(8,128)(2,1)S(1)}, u32[]{:S(2)}, u32[]{:S(2)}) collective-permute-start(bf16[16,4096]{1,0:T(8,128)(2,1)S(1)} %fusion.15), channel_id=1, source_target_pairs={{0,3},{1,2},{2,1},{3,0},{4,7},{5,6},{6,5},{7,4},{8,11},{9,10},{10,... | collective-permute-start | bytes 393224 | tf_op jit(solution)/shard_map/ppermute | solution.py:24
  42.3 2.9 %collective-permute-done.10 = bf16[16,4096]{1,0:T(8,128)(2,1)S(1)} collective-permute-done((bf16[16,4096]{1,0:T(8,128)(2,1)S(1)}, bf16[16,4096]{1,0:T(8,128)(2,1)S(1)}, u32[]{:S(2)}, u32[]{:S(2)}) %collective-permute-start.10) | collective-permute-done | bytes 131104 | tf_op jit(solution)/shard_map/ppermute | solution.py:24
  45.2 0.2 collective-permute-done.11
  45.4 1.7 %collective-permute-done.9 = bf16[16,4096]{1,0:T(8,128)(2,1)S(1)} collective-permute-done((bf16[16,4096]{1,0:T(8,128)(2,1)S(1)}, bf16[16,4096]{1,0:T(8,128)(2,1)S(1)}, u32[]{:S(2)}, u32[]{:S(2)}) %collective-permute-start.9) | collective-permute-done | bytes 131104 | tf_op jit(solution)/shard_map/ppermute | solution.py:24
  47.1 0.5 fusion.17
  47.7 0.5 fusion
  48.2 0.9 %bitcast_reduce_fusion = (f32[8,128]{1,0:T(8,128)S(1)}, f32[128,4096]{1,0:T(8,128)S(1)}) fusion(f32[128,4096]{1,0:T(8,128)S(1)} %get-tuple-element.37, f32[128,4096]{1,0:T(8,128)S(1)} %fusion, f32[128,4096]{1,0:T(8,128)S(1)} %get-tuple-element.35), kind=kLoop, calls=%fused_computation.20 | loop fusion | flops 5766144 | bytes 8392704 | tf_op jit(solution)/shard_map/reduce_sum | solution.py:267
  49.1 0.5 fusion.18
  49.6 0.9 %bitcast_reduce_fusion.1 = (f32[8,128]{1,0:T(8,128)S(1)}, f32[4096,128]{1,0:T(8,128)S(1)}) fusion(f32[4096,128]{1,0:T(8,128)S(1)} %get-tuple-element.34, f32[4096,128]{1,0:T(8,128)S(1)} %fusion.18, f32[4096,128]{1,0:T(8,128)S(1)} %get-tuple-element.27), kind=kLoop, calls=%fused_computation.21 | loop fusion | flops 5766144 | bytes 8392704 | tf_op jit(solution)/shard_map/reduce_sum | solution.py:266
  50.5 3.1 %collective-permute-start.14 = (f32[8,128]{1,0:T(8,128)S(1)}, f32[8,128]{1,0:T(8,128)S(1)}, u32[]{:S(2)}, u32[]{:S(2)}) collective-permute-start(f32[8,128]{1,0:T(8,128)S(1)} %add.95), channel_id=1, source_target_pairs={{0,4},{1,5},{2,6},{3,7},{4,0},{5,1},{6,2},{7,3},{8,12},{9,13},{10,... | collective-permute-start | bytes 12296 | tf_op jit(solution)/shard_map/ppermute | solution.py:24
  53.6 1.6 %collective-permute-done.14 = f32[8,128]{1,0:T(8,128)S(1)} collective-permute-done((f32[8,128]{1,0:T(8,128)S(1)}, f32[8,128]{1,0:T(8,128)S(1)}, u32[]{:S(2)}, u32[]{:S(2)}) %collective-permute-start.14) | collective-permute-done | bytes 4128 | tf_op jit(solution)/shard_map/ppermute | solution.py:24
  55.2 2.0 %collective-permute-start.15 = (f32[8,128]{1,0:T(8,128)S(1)}, f32[8,128]{1,0:T(8,128)S(1)}, u32[]{:S(2)}, u32[]{:S(2)}) collective-permute-start(f32[8,128]{1,0:T(8,128)S(1)} %add.96), channel_id=1, source_target_pairs={{0,3},{1,2},{2,1},{3,0},{4,7},{5,6},{6,5},{7,4},{8,11},{9,10},{10,... | collective-permute-start | bytes 12296 | tf_op jit(solution)/shard_map/ppermute | solution.py:24
  57.2 0.5 collective-permute-start.16
  57.7 1.0 %collective-permute-start.17 = (f32[8,128]{1,0:T(8,128)S(1)}, f32[8,128]{1,0:T(8,128)S(1)}, u32[]{:S(2)}, u32[]{:S(2)}) collective-permute-start(f32[8,128]{1,0:T(8,128)S(1)} %add.96), channel_id=1, source_target_pairs={{0,1},{1,0},{2,3},{3,2},{4,5},{5,4},{6,7},{7,6},{8,9},{9,8},{10,11... | collective-permute-start | bytes 12296 | tf_op jit(solution)/shard_map/ppermute | solution.py:24
  58.7 1.0 %collective-permute-done.15 = f32[8,128]{1,0:T(8,128)S(1)} collective-permute-done((f32[8,128]{1,0:T(8,128)S(1)}, f32[8,128]{1,0:T(8,128)S(1)}, u32[]{:S(2)}, u32[]{:S(2)}) %collective-permute-start.15) | collective-permute-done | bytes 4128 | tf_op jit(solution)/shard_map/ppermute | solution.py:24
  59.7 1.1 %collective-permute-done.16 = f32[8,128]{1,0:T(8,128)S(1)} collective-permute-done((f32[8,128]{1,0:T(8,128)S(1)}, f32[8,128]{1,0:T(8,128)S(1)}, u32[]{:S(2)}, u32[]{:S(2)}) %collective-permute-start.16) | collective-permute-done | bytes 4128 | tf_op jit(solution)/shard_map/ppermute | solution.py:24
  60.8 0.5 collective-permute-done.17
  61.3 1.2 %collective-permute-done.18.other_ref = f32[8,128]{1,0:T(8,128)S(1)} collective-permute-done((f32[8,128]{1,0:T(8,128)S(1)}, f32[8,128]{1,0:T(8,128)S(1)}, u32[]{:S(2)}, u32[]{:S(2)}) %collective-permute-start.18) | collective-permute-done | bytes 4128 | tf_op jit(solution)/shard_map/ppermute | solution.py:24
  62.5 1.6 %scale_directions.1 = (bf16[4096,128]{1,0:T(8,128)(2,1)}, bf16[128,4096]{1,0:T(8,128)(2,1)}) custom-call(f32[8,128]{1,0:T(8,128)S(1)} %add_add_fusion.squares_ref, f32[8,128]{1,0:T(8,128)S(1)} %collective-permute-done.18.other_ref, f32[4096,128]{1,0:T(8,128)S(1)} %get-tuple-element.43.enc_ref, f32[128,4096]{1,0:T(8,128)S(1)} %get-tuple-element.41.dec_ref), custom_call_target="tpu_custom_call" | custom-call | tf_op jit(solution)/shard_map/scale_directions/pallas_call | solution.py:53
  (32 shorter events, 0.5 us)
Async XLA Ops:
  0.6 17.0 %copy-start = (bf16[1,4096,128]{2,1,0:T(8,128)(2,1)S(1)}, bf16[1,4096,128]{2,1,0:T(8,128)(2,1)}, u32[]{:S(2)}) copy-start(bf16[1,4096,128]{2,1,0:T(8,128)(2,1)} %param.10) | copy-start | bytes 3145732
  0.6 18.6 %copy-start.1 = (bf16[1,128,4096]{2,1,0:T(8,128)(2,1)S(1)}, bf16[1,128,4096]{2,1,0:T(8,128)(2,1)}, u32[]{:S(2)}) copy-start(bf16[1,128,4096]{2,1,0:T(8,128)(2,1)} %param.11) | copy-start | bytes 3145732
  1.9 7.7 %collective-permute-start = (bf16[8,4096]{1,0:T(8,128)(2,1)S(1)}, bf16[8,4096]{1,0:T(8,128)(2,1)S(1)}, u32[]{:S(2)}, u32[]{:S(2)}) collective-permute-start(bf16[8,4096]{1,0:T(8,128)(2,1)S(1)} %get-tuple-element.47), channel_id=1, source_target_pairs={{0,4},{1,5},{2,6},{3,7},{4,0},{5,1},{6,2},{7,3},{8,12},{9,13},{10,... | collective-permute-start | bytes 196616 | tf_op jit(solution)/shard_map/ppermute | solution.py:24
  7.5 15.7 %copy-start.2 = (bf16[1,128,4096]{2,1,0:T(8,128)(2,1)S(1)}, bf16[1,128,4096]{2,1,0:T(8,128)(2,1)}, u32[]{:S(2)}) copy-start(bf16[1,128,4096]{2,1,0:T(8,128)(2,1)} %param.15) | copy-start | bytes 3145732
  7.6 15.7 %copy-start.3 = (bf16[1,128,4096]{2,1,0:T(8,128)(2,1)S(1)}, bf16[1,128,4096]{2,1,0:T(8,128)(2,1)}, u32[]{:S(2)}) copy-start(bf16[1,128,4096]{2,1,0:T(8,128)(2,1)} %param.14) | copy-start | bytes 3145732
  7.6 34.8 %collective-permute-start.13 = (f32[128]{0:T(128)S(1)}, f32[128]{0:T(128)S(1)}, u32[]{:S(2)}, u32[]{:S(2)}) collective-permute-start(f32[128]{0:T(128)S(1)} %add_sqrt_fusion), channel_id=1, source_target_pairs={{0,8},{8,0},{1,9},{9,1},{2,10},{10,2},{3,11},{11,3},{4,12},{12,4},... | collective-permute-start | bytes 1544 | tf_op jit(solution)/shard_map/ppermute | solution.py:24
  9.7 7.3 %collective-permute-start.1 = (bf16[16,4096]{1,0:T(8,128)(2,1)S(1)}, bf16[16,4096]{1,0:T(8,128)(2,1)S(1)}, u32[]{:S(2)}, u32[]{:S(2)}) collective-permute-start(bf16[16,4096]{1,0:T(8,128)(2,1)S(1)} %pad_maximum_fusion.1), channel_id=1, source_target_pairs={{0,3},{1,2},{2,1},{3,0},{4,7},{5,6},{6,5},{7,4},{8,11},{9,10},{10,... | collective-permute-start | bytes 393224 | tf_op jit(solution)/shard_map/ppermute | solution.py:24
  11.3 6.1 %collective-permute-start.2 = (bf16[16,4096]{1,0:T(8,128)(2,1)S(1)}, bf16[16,4096]{1,0:T(8,128)(2,1)S(1)}, u32[]{:S(2)}, u32[]{:S(2)}) collective-permute-start(bf16[16,4096]{1,0:T(8,128)(2,1)S(1)} %pad_maximum_fusion.1), channel_id=1, source_target_pairs={{0,1},{1,0},{2,3},{3,2},{4,5},{5,4},{6,7},{7,6},{8,9},{9,8},{10,11... | collective-permute-start | bytes 393224 | tf_op jit(solution)/shard_map/ppermute | solution.py:24
  11.8 5.8 %collective-permute-start.3 = (bf16[16,4096]{1,0:T(8,128)(2,1)S(1)}, bf16[16,4096]{1,0:T(8,128)(2,1)S(1)}, u32[]{:S(2)}, u32[]{:S(2)}) collective-permute-start(bf16[16,4096]{1,0:T(8,128)(2,1)S(1)} %pad_maximum_fusion.1), channel_id=1, source_target_pairs={{0,2},{1,3},{2,0},{3,1},{4,6},{5,7},{6,4},{7,5},{8,10},{9,11},{10,... | collective-permute-start | bytes 393224 | tf_op jit(solution)/shard_map/ppermute | solution.py:24
  17.9 1.3 %collective-permute-start.4 = (f32[64,128]{1,0:T(8,128)S(1)}, f32[64,128]{1,0:T(8,128)S(1)}, u32[]{:S(2)}, u32[]{:S(2)}) collective-permute-start(f32[64,128]{1,0:T(8,128)S(1)} %fusion.12.own_ref), channel_id=1, source_target_pairs={{0,8},{8,0},{1,9},{9,1},{2,10},{10,2},{3,11},{11,3},{4,12},{12,4},... | collective-permute-start | bytes 98312 | tf_op jit(solution)/shard_map/ppermute | solution.py:24
  19.7 8.1 %collective-permute-start.5 = (s16[16,4096]{1,0:T(8,128)(2,1)S(1)}, s16[16,4096]{1,0:T(8,128)(2,1)S(1)}, u32[]{:S(2)}, u32[]{:S(2)}) collective-permute-start(s16[16,4096]{1,0:T(8,128)(2,1)S(1)} %get-tuple-element.21), channel_id=1, source_target_pairs={{0,1},{1,0},{2,3},{3,2},{4,5},{5,4},{6,7},{7,6},{8,9},{9,8},{10,11... | collective-permute-start | bytes 393224 | tf_op jit(solution)/shard_map/ppermute | solution.py:24
  21.2 7.3 %collective-permute-start.6 = (s16[16,4096]{1,0:T(8,128)(2,1)S(1)}, s16[16,4096]{1,0:T(8,128)(2,1)S(1)}, u32[]{:S(2)}, u32[]{:S(2)}) collective-permute-start(s16[16,4096]{1,0:T(8,128)(2,1)S(1)} %get-tuple-element.30), channel_id=1, source_target_pairs={{0,3},{1,2},{2,1},{3,0},{4,7},{5,6},{6,5},{7,4},{8,11},{9,10},{10,... | collective-permute-start | bytes 393224 | tf_op jit(solution)/shard_map/ppermute | solution.py:24
  22.7 1.2 %copy-start.4 = (bf16[1,4096,128]{2,1,0:T(8,128)(2,1)S(1)}, bf16[1,4096,128]{2,1,0:T(8,128)(2,1)}, u32[]{:S(2)}) copy-start(bf16[1,4096,128]{2,1,0:T(8,128)(2,1)} %param.13) | copy-start | bytes 3145732
  22.7 1.5 %copy-start.5 = (bf16[1,4096,128]{2,1,0:T(8,128)(2,1)S(1)}, bf16[1,4096,128]{2,1,0:T(8,128)(2,1)}, u32[]{:S(2)}) copy-start(bf16[1,4096,128]{2,1,0:T(8,128)(2,1)} %param.12) | copy-start | bytes 3145732
  22.7 6.7 %collective-permute-start.7 = (s16[16,4096]{1,0:T(8,128)(2,1)S(1)}, s16[16,4096]{1,0:T(8,128)(2,1)S(1)}, u32[]{:S(2)}, u32[]{:S(2)}) collective-permute-start(s16[16,4096]{1,0:T(8,128)(2,1)S(1)} %get-tuple-element.31), channel_id=1, source_target_pairs={{0,2},{1,3},{2,0},{3,1},{4,6},{5,7},{6,4},{7,5},{8,10},{9,11},{10,... | collective-permute-start | bytes 393224 | tf_op jit(solution)/shard_map/ppermute | solution.py:24
  29.7 8.8 %collective-permute-start.8 = (s16[16,4096]{1,0:T(8,128)(2,1)S(1)}, s16[16,4096]{1,0:T(8,128)(2,1)S(1)}, u32[]{:S(2)}, u32[]{:S(2)}) collective-permute-start(s16[16,4096]{1,0:T(8,128)(2,1)S(1)} %get-tuple-element.33), channel_id=1, source_target_pairs={{0,4},{1,5},{2,6},{3,7},{4,0},{5,1},{6,2},{7,3},{8,12},{9,13},{10,... | collective-permute-start | bytes 393224 | tf_op jit(solution)/shard_map/ppermute | solution.py:24
  38.8 6.4 %collective-permute-start.10 = (bf16[16,4096]{1,0:T(8,128)(2,1)S(1)}, bf16[16,4096]{1,0:T(8,128)(2,1)S(1)}, u32[]{:S(2)}, u32[]{:S(2)}) collective-permute-start(bf16[16,4096]{1,0:T(8,128)(2,1)S(1)} %fusion.15), channel_id=1, source_target_pairs={{0,1},{1,0},{2,3},{3,2},{4,5},{5,4},{6,7},{7,6},{8,9},{9,8},{10,11... | collective-permute-start | bytes 393224 | tf_op jit(solution)/shard_map/ppermute | solution.py:24
  39.7 5.7 %collective-permute-start.11 = (bf16[16,4096]{1,0:T(8,128)(2,1)S(1)}, bf16[16,4096]{1,0:T(8,128)(2,1)S(1)}, u32[]{:S(2)}, u32[]{:S(2)}) collective-permute-start(bf16[16,4096]{1,0:T(8,128)(2,1)S(1)} %fusion.15), channel_id=1, source_target_pairs={{0,2},{1,3},{2,0},{3,1},{4,6},{5,7},{6,4},{7,5},{8,10},{9,11},{10,... | collective-permute-start | bytes 393224 | tf_op jit(solution)/shard_map/ppermute | solution.py:24
  40.4 6.7 %collective-permute-start.9 = (bf16[16,4096]{1,0:T(8,128)(2,1)S(1)}, bf16[16,4096]{1,0:T(8,128)(2,1)S(1)}, u32[]{:S(2)}, u32[]{:S(2)}) collective-permute-start(bf16[16,4096]{1,0:T(8,128)(2,1)S(1)} %fusion.15), channel_id=1, source_target_pairs={{0,3},{1,2},{2,1},{3,0},{4,7},{5,6},{6,5},{7,4},{8,11},{9,10},{10,... | collective-permute-start | bytes 393224 | tf_op jit(solution)/shard_map/ppermute | solution.py:24
  47.6 1.5 %collective-permute-start.12 = (f32[64,128]{1,0:T(8,128)S(1)}, f32[64,128]{1,0:T(8,128)S(1)}, u32[]{:S(2)}, u32[]{:S(2)}) collective-permute-start(f32[64,128]{1,0:T(8,128)S(1)} %fusion.17), channel_id=1, source_target_pairs={{0,8},{8,0},{1,9},{9,1},{2,10},{10,2},{3,11},{11,3},{4,12},{12,4},... | collective-permute-start | bytes 98312 | tf_op jit(solution)/shard_map/ppermute | solution.py:24
  50.5 4.7 %collective-permute-start.14 = (f32[8,128]{1,0:T(8,128)S(1)}, f32[8,128]{1,0:T(8,128)S(1)}, u32[]{:S(2)}, u32[]{:S(2)}) collective-permute-start(f32[8,128]{1,0:T(8,128)S(1)} %add.95), channel_id=1, source_target_pairs={{0,4},{1,5},{2,6},{3,7},{4,0},{5,1},{6,2},{7,3},{8,12},{9,13},{10,... | collective-permute-start | bytes 12296 | tf_op jit(solution)/shard_map/ppermute | solution.py:24
  55.2 4.5 %collective-permute-start.15 = (f32[8,128]{1,0:T(8,128)S(1)}, f32[8,128]{1,0:T(8,128)S(1)}, u32[]{:S(2)}, u32[]{:S(2)}) collective-permute-start(f32[8,128]{1,0:T(8,128)S(1)} %add.96), channel_id=1, source_target_pairs={{0,3},{1,2},{2,1},{3,0},{4,7},{5,6},{6,5},{7,4},{8,11},{9,10},{10,... | collective-permute-start | bytes 12296 | tf_op jit(solution)/shard_map/ppermute | solution.py:24
  57.2 3.6 %collective-permute-start.16 = (f32[8,128]{1,0:T(8,128)S(1)}, f32[8,128]{1,0:T(8,128)S(1)}, u32[]{:S(2)}, u32[]{:S(2)}) collective-permute-start(f32[8,128]{1,0:T(8,128)S(1)} %add.96), channel_id=1, source_target_pairs={{0,2},{1,3},{2,0},{3,1},{4,6},{5,7},{6,4},{7,5},{8,10},{9,11},{10,... | collective-permute-start | bytes 12296 | tf_op jit(solution)/shard_map/ppermute | solution.py:24
  57.7 3.6 %collective-permute-start.17 = (f32[8,128]{1,0:T(8,128)S(1)}, f32[8,128]{1,0:T(8,128)S(1)}, u32[]{:S(2)}, u32[]{:S(2)}) collective-permute-start(f32[8,128]{1,0:T(8,128)S(1)} %add.96), channel_id=1, source_target_pairs={{0,1},{1,0},{2,3},{3,2},{4,5},{5,4},{6,7},{7,6},{8,9},{9,8},{10,11... | collective-permute-start | bytes 12296 | tf_op jit(solution)/shard_map/ppermute | solution.py:24
  61.3 1.2 %collective-permute-start.18 = (f32[8,128]{1,0:T(8,128)S(1)}, f32[8,128]{1,0:T(8,128)S(1)}, u32[]{:S(2)}, u32[]{:S(2)}) collective-permute-start(f32[8,128]{1,0:T(8,128)S(1)} %add_add_fusion.squares_ref), channel_id=1, source_target_pairs={{0,8},{8,0},{1,9},{9,1},{2,10},{10,2},{3,11},{11,3},{4,12},{12,4},... | collective-permute-start | bytes 12296 | tf_op jit(solution)/shard_map/ppermute | solution.py:24
